TPU v7x, 128 devices: a whole 4x4x4 slice. The times are simulated.
128 devices in a mesh: section: 2 (over core), gx: 4 (over x), gy: 16 (over z, y).
Axes of the slice: x: 4, y: 4, z: 4, core: 2. Of those that a mesh axis runs over, the one named last changes fastest.
Arguments:
- inputs: bfloat16 [2, 16, 512, 960], P(None, 'gy', 'gx'), may hold values from -6 to 6
- cotangent: bfloat16 [2, 16, 512, 960], P(None, 'gy', 'gx'), may hold values from -6 to 6
- segment_ids: int32 [2, 16, 512], P(None, 'gy'), may hold values from 0 to 3, as said below
- gain_attn: bfloat16 [2, 960], P('section', ('gx', 'gy')), may hold values from 0.5 to 1.5
- w_qkv: bfloat16 [2, 960, 1600], P('section', ('gx', 'gy')), may hold values from -0.1875 to 0.1875
- w_out: bfloat16 [2, 960, 960], P('section', ('gx', 'gy')), may hold values from -1 to 1
- gain_ffn: bfloat16 [2, 960], P('section', ('gx', 'gy')), may hold values from 0.5 to 1.5
- w_gate: bfloat16 [2, 960, 2560], P('section', 'gx', 'gy'), may hold values from -0.1875 to 0.1875
- w_up: bfloat16 [2, 960, 2560], P('section', 'gx', 'gy'), may hold values from -0.1875 to 0.1875
- w_down: bfloat16 [2, 2560, 960], P('section', 'gy', 'gx'), may hold values from -0.125 to 0.125
Outputs:
- layer_out: bfloat16 [2, 2, 16, 512, 960], P('section', None, 'gy', 'gx')
- input_grad: bfloat16 [2, 2, 16, 512, 960], P('section', None, 'gy', 'gx')
- grad_gain_attn: float32 [2, 960], P('section', ('gx', 'gy'))
- grad_w_qkv: float32 [2, 960, 1600], P('section', ('gx', 'gy'))
- grad_w_out: float32 [2, 960, 960], P('section', ('gx', 'gy'))
- grad_gain_ffn: float32 [2, 960], P('section', ('gx', 'gy'))
- grad_w_gate: float32 [2, 960, 2560], P('section', 'gx', 'gy')
- grad_w_up: float32 [2, 960, 2560], P('section', 'gx', 'gy')
- grad_w_down: float32 [2, 2560, 960], P('section', 'gy', 'gx')
Inputs may be any that keep to these rules, and one draw needn't show every extreme that they name: `segment_ids`: along each sequence the segment ids never fall, start at 0 and reach 3; the last document of every sequence begins within its first 128 tokens.
All inputs are finite; a program needn't handle non-finite values.
Results may differ from a plain program's by a relative error of at most 0.02.
Values may be sent and summed in bfloat16 or wider, within the bound.
No kernel may reach another device: no remote copies, remote signals or barrier semaphores. Data moves between devices by JAX's collectives and lax.ppermute only.
A program may use at most 192 MiB of HBM per device.

v0:
```python
import jax
import jax.numpy as jnp
from jax import lax
from jax.sharding import PartitionSpec as P

HQ = 15
HK = 5
HD = 64
QW = 960
KW = 320


epsilon = 1e-05
rope_base = 100000.0
masked_score = -1e30


def passed_along(value, axis, steps):
    count = lax.axis_size(axis)
    leading, last = (max(0, -steps), min(count, count - steps))
    return lax.ppermute(value, axis, [(source, source + steps) for source in range(leading, last)])


def rope_tables(positions):
    half_width = HD // 2
    frequency = rope_base ** (-(jnp.arange(half_width, dtype=jnp.float32) * 2.0) / HD)
    angles = positions.astype(jnp.float32)[:, None] * frequency[None, :]
    cosine = jnp.cos(angles)
    sine_part = jnp.sin(angles)
    return (jnp.concatenate([cosine, cosine], 1), jnp.concatenate([sine_part, sine_part], 1))


def rotate(values, cosine, sine_part, head_count):
    row_count = values.shape[0]
    shaped = values.reshape(row_count, head_count, HD)
    half_width = HD // 2
    turned = jnp.concatenate([-shaped[:, :, half_width:], shaped[:, :, :half_width]], 2)
    return (shaped * cosine[:, None, :] + turned * sine_part[:, None, :]).reshape(
        row_count, head_count * HD
    )


def rotate_back(gradient, cosine, sine_part, head_count):
    row_count = gradient.shape[0]
    shaped = gradient.reshape(row_count, head_count, HD)
    half_width = HD // 2
    scaled = shaped * sine_part[:, None, :]
    turned = jnp.concatenate([scaled[:, :, half_width:], -scaled[:, :, :half_width]], 2)
    return (shaped * cosine[:, None, :] + turned).reshape(row_count, head_count * HD)


def token_layout(segments, first_row, row_count):
    local_ids = lax.dynamic_slice_in_dim(segments, first_row, row_count, 0)
    own_index = first_row + jnp.arange(row_count, dtype=jnp.int32)
    doc_start = jnp.sum((segments[None, :] < local_ids[:, None]).astype(jnp.int32), axis=1)
    key_index = jnp.arange(segments.shape[0], dtype=jnp.int32)
    allowed = (local_ids[:, None] == segments[None, :]) & (key_index[None, :] <= own_index[:, None])
    cosine, sine_part = rope_tables(own_index - doc_start)
    return (allowed, cosine, sine_part)


def split_heads(queries, kv_all):
    row_count = queries.shape[0]
    grouped = queries.reshape(row_count, HK, HQ // HK, HD).transpose(1, 0, 2, 3)
    key_heads = kv_all[:, :KW].reshape(-1, HK, HD).transpose(1, 0, 2)
    value_heads = kv_all[:, KW:].reshape(-1, HK, HD).transpose(1, 0, 2)
    return (grouped, key_heads, value_heads)


def group_scores(query_group, key_group, allowed):
    scores = (
        jnp.einsum("ngd,sd->gns", query_group, key_group, preferred_element_type=jnp.float32)
        * 0.125
    )
    return jnp.where(allowed[None], scores, masked_score)


def attend(queries, kv_all, allowed):
    row_count = queries.shape[0]
    grouped, key_heads, value_heads = split_heads(queries, kv_all)

    def one_group(items):
        query_group, key_group, value_group = items
        scores = group_scores(query_group, key_group, allowed)
        highest = jnp.max(scores, axis=2, keepdims=True)
        exponent_terms = jnp.exp(scores - highest)
        totals = jnp.sum(exponent_terms, axis=2, keepdims=True)
        soft_weights = (exponent_terms / totals).astype(jnp.bfloat16)
        result = jnp.einsum(
            "gns,sd->ngd", soft_weights, value_group, preferred_element_type=jnp.float32
        )
        return (result.astype(jnp.bfloat16), highest + jnp.log(totals))

    attended, log_total = lax.map(one_group, (grouped, key_heads, value_heads))
    return (attended.transpose(1, 0, 2, 3).reshape(row_count, QW), log_total)


def attend_back(queries, kv_all, allowed, log_total, d_attended):
    row_count = queries.shape[0]
    key_count = kv_all.shape[0]
    grouped, key_heads, value_heads = split_heads(queries, kv_all)
    d_grouped = d_attended.reshape(row_count, HK, HQ // HK, HD).transpose(1, 0, 2, 3)

    def one_group(items):
        query_group, key_group, value_group, group_total, d_group = items
        scores = group_scores(query_group, key_group, allowed)
        probs = jnp.exp(scores - group_total)
        d_probs = jnp.einsum(
            "ngd,sd->gns", d_group, value_group, preferred_element_type=jnp.float32
        )
        inner = jnp.sum(probs * d_probs, axis=2, keepdims=True)
        d_scores = (probs * (d_probs - inner)).astype(jnp.bfloat16)
        d_query = (
            jnp.einsum("gns,sd->ngd", d_scores, key_group, preferred_element_type=jnp.float32)
            * 0.125
        )
        d_key = (
            jnp.einsum("gns,ngd->sd", d_scores, query_group, preferred_element_type=jnp.float32)
            * 0.125
        )
        d_value = jnp.einsum(
            "gns,ngd->sd", probs.astype(jnp.bfloat16), d_group, preferred_element_type=jnp.float32
        )
        return (d_query, d_key, d_value)

    d_query, d_key, d_value = lax.map(
        one_group, (grouped, key_heads, value_heads, log_total, d_grouped)
    )
    d_queries = d_query.transpose(1, 0, 2, 3).reshape(row_count, QW)
    d_keys = d_key.transpose(1, 0, 2).reshape(key_count, KW)
    d_values = d_value.transpose(1, 0, 2).reshape(key_count, KW)
    return (d_queries, jnp.concatenate([d_keys, d_values], 1))


def forward_layer(section_in, allowed, cosine, sine_part, weights):
    gain_one, qkv_matrix, out_matrix, gain_two, gate_matrix, up_matrix, down_matrix = weights
    resid = section_in.astype(jnp.float32)
    rstd_one = lax.rsqrt(jnp.mean(resid * resid, axis=1, keepdims=True) + epsilon)
    normed_one = (resid * rstd_one * gain_one).astype(jnp.bfloat16)
    projected = jnp.dot(normed_one, qkv_matrix, preferred_element_type=jnp.float32)
    queries = rotate(projected[:, :QW], cosine, sine_part, HQ).astype(jnp.bfloat16)
    keys_local = rotate(projected[:, QW : QW + KW], cosine, sine_part, HK)
    kv_local = jnp.concatenate([keys_local, projected[:, QW + KW :]], 1).astype(jnp.bfloat16)
    kv_all = lax.all_gather(kv_local, "gx", axis=0, tiled=True)
    attended, log_total = attend(queries, kv_all, allowed)
    middle = resid + jnp.dot(attended, out_matrix, preferred_element_type=jnp.float32)
    rstd_two = lax.rsqrt(jnp.mean(middle * middle, axis=1, keepdims=True) + epsilon)
    normed_two = (middle * rstd_two * gain_two).astype(jnp.bfloat16)
    normed_rows = lax.all_gather(normed_two, "gy", axis=0, tiled=True)
    gate = jnp.dot(normed_rows, gate_matrix, preferred_element_type=jnp.float32)
    up_part = jnp.dot(normed_rows, up_matrix, preferred_element_type=jnp.float32)
    hidden = (jax.nn.silu(gate) * up_part).astype(jnp.bfloat16)
    branch = lax.psum_scatter(
        jnp.dot(hidden, down_matrix, preferred_element_type=jnp.float32),
        "gy",
        scatter_dimension=0,
        tiled=True,
    )
    output = middle + branch
    kept = (
        section_in,
        rstd_one,
        normed_one,
        queries,
        kv_all,
        log_total,
        attended,
        middle,
        rstd_two,
        normed_rows,
        gate,
        up_part,
        hidden,
    )
    return (output, kept)


def backward_layer(grad_out, kept, allowed, cosine, sine_part, weights):
    gain_one, qkv_matrix, out_matrix, gain_two, gate_matrix, up_matrix, down_matrix = weights
    (
        section_in,
        rstd_one,
        normed_one,
        queries,
        kv_all,
        log_total,
        attended,
        middle,
        rstd_two,
        normed_rows,
        gate,
        up_part,
        hidden,
    ) = kept
    resid = section_in.astype(jnp.float32)
    d_branch = grad_out.astype(jnp.bfloat16)
    d_rows = lax.all_gather(d_branch, "gy", axis=0, tiled=True)
    grad_down = jnp.einsum("nf,nd->fd", hidden, d_rows, preferred_element_type=jnp.float32)
    d_hidden = jnp.einsum("nd,fd->nf", d_rows, down_matrix, preferred_element_type=jnp.float32)
    sigma = jax.nn.sigmoid(gate)
    d_gate = (d_hidden * up_part * sigma * (1.0 + gate * (1.0 - sigma))).astype(jnp.bfloat16)
    d_up = (d_hidden * gate * sigma).astype(jnp.bfloat16)
    grad_gate = jnp.einsum("nd,nf->df", normed_rows, d_gate, preferred_element_type=jnp.float32)
    grad_up = jnp.einsum("nd,nf->df", normed_rows, d_up, preferred_element_type=jnp.float32)
    first_term = jnp.einsum("nf,df->nd", d_gate, gate_matrix, preferred_element_type=jnp.float32)
    d_normed_two = lax.psum_scatter(
        first_term + jnp.einsum("nf,df->nd", d_up, up_matrix, preferred_element_type=jnp.float32),
        "gy",
        scatter_dimension=0,
        tiled=True,
    )
    scaled_two = middle * rstd_two
    grad_gain_two = jnp.sum(d_normed_two * scaled_two, axis=0)
    inner_two = d_normed_two * gain_two
    d_middle = grad_out + rstd_two * (
        inner_two - scaled_two * jnp.mean(inner_two * scaled_two, axis=1, keepdims=True)
    )
    d_proj = d_middle.astype(jnp.bfloat16)
    grad_wout = jnp.einsum("nq,nd->qd", attended, d_proj, preferred_element_type=jnp.float32)
    d_attended = jnp.einsum(
        "nd,qd->nq", d_proj, out_matrix, preferred_element_type=jnp.float32
    ).astype(jnp.bfloat16)
    d_queries, d_keyvals = attend_back(queries, kv_all, allowed, log_total, d_attended)
    d_kv = lax.psum_scatter(
        d_keyvals.astype(jnp.bfloat16), "gx", scatter_dimension=0, tiled=True
    ).astype(jnp.float32)
    d_projected = jnp.concatenate(
        [
            rotate_back(d_queries, cosine, sine_part, HQ),
            rotate_back(d_kv[:, :KW], cosine, sine_part, HK),
            d_kv[:, KW:],
        ],
        1,
    ).astype(jnp.bfloat16)
    grad_qkv = jnp.einsum("nd,nc->dc", normed_one, d_projected, preferred_element_type=jnp.float32)
    d_normed_one = jnp.einsum(
        "nc,dc->nd", d_projected, qkv_matrix, preferred_element_type=jnp.float32
    )
    scaled_one = resid * rstd_one
    grad_gain_one = jnp.sum(d_normed_one * scaled_one, axis=0)
    inner_one = d_normed_one * gain_one
    d_input = d_middle + rstd_one * (
        inner_one - scaled_one * jnp.mean(inner_one * scaled_one, axis=1, keepdims=True)
    )
    return (
        d_input.astype(jnp.bfloat16),
        (grad_gain_one, grad_qkv, grad_wout, grad_gain_two, grad_gate, grad_up, grad_down),
    )


def per_device(
    inputs, cotangent, segment_ids, gain_attn, w_qkv, w_out, gain_ffn, w_gate, w_up, w_down
):
    section_index = lax.axis_index("section")
    is_first = section_index == 0
    batch_count = inputs.shape[0]
    row_count = inputs.shape[2]
    width = inputs.shape[3]
    first_row = lax.axis_index("gx") * row_count
    gain_full, qkv_full, out_full, gain_second = (
        lax.all_gather(gain_attn, ("gx", "gy"), axis=1, tiled=True),
        lax.all_gather(w_qkv, ("gx", "gy"), axis=1, tiled=True),
        lax.all_gather(w_out, ("gx", "gy"), axis=1, tiled=True),
        lax.all_gather(gain_ffn, ("gx", "gy"), axis=1, tiled=True),
    )
    gate_part, up_piece, down_part = (
        lax.all_gather(w_gate, "gx", axis=1, tiled=True),
        lax.all_gather(w_up, "gx", axis=1, tiled=True),
        lax.all_gather(w_down, "gx", axis=2, tiled=True),
    )
    gate_matrix = gate_part[0]
    up_matrix = up_piece[0]
    down_matrix = down_part[0]
    weights = (
        gain_full[0].astype(jnp.float32),
        qkv_full[0],
        out_full[0],
        gain_second[0].astype(jnp.float32),
        gate_matrix,
        up_matrix,
        down_matrix,
    )
    own_segments = segment_ids[:, 0]

    def layout_for(batch_now):
        segments = lax.dynamic_index_in_dim(own_segments, batch_now, 0, keepdims=False)
        return token_layout(segments, first_row, row_count)

    received = jnp.zeros((row_count, width), jnp.bfloat16)
    outputs_tick = []
    kept_tick = []
    for step_tick in range(batch_count + 1):
        batch_now = jnp.clip(step_tick - section_index, 0, batch_count - 1)
        allowed, cosine, sine_part = layout_for(batch_now)
        section_in = jnp.where(is_first, inputs[min(step_tick, batch_count - 1), 0], received)
        output, kept = forward_layer(section_in, allowed, cosine, sine_part, weights)
        output = output.astype(jnp.bfloat16)
        outputs_tick.append(output)
        kept_tick.append(kept)
        if step_tick < batch_count:
            received = passed_along(output, "section", 1)
    sent_back = jnp.zeros((row_count, width), jnp.bfloat16)
    running = None
    grads_tick = []
    for step_tick in range(batch_count + 1):
        batch_raw = step_tick - 1 + section_index
        in_range = (batch_raw >= 0) & (batch_raw < batch_count)
        batch_now = jnp.clip(batch_raw, 0, batch_count - 1)
        allowed, cosine, sine_part = layout_for(batch_now)
        kept = jax.tree.map(
            lambda early, late: jnp.where(is_first, early, late),
            kept_tick[max(step_tick - 1, 0)],
            kept_tick[min(step_tick + 1, batch_count)],
        )
        grad_in = jnp.where(
            is_first, sent_back, cotangent[min(step_tick, batch_count - 1), 0]
        ).astype(jnp.float32)
        d_input, parts = backward_layer(grad_in, kept, allowed, cosine, sine_part, weights)
        grads_tick.append(d_input)
        parts = jax.tree.map(lambda member: jnp.where(in_range, member, 0.0), parts)
        running = parts if running is None else jax.tree.map(jnp.add, running, parts)
        if step_tick < batch_count:
            sent_back = passed_along(d_input, "section", -1)
    layer_out = jnp.stack(
        [
            jnp.where(is_first, outputs_tick[batch_slot], outputs_tick[batch_slot + 1])
            for batch_slot in range(batch_count)
        ]
    )[None, :, None]
    input_grad = jnp.stack(
        [
            jnp.where(is_first, grads_tick[batch_slot + 1], grads_tick[batch_slot])
            for batch_slot in range(batch_count)
        ]
    )[None, :, None]
    grad_one, grad_qkv, grad_wout, grad_two, grad_gate, grad_up, grad_down = running
    grad_one, grad_qkv, grad_wout, grad_two = (
        lax.psum_scatter(grad_one, ("gx", "gy"), scatter_dimension=0, tiled=True),
        lax.psum_scatter(grad_qkv, ("gx", "gy"), scatter_dimension=0, tiled=True),
        lax.psum_scatter(grad_wout, ("gx", "gy"), scatter_dimension=0, tiled=True),
        lax.psum_scatter(grad_two, ("gx", "gy"), scatter_dimension=0, tiled=True),
    )
    grad_gate, grad_up, grad_down = (
        lax.psum_scatter(
            grad_gate.astype(jnp.bfloat16), "gx", scatter_dimension=0, tiled=True
        ).astype(jnp.float32),
        lax.psum_scatter(
            grad_up.astype(jnp.bfloat16), "gx", scatter_dimension=0, tiled=True
        ).astype(jnp.float32),
        lax.psum_scatter(
            grad_down.astype(jnp.bfloat16), "gx", scatter_dimension=1, tiled=True
        ).astype(jnp.float32),
    )
    return (
        layer_out,
        input_grad,
        grad_one[None],
        grad_qkv[None],
        grad_wout[None],
        grad_two[None],
        grad_gate[None],
        grad_up[None],
        grad_down[None],
    )


def solution(mesh):
    return jax.shard_map(
        per_device,
        mesh=mesh,
        in_specs=(
            P(None, "gy", "gx", None),
            P(None, "gy", "gx", None),
            P(None, "gy", None),
            P("section", ("gx", "gy")),
            P("section", ("gx", "gy"), None),
            P("section", ("gx", "gy"), None),
            P("section", ("gx", "gy")),
            P("section", "gx", "gy"),
            P("section", "gx", "gy"),
            P("section", "gy", "gx"),
        ),
        out_specs=(
            P("section", None, "gy", "gx", None),
            P("section", None, "gy", "gx", None),
            P("section", ("gx", "gy")),
            P("section", ("gx", "gy"), None),
            P("section", ("gx", "gy"), None),
            P("section", ("gx", "gy")),
            P("section", "gx", "gy"),
            P("section", "gx", "gy"),
            P("section", "gy", "gx"),
        ),
        check_vma=False,
    )
```

profile of v0, /device:TPU:54, one launch (start us, length us, event | category | flops | bytes accessed | tf_op | source)
XLA Modules:
  0.0 1898.7 jit_solution(4941055397920914928)
XLA Ops:
  14.2 150.3 %all-reduce.9 = (bf16[960]{0:T(1024)(128)(2,1)S(1)}, bf16[960]{0:T(1024)(128)(2,1)S(1)}) all-reduce(bf16[960]{0:T(1024)(128)(2,1)S(1)} %dynamic-update-slice, bf16[960]{0:T(1024)(128)(2,1)S(1)} %dynamic-update-slice.1), channel_id=1, replica_groups=mesh['section'=2,'gx'=4,'gy'=16] {'gx','gy'}, use_global_device_ids=true, to_apply=%add | all-reduce | flops 1920 | bytes 7680
  177.9 25.6 %all_gather.50 = bf16[512,640]{0,1:T(8,128)(2,1)S(1)} all-gather(bf16[128,640]{0,1:T(8,128)(2,1)S(1)} %pad_maximum_fusion.15), channel_id=1, replica_groups=mesh['section'=2,'gx'=4,'gy'=16] {'gx'}, dimensions={0}, use_global_device_ids=true | all-gather | bytes 819200 | tf_op jit(solution)/shard_map/all_gather | solution.py:144
  205.3 16.0 while.84
  224.1 15.1 all_gather.54
  241.7 14.4 all_gather.55
  258.6 14.4 all_gather.56
  275.4 16.5 all-gather.14.cloned.1.call-done
  298.3 4.5 fusion.255
  302.9 83.7 %reduce-scatter.29.cloned.1.call-done = f32[128,960]{0,1:T(8,128)} async-done(((f32[2048,960]{0,1:T(8,128)}), f32[128,960]{0,1:T(8,128)}) %reduce-scatter.29.cloned.1.call-update) | async-done | bytes 491536 | tf_op jit(solution)/shard_map/reduce_scatter | solution.py:153
  395.9 14.6 all_gather.57
  412.3 15.9 while.85
  433.6 54.1 %all-gather.16.cloned.1.call-done = bf16[2048,960]{0,1:T(8,128)(2,1)} async-done(((bf16[128,960]{0,1:T(8,128)(2,1)}), bf16[2048,960]{0,1:T(8,128)(2,1)}) %all-gather.16.cloned.1.call-update) | async-done | bytes 3932176 | tf_op jit(solution)/shard_map/all_gather | solution.py:149
  487.7 4.2 fusion.262
  493.9 51.7 %all-gather.24.cloned.1.call-done = bf16[1,1,2048,960]{2,3,1,0:T(8,128)(2,1)} async-done(((bf16[1,1,128,960]{2,3,1,0:T(8,128)(2,1)}), bf16[1,1,2048,960]{2,3,1,0:T(8,128)(2,1)}) %all-gather.24.cloned.1.call-update) | async-done | bytes 3932176 | tf_op jit(solution)/shard_map/all_gather | solution.py:197
  545.6 6.5 multiply_convert_fusion.7
  553.0 4.4 fusion.253
  559.9 4.5 convolution_add_fusion.2
  564.5 76.3 %reduce-scatter.31.cloned.1.call-done = f32[128,960]{0,1:T(8,128)} async-done(((f32[2048,960]{0,1:T(8,128)}), f32[128,960]{0,1:T(8,128)}) %reduce-scatter.31.cloned.1.call-update) | async-done | bytes 491536 | tf_op jit(solution)/shard_map/reduce_scatter | solution.py:153
  652.7 14.6 all_gather.59
  669.1 12.9 while.86
  688.1 39.2 %reduce-scatter.35.cloned.1.call-done = f32[128,960]{0,1:T(8,128)} async-done(((f32[2048,960]{0,1:T(8,128)}), f32[128,960]{0,1:T(8,128)}) %reduce-scatter.35.cloned.1.call-update) | async-done | bytes 491536 | tf_op jit(solution)/shard_map/reduce_scatter | solution.py:206
  736.6 41.4 %while.87 = (s32[]{:T(128)}, f32[5,128,3,64]{1,3,2,0:T(8,128)}, bf16[5,512,64]{1,2,0:T(8,128)(2,1)}, bf16[5,512,64]{1,2,0:T(8,128)(2,1)}, bf16[5,512,64]{1,2,0:T...) while((s32[]{:T(128)}, f32[5,128,3,64]{1,3,2,0:T(8,128)}, ...), condition=%wide.region_28.29_spmd.clone, body=%wide.region_26.28_spmd.clone.sunk | while | flops 127852160 | bytes 6798977 | solution.py:126
  786.1 16.8 reduce-scatter.41.cloned.1.call-done
  810.5 3.8 multiply_reduce_fusion.8
  819.7 41.9 %all-gather.18.cloned.1.call-done = bf16[2048,960]{0,1:T(8,128)(2,1)} async-done(((bf16[128,960]{0,1:T(8,128)(2,1)}), bf16[2048,960]{0,1:T(8,128)(2,1)}) %all-gather.18.cloned.1.call-update) | async-done | bytes 3932176 | tf_op jit(solution)/shard_map/all_gather | solution.py:149
  861.6 4.3 fusion.264
  867.8 51.9 %all-gather.20.cloned.1.call-done = bf16[2048,960]{0,1:T(8,128)(2,1)} async-done(((bf16[128,960]{0,1:T(8,128)(2,1)}), bf16[2048,960]{0,1:T(8,128)(2,1)}) %all-gather.20.cloned.1.call-update) | async-done | bytes 3932176 | tf_op jit(solution)/shard_map/all_gather | solution.py:197
  919.6 6.2 multiply_convert_fusion.5
  927.2 4.5 convolution_add_fusion.1
  935.4 79.7 %reduce-scatter.37.cloned.1.call-done = f32[128,960]{0,1:T(8,128)} async-done(((f32[2048,960]{0,1:T(8,128)}), f32[128,960]{0,1:T(8,128)}) %reduce-scatter.37.cloned.1.call-update) | async-done | bytes 491536 | tf_op jit(solution)/shard_map/reduce_scatter | solution.py:206
  1022.6 41.5 %while.88 = (s32[]{:T(128)}, f32[5,128,3,64]{1,3,2,0:T(8,128)}, bf16[5,512,64]{1,2,0:T(8,128)(2,1)}, bf16[5,512,64]{1,2,0:T(8,128)(2,1)}, bf16[5,512,64]{1,2,0:T...) while((s32[]{:T(128)}, f32[5,128,3,64]{1,3,2,0:T(8,128)}, ...), condition=%wide.region_36.37_spmd.clone, body=%wide.region_34.36_spmd.clone.sunk | while | flops 127852160 | bytes 6798977 | solution.py:126
  1071.7 17.5 reduce-scatter.43.cloned.1.call-done
  1096.6 3.9 multiply_reduce_fusion.7
  1106.4 5.7 fusion.251
  1112.6 4.7 fusion.186
  1117.3 3.8 fusion.221
  1127.7 35.1 %all-gather.22.cloned.1.call-done = bf16[2048,960]{0,1:T(8,128)(2,1)} async-done(((bf16[128,960]{0,1:T(8,128)(2,1)}), bf16[2048,960]{0,1:T(8,128)(2,1)}) %all-gather.22.cloned.1.call-update) | async-done | bytes 3932176 | tf_op jit(solution)/shard_map/all_gather | solution.py:197
  1162.8 3.8 convolution_select_fusion
  1171.0 5.4 multiply_convert_fusion.3
  1181.4 4.6 fusion.212
  1188.0 5.5 fusion.266
  1193.6 8.1 convolution_add_fusion
  1207.2 3.9 fusion.288
  1211.1 4.7 fusion.293
  1215.9 34.2 %reduce-scatter.33.cloned.1.call-done = f32[128,960]{0,1:T(8,128)} async-done(((f32[2048,960]{0,1:T(8,128)}), f32[128,960]{0,1:T(8,128)}) %reduce-scatter.33.cloned.1.call-update) | async-done | bytes 491536 | tf_op jit(solution)/shard_map/reduce_scatter | solution.py:153
  1253.2 3.8 fusion.286
  1260.8 11.8 reduce-scatter.51.cloned.1.call-done
  1273.6 22.2 %reduce-scatter.49.cloned.1.call-done = bf16[240,160]{1,0:T(8,128)(2,1)} async-done(((bf16[960,160]{1,0:T(8,128)(2,1)}), bf16[240,160]{1,0:T(8,128)(2,1)}) %reduce-scatter.49.cloned.1.call-update) | async-done | bytes 76816
  1296.8 22.4 %reduce-scatter.47.cloned.1.call-done = bf16[240,160]{1,0:T(8,128)(2,1)} async-done(((bf16[960,160]{1,0:T(8,128)(2,1)}), bf16[240,160]{1,0:T(8,128)(2,1)}) %reduce-scatter.47.cloned.1.call-update) | async-done | bytes 76816
  1322.2 84.9 %reduce-scatter.39.cloned.1.call-done = f32[128,960]{0,1:T(8,128)} async-done(((f32[2048,960]{0,1:T(8,128)}), f32[128,960]{0,1:T(8,128)}) %reduce-scatter.39.cloned.1.call-update) | async-done | bytes 491536 | tf_op jit(solution)/shard_map/reduce_scatter | solution.py:206
  1412.2 34.4 %while.89 = (s32[]{:T(128)}, f32[5,128,3,64]{1,3,2,0:T(8,128)S(1)}, bf16[5,512,64]{1,2,0:T(8,128)(2,1)}, bf16[5,512,64]{1,2,0:T(8,128)(2,1)}, bf16[5,512,64]{1,2...) while((s32[]{:T(128)}, f32[5,128,3,64]{1,3,2,0:T(8,128)S(1)}, ...), condition=%wide.region_44.45_spmd.clone, body=%wide.region_42.44_spmd.clone.sunk | while | flops 127852160 | bytes 6798977 | solution.py:126
  1451.0 5.1 select_add_fusion.1
  1456.1 13.6 reduce-scatter.45.cloned.1.call-done
  1471.1 6.8 select_add_fusion
  1477.9 184.9 %fusion.334 = (f32[16,1600]{1,0:T(8,128)S(1)}, f32[16,960]{1,0:T(8,128)S(1)}) fusion(f32[960,1600]{1,0:T(8,128)} %select_add_fusion, f32[960,960]{1,0:T(8,128)} %select_add_fusion.1), kind=kCustom, calls=%all-reduce-scatter.2 | all-reduce-scatter fusion | flops 2621441 | bytes 9994752
  1662.8 11.5 collective-permute-start.10
  1674.3 5.0 collective-permute-start.8
  1679.3 11.0 collective-permute-start.9
  1690.4 5.4 collective-permute-start.4
  1695.8 6.4 collective-permute-start.11
  1705.3 148.4 %all-reduce.8 = (f32[960]{0:T(1024)S(1)}, f32[960]{0:T(1024)S(1)}) all-reduce(f32[960]{0:T(1024)S(1)} %select_add_fusion.3, f32[960]{0:T(1024)S(1)} %select_add_fusion.2), channel_id=12, replica_groups=mesh['section'=2,'gx'=4,'gy'=16] {'gx','gy'}, use_global_device_ids=true, to_apply=%region_51.52.clone | all-reduce | flops 1920 | bytes 15360
  1856.0 8.2 collective-permute-start.5
  1864.2 9.6 collective-permute-start.6
  1873.8 12.7 collective-permute-start.7
  (710 shorter events, 361.1 us)
Async XLA Ops:
  7.2 162.4 %all-gather.12.cloned.1.call-start = ((), (), s32[]{:S(2)}) async-start(), calls=%async_computation.13 | async-start | bytes 3993600 | tf_op jit(solution)/shard_map/all_gather | solution.py:263
  8.7 163.8 %all-gather.10.cloned.1.call-start = ((), (), s32[]{:S(2)}) async-start(), calls=%async_computation.12 | async-start | bytes 6489600 | tf_op jit(solution)/shard_map/all_gather | solution.py:262
  10.3 281.6 %all-gather.14.cloned.1.call-start = ((), (), s32[]{:S(2)}) async-start(), calls=%async_computation.14 | async-start | bytes 4177920 | tf_op jit(solution)/shard_map/all_gather | solution.py:149
  169.6 6.3 copy-start.115
  169.6 6.3 copy-start.105
  222.0 19.5 %copy-start.82 = (bf16[1,240,160]{1,2,0:T(8,128)(2,1)S(1)}, bf16[1,240,160]{1,2,0:T(8,128)(2,1)}, u32[]{:S(2)}) copy-start(bf16[1,240,160]{1,2,0:T(8,128)(2,1)} %param.30) | copy-start | bytes 230404
  222.9 163.7 %copy-start.8 = (f32[128,960]{0,1:T(8,128)}, f32[128,960]{0,1:T(8,128)S(1)}, u32[]{:S(2)}) copy-start(f32[128,960]{0,1:T(8,128)S(1)} %get-tuple-element.772) | copy-start | bytes 1474564
  222.9 35.5 %copy-start.83 = (bf16[1,160,240]{2,1,0:T(8,128)(2,1)S(1)}, bf16[1,160,240]{2,1,0:T(8,128)(2,1)}, u32[]{:S(2)}) copy-start(bf16[1,160,240]{2,1,0:T(8,128)(2,1)} %param.31) | copy-start | bytes 230404
  223.8 162.8 %reduce-scatter.29.cloned.1.call-start = ((), (), s32[]{:S(2)}) async-start(), calls=%async_computation.15 | async-start | bytes 8355840 | tf_op jit(solution)/shard_map/reduce_scatter | solution.py:153
  258.4 301.5 %copy-start.9 = (bf16[1,960,160]{1,2,0:T(8,128)(2,1)}, bf16[1,960,160]{1,2,0:T(8,128)(2,1)S(1)}, u32[]{:S(2)}) copy-start(bf16[1,960,160]{1,2,0:T(8,128)(2,1)S(1)} %copy.97) | copy-start | bytes 921604
  275.4 22.1 %copy-start.31 = (bf16[1,160,960]{2,1,0:T(8,128)(2,1)}, bf16[1,160,960]{2,1,0:T(8,128)(2,1)S(1)}, u32[]{:S(2)}) copy-start(bf16[1,160,960]{2,1,0:T(8,128)(2,1)S(1)} %copy.99) | copy-start | bytes 921604
  302.8 86.7 %copy-start.88 = (f32[128,32]{0,1:T(8,128)S(1)}, f32[128,32]{0,1:T(8,128)}, u32[]{:S(2)}) copy-start(f32[128,32]{0,1:T(8,128)} %get-tuple-element.757) | copy-start | bytes 49156
  302.8 86.7 %copy-start.87 = (f32[128,32]{0,1:T(8,128)S(1)}, f32[128,32]{0,1:T(8,128)}, u32[]{:S(2)}) copy-start(f32[128,32]{0,1:T(8,128)} %get-tuple-element.758) | copy-start | bytes 49156
  302.8 184.9 %all-gather.16.cloned.1.call-start = ((), (), s32[]{:S(2)}) async-start(), calls=%async_computation.16 | async-start | bytes 4177920 | tf_op jit(solution)/shard_map/all_gather | solution.py:149
  387.7 2.4 collective-permute-start
  428.2 63.6 %copy-start.91 = (f32[5,3,128,1]{2,1,3,0:T(4,128)}, f32[5,3,128,1]{2,1,3,0:T(4,128)S(1)}, u32[]{:S(2)}) copy-start(f32[5,3,128,1]{2,1,3,0:T(4,128)S(1)} %get-tuple-element.289) | copy-start | bytes 23044
  430.8 61.0 %copy-start.116 = (f32[128]{0:T(128)}, f32[128]{0:T(128)S(1)}, u32[]{:S(2)}) copy-start(f32[128]{0:T(128)S(1)} %get-tuple-element.775) | copy-start | bytes 1540
  431.8 113.8 %all-gather.24.cloned.1.call-start = ((), (), s32[]{:S(2)}) async-start(), calls=%async_computation.25 | async-start | bytes 4177920 | tf_op jit(solution)/shard_map/all_gather | solution.py:197
  433.5 207.3 %reduce-scatter.31.cloned.1.call-start = ((), (), s32[]{:S(2)}) async-start(), calls=%async_computation.17 | async-start | bytes 8355840 | tf_op jit(solution)/shard_map/reduce_scatter | solution.py:153
  545.6 7.3 copy-start.32
  557.4 169.9 %reduce-scatter.35.cloned.1.call-start = ((), (), s32[]{:S(2)}) async-start(), calls=%async_computation.20 | async-start | bytes 8355840 | tf_op jit(solution)/shard_map/reduce_scatter | solution.py:206
  564.4 82.1 %copy-start.12 = (bf16[2,1,128,960]{2,3,1,0:T(8,128)(2,1)S(1)}, bf16[2,1,128,960]{2,3,1,0:T(8,128)(2,1)}, u32[]{:S(2)}) copy-start(bf16[2,1,128,960]{2,3,1,0:T(8,128)(2,1)} %param.22) | copy-start | bytes 1474564
  564.4 238.5 %reduce-scatter.41.cloned.1.call-start = ((), (), s32[]{:S(2)}) async-start(), calls=%async_computation.26 | async-start | bytes 819200
  642.8 3.7 collective-permute-start.1
  669.1 15.6 copy-start.117
  727.3 6.3 copy-start.90
  727.3 6.3 copy-start.92
  727.3 6.3 copy-start.94
  782.1 79.4 %all-gather.18.cloned.1.call-start = ((), (), s32[]{:S(2)}) async-start(), calls=%async_computation.18 | async-start | bytes 4177920 | tf_op jit(solution)/shard_map/all_gather | solution.py:149
  782.7 136.9 %all-gather.20.cloned.1.call-start = ((), (), s32[]{:S(2)}) async-start(), calls=%async_computation.21 | async-start | bytes 4177920 | tf_op jit(solution)/shard_map/all_gather | solution.py:197
  810.5 8.2 copy-start.48
  815.2 3.4 collective-permute-start.2
  819.4 195.7 %reduce-scatter.37.cloned.1.call-start = ((), (), s32[]{:S(2)}) async-start(), calls=%async_computation.22 | async-start | bytes 8355840 | tf_op jit(solution)/shard_map/reduce_scatter | solution.py:206
  931.7 83.4 %copy-start.110 = (f32[128]{0:T(128)S(1)}, f32[128]{0:T(128)}, u32[]{:S(2)}) copy-start(f32[128]{0:T(128)} %get-tuple-element.769) | copy-start | bytes 1540
  931.7 157.4 %reduce-scatter.43.cloned.1.call-start = ((), (), s32[]{:S(2)}) async-start(), calls=%async_computation.27 | async-start | bytes 819200
  1068.3 94.6 %all-gather.22.cloned.1.call-start = ((), (), s32[]{:S(2)}) async-start(), calls=%async_computation.23 | async-start | bytes 4177920 | tf_op jit(solution)/shard_map/all_gather | solution.py:197
  1096.6 8.9 copy-start.49
  1102.2 3.4 collective-permute-start.3
  1106.3 143.7 %reduce-scatter.33.cloned.1.call-start = ((), (), s32[]{:S(2)}) async-start(), calls=%async_computation.19 | async-start | bytes 8355840 | tf_op jit(solution)/shard_map/reduce_scatter | solution.py:153
  1112.1 160.5 %reduce-scatter.51.cloned.1.call-start = ((), (), s32[]{:S(2)}) async-start(), calls=%async_computation.31 | async-start | bytes 614400
  1170.9 124.9 %reduce-scatter.49.cloned.1.call-start = ((), (), s32[]{:S(2)}) async-start(), calls=%async_computation.30 | async-start | bytes 614400
  1171.0 6.3 copy-start.3
  1171.0 6.3 copy-start.6
  1181.3 137.9 %reduce-scatter.47.cloned.1.call-start = ((), (), s32[]{:S(2)}) async-start(), calls=%async_computation.29 | async-start | bytes 614400
  1193.5 213.6 %reduce-scatter.39.cloned.1.call-start = ((), (), s32[]{:S(2)}) async-start(), calls=%async_computation.24 | async-start | bytes 8355840 | tf_op jit(solution)/shard_map/reduce_scatter | solution.py:206
  1201.7 9.4 copy-start.69
  1201.7 268.0 %reduce-scatter.45.cloned.1.call-start = ((), (), s32[]{:S(2)}) async-start(), calls=%async_computation.28 | async-start | bytes 819200
  1203.2 7.9 copy-start.57
  1203.2 7.9 copy-start.71
  1211.1 42.1 %copy-start.39 = (bf16[5,128,3,64]{1,3,2,0:T(8,128)(2,1)S(1)}, bf16[5,128,3,64]{1,3,2,0:T(8,128)(2,1)}, u32[]{:S(2)}) copy-start(bf16[5,128,3,64]{1,3,2,0:T(8,128)(2,1)} %copy-done.38) | copy-start | bytes 737284
  1257.1 150.1 %copy-start.109 = (f32[128]{0:T(128)S(1)}, f32[128]{0:T(128)}, u32[]{:S(2)}) copy-start(f32[128]{0:T(128)} %get-tuple-element.767) | copy-start | bytes 1540
  1451.0 20.1 %copy-start.20 = (bf16[128,960]{0,1:T(8,128)(2,1)S(1)}, bf16[128,960]{0,1:T(8,128)(2,1)}, u32[]{:S(2)}) copy-start(bf16[128,960]{0,1:T(8,128)(2,1)} %copy-done.18) | copy-start | bytes 737284
  1451.0 20.1 %copy-start.108 = (f32[128]{0:T(128)S(1)}, f32[128]{0:T(128)}, u32[]{:S(2)}) copy-start(f32[128]{0:T(128)} %copy-done.107) | copy-start | bytes 1540
  1477.9 224.3 %copy-start.114 = (f32[128]{0:T(128)S(1)}, f32[128]{0:T(128)}, u32[]{:S(2)}) copy-start(f32[128]{0:T(128)} %get-tuple-element.753) | copy-start | bytes 1540
  1662.8 201.3 %collective-permute-start.10 = (f32[16,960]{1,0:T(8,128)S(1)}, f32[16,960]{1,0:T(8,128)S(1)}, u32[]{:S(2)}, u32[]{:S(2)}) collective-permute-start(f32[16,960]{1,0:T(8,128)S(1)} %get-tuple-element.637), channel_id=1, source_target_pairs={{0,3},{1,4},{2,5},{3,6},{4,7},{5,8},{6,9},{7,10},{8,11},{9,12},{10... | collective-permute-start | bytes 184328
  1674.3 199.5 %collective-permute-start.8 = (f32[16,960]{1,0:T(8,128)S(1)}, f32[16,960]{1,0:T(8,128)}, u32[]{:S(2)}, u32[]{:S(2)}) collective-permute-start(f32[16,960]{1,0:T(8,128)S(1)} %get-tuple-element.637), channel_id=1, source_target_pairs={{0,1},{1,2},{2,3},{3,4},{4,5},{5,6},{6,7},{7,8},{8,9},{9,10},{10,1... | collective-permute-start | bytes 184328
  1679.3 207.2 %collective-permute-start.9 = (f32[16,960]{1,0:T(8,128)S(1)}, f32[16,960]{1,0:T(8,128)}, u32[]{:S(2)}, u32[]{:S(2)}) collective-permute-start(f32[16,960]{1,0:T(8,128)S(1)} %get-tuple-element.637), channel_id=1, source_target_pairs={{0,2},{1,3},{2,4},{3,5},{4,6},{5,7},{6,8},{7,9},{8,10},{9,11},{10,... | collective-permute-start | bytes 184328
  1690.4 199.9 %collective-permute-start.4 = (f32[16,1600]{1,0:T(8,128)S(1)}, f32[16,1600]{1,0:T(8,128)S(1)}, u32[]{:S(2)}, u32[]{:S(2)}) collective-permute-start(f32[16,1600]{1,0:T(8,128)S(1)} %get-tuple-element.636), channel_id=1, source_target_pairs={{0,1},{1,2},{2,3},{3,4},{4,5},{5,6},{6,7},{7,8},{8,9},{9,10},{10,1... | collective-permute-start | bytes 307208
  1695.8 160.2 %collective-permute-start.11 = (f32[15,960]{1,0:T(8,128)S(1)}, f32[15,960]{1,0:T(8,128)}, u32[]{:S(2)}, u32[]{:S(2)}) collective-permute-start(f32[15,960]{1,0:T(8,128)S(1)} %slice.292), channel_id=1, source_target_pairs={{0,4},{1,5},{2,6},{3,7},{4,8},{5,9},{6,10},{7,11},{8,12},{9,13},{1... | collective-permute-start | bytes 172808
  1702.2 152.1 %copy-start.62 = (bf16[128,960]{0,1:T(8,128)(2,1)S(1)}, bf16[128,960]{0,1:T(8,128)(2,1)}, u32[]{:S(2)}) copy-start(bf16[128,960]{0,1:T(8,128)(2,1)} %copy-done.61) | copy-start | bytes 737284
  1702.2 152.4 %copy-start.63 = (bf16[1,128,960]{1,2,0:T(8,128)(2,1)S(1)}, bf16[1,128,960]{1,2,0:T(8,128)(2,1)}, u32[]{:S(2)}) copy-start(bf16[1,128,960]{1,2,0:T(8,128)(2,1)} %get-tuple-element.638) | copy-start | bytes 737284
  1856.0 34.3 %collective-permute-start.5 = (f32[16,1600]{1,0:T(8,128)S(1)}, f32[16,1600]{1,0:T(8,128)S(1)}, u32[]{:S(2)}, u32[]{:S(2)}) collective-permute-start(f32[16,1600]{1,0:T(8,128)S(1)} %get-tuple-element.636), channel_id=1, source_target_pairs={{0,2},{1,3},{2,4},{3,5},{4,6},{5,7},{6,8},{7,9},{8,10},{9,11},{10,... | collective-permute-start | bytes 307208
  1864.2 26.1 %collective-permute-start.6 = (f32[16,1600]{1,0:T(8,128)S(1)}, f32[16,1600]{1,0:T(8,128)S(1)}, u32[]{:S(2)}, u32[]{:S(2)}) collective-permute-start(f32[16,1600]{1,0:T(8,128)S(1)} %get-tuple-element.636), channel_id=1, source_target_pairs={{0,3},{1,4},{2,5},{3,6},{4,7},{5,8},{6,9},{7,10},{8,11},{9,12},{10... | collective-permute-start | bytes 307208
  1873.8 16.4 collective-permute-start.7
  (90 other events, 259.7 us)
Sparse Core Ops, SparseCore 0:
  11.3 66.6 all-gather.11
  81.5 72.0 all-gather.9
  223.9 67.8 all-gather.13
  303.0 83.5 reduce-scatter.28
  431.9 55.7 all-gather.15
  489.9 55.6 all-gather.23
  557.5 83.2 reduce-scatter.30
  644.3 82.9 reduce-scatter.34
  782.3 20.6 reduce-scatter.40
  805.1 56.3 all-gather.17
  863.9 55.7 all-gather.19
  931.8 83.2 reduce-scatter.36
  1068.4 20.6 reduce-scatter.42
  1106.4 56.3 all-gather.21
  1166.2 83.8 reduce-scatter.32
  1252.4 20.0 reduce-scatter.50
  1274.8 20.9 reduce-scatter.48
  1298.2 20.9 reduce-scatter.46
  1322.7 84.4 reduce-scatter.38
  1449.0 20.5 reduce-scatter.44
where the time goes:
time: 1910 us; the launch traced here: 1900 us
  waiting for transfers between devices  759 us (40%)
  blocking collectives  582 us (30%)
  matrix products  297 us (16%)
  local copies, waits for them, and re-layouts  89.1 us (5%)
  starting transfers between devices  77.9 us (4%)
  other arithmetic  74.1 us (4%)
    unnamed x3, blocking collectives  484 us
    reduce_scatter x3, waiting for transfers between devices, backward_layer(): lax.psum_scatter(first_term + jnp.einsum('nf,df->nd', d_up, up_matrix, pr...  204 us
    reduce_scatter x3, waiting for transfers between devices, forward_layer(): lax.psum_scatter(jnp.dot(hidden, down_matrix, preferred_element_type=jnp....  194 us
    all_gather x3, waiting for transfers between devices, backward_layer(): d_rows = lax.all_gather(d_branch, 'gy', axis=0, tiled=True)  139 us
    all_gather x3, waiting for transfers between devices, forward_layer(): normed_rows = lax.all_gather(normed_two, 'gy', axis=0, tiled=True)  112 us
    unnamed x34, waiting for transfers between devices  105 us
    unnamed x14, starting transfers between devices  70.7 us
    all_gather x3, blocking collectives, forward_layer(): kv_all = lax.all_gather(kv_local, 'gx', axis=0, tiled=True)  54.8 us
  transfers between devices with their start and end apart: 32, of which 21 were waited for; matrix products, arithmetic and copies ran while one was open for 10% of the time, Pallas kernels for 0%

commit v1 on v0

v1 whole, which is shorter than its diff:
```python
import functools

import jax
import jax.numpy as jnp
from jax import lax
from jax.experimental import pallas as pl
from jax.experimental.pallas import tpu as pltpu
from jax.sharding import PartitionSpec as P

HQ, HK, HD = 15, 5, 64
D, QW, KW = 960, 960, 320
TOK, LEN = 128, 512
WA = 1024
QKVW = 1792
FROWS, AROWS = 480, 176
epsilon = 1e-05
rope_base = 100000.0
masked_score = -1e30
VMEM = 60 * 2**20
bf16, f32 = jnp.bfloat16, jnp.float32


def nn(a, b):
    return jnp.dot(a, b, preferred_element_type=f32)


def nt(a, b):
    return lax.dot_general(a, b, (((1,), (1,)), ((), ())), preferred_element_type=f32)


def tn(a, b):
    return lax.dot_general(a, b, (((0,), (0,)), ((), ())), preferred_element_type=f32)


def call(kernel, outs, ins, specs=None, scratch=(), grid=None, out_specs=None, name=None):
    vm = pl.BlockSpec(memory_space=pltpu.VMEM)
    kwargs = {}
    if grid is not None:
        kwargs["grid"] = grid
    return pl.pallas_call(
        kernel,
        out_shape=outs,
        in_specs=specs if specs is not None else [vm] * len(ins),
        out_specs=out_specs if out_specs is not None else [vm] * len(outs),
        scratch_shapes=list(scratch),
        compiler_params=pltpu.CompilerParams(vmem_limit_bytes=VMEM),
        name=name,
        **kwargs,
    )(*ins)


def sds(shape, dt):
    return jax.ShapeDtypeStruct(shape, dt)


def pick(sel_ref, own, recv, first, rows, buf, sem):
    @pl.when(sel_ref[0] == 0)
    def _():
        pltpu.make_async_copy(own.at[:, pl.ds(first, rows), :], buf, sem).start()

    @pl.when(sel_ref[0] != 0)
    def _():
        pltpu.make_async_copy(recv.at[:, pl.ds(first, rows), :], buf, sem).start()


def arrived(own, first, rows, buf, sem):
    pltpu.make_async_copy(own.at[:, pl.ds(first, rows), :], buf, sem).wait()


def chunk_of(buf, j):
    return buf[:, 16 * j : 16 * j + 16, :].reshape(WA, 256)


def rstd_of(v):
    return lax.rsqrt(jnp.sum(v * v, axis=1, keepdims=True) * (1.0 / D) + epsilon)


def lane_in_head(shape):
    return lax.broadcasted_iota(jnp.int32, shape, 1) % HD


def project_kernel(has_x, sel, own, recv, pab, pba, cosw, sinw, *rest):
    if has_x:
        x_ref, norm_ref, qkv_ref, kv_ref, gain_ref, buf, sem = rest
    else:
        mid_ref, yo_ref, yr_ref, x_out, norm_ref, qkv_ref, kv_ref, gain_ref, buf, sem = rest
    pick(sel, own, recv, 0, 112, buf, sem)
    if has_x:
        x = x_ref[...].astype(f32)
    else:
        xb = (mid_ref[...] + yo_ref[...] + yr_ref[...]).astype(bf16)
        x_out[...] = xb
        x = xb.astype(f32)
    rstd = rstd_of(x)
    arrived(own, 0, 112, buf, sem)
    gains = nn(chunk_of(buf, 6).astype(f32).T.astype(bf16), pba[...])[64:72, :]
    gain_ref[...] = gains
    normed = (x * rstd * gains[0:1, :]).astype(bf16)
    norm_b = nn(normed, pab[...]).astype(bf16)
    norm_ref[...] = norm_b
    proj = jnp.concatenate([nn(norm_b, chunk_of(buf, j)) for j in range(7)], axis=1)
    low = lane_in_head(proj.shape) < HD // 2
    turned = jnp.where(low, -pltpu.roll(proj, QKVW - 32, 1), pltpu.roll(proj, 32, 1))
    out = (proj * cosw[...] + turned * sinw[...]).astype(bf16)
    qkv_ref[...] = out
    kv_ref[...] = out[:, : 2 * KW]


def heads_of(ref, base, i):
    return jnp.concatenate([ref[:, base + HD * (3 * i + h) : base + HD * (3 * i + h + 1)] for h in range(3)], axis=0)


def softmax_terms(q3, kg, allowed3):
    scores = nt(q3, kg) * 0.125
    scores = jnp.where(allowed3, scores, masked_score)
    highest = jnp.max(scores, axis=1, keepdims=True)
    terms = jnp.exp(scores - highest)
    return terms / jnp.sum(terms, axis=1, keepdims=True)


def attend_kernel(sel, own, recv, qkv, r1, r2, r3, mask, x_ref, gain_ref, pnb, attb_ref, mid_ref, n2_ref, buf, kvs, att, sem):
    pick(sel, own, recv, 112, 64, buf, sem)
    for k, part in enumerate((r3, r2, r1)):
        kvs[TOK * k : TOK * k + TOK, :] = part[...]
    kvs[3 * TOK :, :] = qkv[:, : 2 * KW]
    allowed = mask[...] > 0.5
    allowed3 = jnp.concatenate([allowed] * 3, axis=0)
    for i in range(HK):
        kg = kvs[:, HD * i : HD * i + HD]
        vg = kvs[:, KW + HD * i : KW + HD * i + HD]
        probs = softmax_terms(heads_of(qkv, 2 * KW, i), kg, allowed3).astype(bf16)
        o3 = nn(probs, vg).astype(bf16)
        for h in range(3):
            lane = HD * (3 * i + h)
            att[:, lane : lane + HD] = o3[TOK * h : TOK * h + TOK, :]
    attb = nn(att[...], pnb[...]).astype(bf16)
    attb_ref[...] = attb
    arrived(own, 112, 64, buf, sem)
    out = jnp.concatenate([nn(attb, chunk_of(buf, j)) for j in range(4)], axis=1)
    mid = x_ref[...].astype(f32) + out
    mid_ref[...] = mid
    n2_ref[...] = (mid * rstd_of(mid) * gain_ref[1:2, :]).astype(bf16)


def hidden_parts(xs, wg, wu):
    gate = up = None
    for g in range(4):
        xg = xs[:, 256 * g : 256 * g + 256]
        a, b = nt(xg, wg[g].reshape(320, 256)), nt(xg, wu[g].reshape(320, 256))
        gate, up = (a, b) if g == 0 else (gate + a, up + b)
    return gate, up, 1.0 / (1.0 + jnp.exp(-gate))


def ffn_kernel(xo, xr, wg, wu, wd, yo, yr):
    j = pl.program_id(0)

    @pl.when(j == 0)
    def _():
        yo[...] = jnp.zeros_like(yo)
        yr[...] = jnp.zeros_like(yr)

    xs = jnp.concatenate([xo[...], xr[...]], axis=0)
    gate, up, sigma = hidden_parts(xs, wg, wu)
    hidden = (gate * sigma * up).astype(bf16)
    for g in range(4):
        y = nn(hidden, wd[g].reshape(320, 256))
        yo[:, 256 * g : 256 * g + 256] += y[:TOK]
        yr[:, 256 * g : 256 * g + 256] += y[TOK:]


def ffn_back_kernel(xo, xr, do, dr, wg, wu, wd, grads, no, nr):
    j = pl.program_id(0)

    @pl.when(j == 0)
    def _():
        no[...] = jnp.zeros_like(no)
        nr[...] = jnp.zeros_like(nr)

    xs = jnp.concatenate([xo[...], xr[...]], axis=0)
    ds = jnp.concatenate([do[...], dr[...]], axis=0)
    gate, up, sigma = hidden_parts(xs, wg, wu)
    hidden = gate * sigma * up
    d_hidden = None
    for g in range(4):
        a = nt(ds[:, 256 * g : 256 * g + 256], wd[g].reshape(320, 256))
        d_hidden = a if g == 0 else d_hidden + a
    d_gate = (d_hidden * up * sigma * (1.0 + gate * (1.0 - sigma))).astype(bf16)
    d_up = (d_hidden * gate * sigma).astype(bf16)
    hid_t = hidden.astype(bf16).T
    dg_t = d_gate.T
    du_t = d_up.T
    for g in range(4):
        xg = xs[:, 256 * g : 256 * g + 256]
        grads[g, :, 0:80, :] = nn(dg_t, xg).astype(bf16).reshape(4, 80, 256)
        grads[g, :, 80:160, :] = nn(du_t, xg).astype(bf16).reshape(4, 80, 256)
        grads[g, :, 160:240, :] = nn(hid_t, ds[:, 256 * g : 256 * g + 256]).astype(bf16).reshape(4, 80, 256)
        dn = nn(d_gate, wg[g].reshape(320, 256)) + nn(d_up, wu[g].reshape(320, 256))
        no[:, 256 * g : 256 * g + 256] += dn[:TOK]
        nr[:, 256 * g : 256 * g + 256] += dn[TOK:]


def norm_back(e, z, rstd):
    return rstd * (e - z * (jnp.sum(e * z, axis=1, keepdims=True) * (1.0 / D)))


def attend_back_kernel(
    sel, own, recv, no, nr, mid_ref, gain_ref, dy_ref, qkv, r1, r2, r3, mask, pnb,
    dmid_ref, dproj_ref, gg_ref, dq_ref, dkv_ref, d1, d2, d3, buf, kvs, dkv, sem,
):
    pick(sel, own, recv, 112, 64, buf, sem)
    for k, part in enumerate((r3, r2, r1)):
        kvs[TOK * k : TOK * k + TOK, :] = part[...]
    kvs[3 * TOK :, :] = qkv[:, : 2 * KW]
    mid = mid_ref[...]
    rstd = rstd_of(mid)
    z = mid * rstd
    dn = no[...] + nr[...]
    gg_ref[...] = jnp.broadcast_to(jnp.sum(dn * z, axis=0, keepdims=True), gg_ref.shape)
    dmid = dy_ref[...].astype(f32) + norm_back(dn * gain_ref[1:2, :], z, rstd)
    dmid_ref[...] = dmid
    dproj = dmid.astype(bf16)
    dproj_ref[...] = dproj
    arrived(own, 112, 64, buf, sem)
    datt = None
    for j in range(4):
        a = nt(dproj[:, 256 * j : 256 * j + 256], chunk_of(buf, j))
        datt = a if j == 0 else datt + a
    datt = nt(datt.astype(bf16), pnb[...]).astype(bf16)
    allowed = mask[...] > 0.5
    allowed3 = jnp.concatenate([allowed] * 3, axis=0)
    dq_ref[:, 896:] = jnp.zeros((TOK, 256), f32)
    for i in range(HK):
        kg = kvs[:, HD * i : HD * i + HD]
        vg = kvs[:, KW + HD * i : KW + HD * i + HD]
        q3 = heads_of(qkv, 2 * KW, i)
        do3 = jnp.concatenate([datt[:, HD * (3 * i + h) : HD * (3 * i + h + 1)] for h in range(3)], axis=0)
        probs = softmax_terms(q3, kg, allowed3)
        d_probs = nt(do3, vg)
        inner = jnp.sum(probs * d_probs, axis=1, keepdims=True)
        d_scores = (probs * (d_probs - inner)).astype(bf16)
        dq3 = nn(d_scores, kg) * 0.125
        for h in range(3):
            lane = HD * (3 * i + h)
            dq_ref[:, lane : lane + HD] = dq3[TOK * h : TOK * h + TOK, :]
        dkv[:, HD * i : HD * i + HD] = tn(d_scores, q3) * 0.125
        dkv[:, KW + HD * i : KW + HD * i + HD] = tn(probs.astype(bf16), do3)
    dkv_ref[...] = dkv[3 * TOK :, :]
    for k, part in enumerate((d3, d2, d1)):
        part[...] = dkv[TOK * k : TOK * k + TOK, :].astype(bf16)


def split3(v):
    hi = v.astype(bf16)
    rest = v - hi.astype(f32)
    middle = rest.astype(bf16)
    return hi, middle, (rest - middle.astype(f32)).astype(bf16)


def project_back_kernel(
    sel, own, recv, dq, dkv, e1, e2, e3, cosw, sinw, norm_ref, x_ref, gain_ref, dmid_ref, pba, attb, dproj, gg,
    dx_ref, grads, buf, sem,
):
    pick(sel, own, recv, 0, 112, buf, sem)
    kv = dkv[...] + e1[...].astype(f32) + e2[...].astype(f32) + e3[...].astype(f32)
    d = jnp.concatenate([kv, dq[...]], axis=1)
    low = lane_in_head(d.shape) < HD // 2
    scaled = d * sinw[...]
    turned = jnp.where(low, pltpu.roll(scaled, QKVW - 32, 1), -pltpu.roll(scaled, 32, 1))
    dp = (d * cosw[...] + turned).astype(bf16)
    arrived(own, 0, 112, buf, sem)
    dn_b = None
    for j in range(7):
        a = nt(dp[:, 256 * j : 256 * j + 256], chunk_of(buf, j))
        dn_b = a if j == 0 else dn_b + a
    hi, middle, lo = split3(dn_b)
    dn = nn(hi, pba[...]) + nn(middle, pba[...]) + nn(lo, pba[...])
    x = x_ref[...].astype(f32)
    rstd = rstd_of(x)
    z = x * rstd
    g1 = jnp.sum(dn * z, axis=0, keepdims=True)
    dx_ref[...] = (dmid_ref[...] + norm_back(dn * gain_ref[0:1, :], z, rstd)).astype(bf16)
    row = lax.broadcasted_iota(jnp.int32, (256, WA), 0)
    gains = jnp.where(row == 64, g1, jnp.where(row == 65, gg[0:1, :], 0.0)).astype(bf16)
    norm_t = norm_ref[...].T
    for j in range(7):
        g = nn(norm_t, dp[:, 256 * j : 256 * j + 256])
        if j == 6:
            g = g + nt(pba[...], gains)
        grads[:, 16 * j : 16 * j + 16, :] = g.astype(bf16).reshape(64, 16, 256)
    att_t = attb[...].T
    for j in range(4):
        g = nn(att_t, dproj[:, 256 * j : 256 * j + 256])
        grads[:, 112 + 16 * j : 128 + 16 * j, :] = g.astype(bf16).reshape(64, 16, 256)
    grads[:, 176:192, :] = jnp.zeros((64, 16, 256), bf16)


VM = pl.BlockSpec(memory_space=pltpu.VMEM)
ANY = pl.BlockSpec(memory_space=pl.ANY)
SM = pl.BlockSpec(memory_space=pltpu.SMEM)


def weight_scratch(rows):
    return pltpu.VMEM((64, rows, 256), bf16)


def project(sel, own, recv, pab, pba, cosw, sinw, x=None, parts=None):
    outs = [sds((TOK, WA), bf16), sds((TOK, QKVW), bf16), sds((TOK, 2 * KW), bf16), sds((8, WA), f32)]
    ins = [sel, own, recv, pab, pba, cosw, sinw] + ([x] if parts is None else list(parts))
    if parts is not None:
        outs = [sds((TOK, WA), bf16)] + outs
    res = call(
        functools.partial(project_kernel, parts is None),
        outs, ins, [SM, ANY, ANY] + [VM] * (len(ins) - 3),
        [weight_scratch(112), pltpu.SemaphoreType.DMA], name="project",
    )
    return ([x] + list(res)) if parts is None else res


def attend(sel, own, recv, qkv, chunks, mask, x, gains, pnb):
    ins = [sel, own, recv, qkv, *chunks, mask, x, gains, pnb]
    return call(
        attend_kernel,
        [sds((TOK, WA), bf16), sds((TOK, WA), f32), sds((TOK, WA), bf16)],
        ins, [SM, ANY, ANY] + [VM] * (len(ins) - 3),
        [weight_scratch(64), pltpu.VMEM((LEN, 2 * KW), bf16), pltpu.VMEM((TOK, QW), bf16), pltpu.SemaphoreType.DMA],
        name="attend",
    )


def weight_specs(section):
    return [pl.BlockSpec((4, 4, 80, 256), lambda j, m=m: (0, j, 3 * section + m, 0)) for m in range(3)]


def whole(shape):
    return pl.BlockSpec(shape, lambda j: (0,) * len(shape))


def ffn(section, xo, xr, packed):
    row = whole((TOK, WA))
    return call(
        ffn_kernel, [sds((TOK, WA), f32)] * 2, [xo, xr, packed, packed, packed],
        [row, row] + weight_specs(section), grid=(4,), out_specs=[row, row], name="ffn",
    )


def ffn_back(section, xo, xr, do, dr, packed):
    row = whole((TOK, WA))
    return call(
        ffn_back_kernel, [sds((4, 16, 240, 256), bf16)] + [sds((TOK, WA), f32)] * 2,
        [xo, xr, do, dr, packed, packed, packed],
        [row] * 4 + weight_specs(section), grid=(4,),
        out_specs=[pl.BlockSpec((4, 4, 240, 256), lambda j: (0, j, 0, 0)), row, row], name="ffn_back",
    )


def attend_back(sel, own, recv, no, nr, mid, gains, dy, qkv, chunks, mask, pnb):
    ins = [sel, own, recv, no, nr, mid, gains, dy, qkv, *chunks, mask, pnb]
    small = sds((TOK, 2 * KW), bf16)
    return call(
        attend_back_kernel,
        [sds((TOK, WA), f32), sds((TOK, WA), bf16), sds((8, WA), f32), sds((TOK, 1152), f32), sds((TOK, 2 * KW), f32), small, small, small],
        ins, [SM, ANY, ANY] + [VM] * (len(ins) - 3),
        [weight_scratch(64), pltpu.VMEM((LEN, 2 * KW), bf16), pltpu.VMEM((LEN, 2 * KW), f32), pltpu.SemaphoreType.DMA],
        name="attend_back",
    )


def project_back(sel, own, recv, *rest):
    ins = [sel, own, recv, *rest]
    return call(
        project_back_kernel, [sds((TOK, WA), bf16), sds((64, 192, 256), bf16)],
        ins, [SM, ANY, ANY] + [VM] * (len(ins) - 3),
        [weight_scratch(112), pltpu.SemaphoreType.DMA], name="project_back",
    )


def other_core(v):
    return lax.ppermute(v, "section", [(0, 1), (1, 0)])


def shift_perm(name, k):
    if name == "x":
        return "gx", [(i, (i + k) % 4) for i in range(4)]
    if name == "z":
        return "gy", [(i, (i + 4 * k) % 16) for i in range(16)]
    return "gy", [(i, (i // 4) * 4 + (i % 4 + k) % 4) for i in range(16)]


def reduce_stage(v, dim, name, me):
    got = []
    for k in (1, 3, 2):
        piece = lax.dynamic_index_in_dim(v, (me + k) % 4, dim, keepdims=False)
        axis, perm = shift_perm(name, k)
        got.append(lax.ppermute(piece, axis, perm))
    total = lax.dynamic_index_in_dim(v, me, dim, keepdims=False).astype(f32)
    for piece in got:
        total = total + piece.astype(f32)
    return total.astype(bf16)


def reduce_parts(parts, place):
    names = ["x", "z", "y"]
    orders = [["x", "y", "z"], ["y", "z", "x"], ["z", "x", "y"]]
    state = [(p, list(names)) for p in parts]
    for step in range(3):
        after = []
        for index, (v, left) in enumerate(state):
            name = orders[index % 3][step]
            dim = left.index(name)
            v = reduce_stage(v, dim, name, place[name])
            after.append((v, [n for n in left if n != name]))
        state = after
    return [v for v, _ in state]


def rope_tables(positions):
    frequency = rope_base ** (-(jnp.arange(HD // 2, dtype=f32) * 2.0) / HD)
    angles = positions.astype(f32)[:, None] * frequency[None, :]
    cosine, sine = jnp.cos(angles), jnp.sin(angles)
    cosine, sine = jnp.concatenate([cosine, cosine], 1), jnp.concatenate([sine, sine], 1)

    def wide(table, plain):
        rest = jnp.full((TOK, KW), plain, f32)
        return jnp.concatenate([jnp.tile(table, (1, HK)), rest, jnp.tile(table, (1, HQ)), jnp.full((TOK, 192), plain, f32)], 1)

    return wide(cosine, 1.0), wide(sine, 0.0)


def to_a(v):
    rows = v.shape[0]
    return jnp.pad(v.reshape(rows, 4, 240), ((0, 0), (0, 0), (0, 16))).reshape(rows, WA)


def from_a(v):
    return v.reshape(v.shape[:-1] + (4, 256))[..., :240].reshape(v.shape[:-1] + (D,))


def place_matrices():
    a = jnp.arange(WA, dtype=jnp.int32)
    in_a = jnp.where(a % 256 < 240, (a // 256) * 240 + a % 256, -1)
    in_b = jnp.where(a % 16 < 15, (a // 16) * 15 + a % 16, -2)
    pab = (in_a[:, None] == in_b[None, :]).astype(bf16)
    pba = (in_b[:, None] == in_a[None, :]).astype(bf16)
    pnb = (jnp.arange(QW, dtype=jnp.int32)[:, None] == in_b[None, :]).astype(bf16)
    return pab, pba, pnb


def per_device(inputs, cotangent, segment_ids, gain_attn, w_qkv, w_out, gain_ffn, w_gate, w_up, w_down):
    core = lax.axis_index("section")
    gx = lax.axis_index("gx")
    gy = lax.axis_index("gy")
    first = core == 0
    place = {"x": gx, "z": gy // 4, "y": gy % 4}

    pieces = jnp.stack([w_gate[0].T, w_up[0].T, w_down[0]]).reshape(3, 2, 80, 240)
    keep = jnp.where(first, pieces[:, 0], pieces[:, 1])
    got = other_core(jnp.where(first, pieces[:, 1], pieces[:, 0]))
    halves = jnp.concatenate([jnp.where(first, keep, got), jnp.where(first, got, keep)], 0)
    halves = jnp.pad(halves.reshape(FROWS, 240), ((0, 0), (0, 16)))
    attn = jnp.concatenate(
        [
            w_qkv[0][:, QW:],
            w_qkv[0][:, :QW],
            gain_attn[0][:, None],
            gain_ffn[0][:, None],
            jnp.zeros((15, 190), bf16),
            to_a(w_out[0]),
        ],
        1,
    )
    attn = jnp.pad(attn, ((0, 1), (0, 0))).reshape(16, 11, 256).transpose(1, 0, 2).reshape(AROWS, 256)
    packed = lax.all_gather(jnp.concatenate([halves, attn], 0)[None], ("gx", "gy"), axis=0, tiled=True)
    own = packed[:, FROWS:, :]
    recv = other_core(own)
    packed = packed.reshape(4, 16, FROWS + AROWS, 256)

    own_in = to_a(jnp.where(first, inputs[0, 0], inputs[1, 0]))
    cot0, cot1 = to_a(cotangent[0, 0]), to_a(cotangent[1, 0])
    cot_own, cot_other = jnp.where(first, cot0, cot1), jnp.where(first, cot1, cot0)
    segments = jnp.where(first, segment_ids[0, 0], segment_ids[1, 0])
    local_ids = lax.dynamic_slice_in_dim(segments, gx * TOK, TOK, 0)
    own_index = gx * TOK + jnp.arange(TOK, dtype=jnp.int32)
    doc_start = jnp.sum((segments[None, :] < local_ids[:, None]).astype(jnp.int32), axis=1)
    key_index = (gx - 3) * TOK + jnp.arange(LEN, dtype=jnp.int32)
    key_ids = lax.dynamic_slice_in_dim(jnp.pad(segments, (3 * TOK, 0), constant_values=-1), gx * TOK, LEN, 0)
    mask = ((local_ids[:, None] == key_ids[None, :]) & (key_index[None, :] <= own_index[:, None])).astype(f32)
    cosw, sinw = rope_tables(own_index - doc_start)
    pab, pba, pnb = place_matrices()

    def ahead(v, k):
        return lax.ppermute(v, "gx", [(i, i + k) for i in range(4 - k)])

    def back(v, k):
        return lax.ppermute(v, "gx", [(i + k, i) for i in range(4 - k)])

    sels = [core[None].astype(jnp.int32), (1 - core)[None].astype(jnp.int32)]
    kept = []
    x, parts = own_in, None
    for section in range(2):
        sel = sels[section]
        x, norm_b, qkv, kv, gains = project(sel, own, recv, pab, pba, cosw, sinw, x, parts)
        chunks = [ahead(kv, 1), ahead(kv, 2), ahead(kv, 3)]
        attb, mid, n2 = attend(sel, own, recv, qkv, chunks, mask, x, gains, pnb)
        n2_other = other_core(n2)
        yo, yr = ffn(section, n2, n2_other, packed)
        parts = (mid, yo, other_core(yr))
        kept.append((x, norm_b, qkv, gains, chunks, attb, mid, n2, n2_other))
    outs = [kept[1][0], (parts[0] + parts[1] + parts[2]).astype(bf16)]

    dy, dy_other = cot_own, cot_other
    grads_in, ffn_grads, attn_grads = [None, None], [None, None], [None, None]
    for section in (1, 0):
        sel = sels[section]
        x, norm_b, qkv, gains, chunks, attb, mid, n2, n2_other = kept[section]
        ffn_grads[section], no, nr = ffn_back(section, n2, n2_other, dy, dy_other, packed)
        dmid, dproj, gg, dq, dkv, d1, d2, d3 = attend_back(
            sel, own, recv, no, other_core(nr), mid, gains, dy, qkv, chunks, mask, pnb
        )
        dy, attn_grads[section] = project_back(
            sel, own, recv, dq, dkv, back(d1, 1), back(d2, 2), back(d3, 3),
            cosw, sinw, norm_b, x, gains, dmid, pba, attb, dproj, gg,
        )
        grads_in[section] = dy
        if section == 1:
            dy_other = other_core(dy)

    late = lax.psum_scatter(ffn_grads[1], "gx", scatter_dimension=0, tiled=True)
    late = lax.psum_scatter(late[0], "gy", scatter_dimension=0, tiled=True)[0]

    def half_sum(v):
        send = lax.dynamic_slice_in_dim(v, (1 - core) * 96, 96, 1)
        mine = lax.dynamic_slice_in_dim(v, core * 96, 96, 1)
        return (mine.astype(f32) + other_core(send).astype(f32)).astype(bf16)

    halved = [half_sum(attn_grads[0]), half_sum(attn_grads[1])]
    early = ffn_grads[0].reshape(64, 240, 256)
    chunks = [
        jnp.concatenate([early[:, :144]], 1),
        jnp.concatenate([early[:, 144:], halved[0][:, :48]], 1),
        jnp.concatenate([halved[0][:, 48:], halved[1]], 1),
    ]
    done = reduce_parts([c.reshape(4, 4, 4, 144, 256) for c in chunks], place)
    flat = jnp.concatenate(done, 0)
    half = [jnp.concatenate([flat[:240], flat[240:336]], 0), jnp.concatenate([late, flat[336:432]], 0)]
    mine = jnp.where(first, half[0], half[1])
    theirs = other_core(jnp.where(first, half[1], half[0]))
    low, high = jnp.where(first, mine, theirs), jnp.where(first, theirs, mine)
    ff = jnp.concatenate([low[:240].reshape(3, 80, 256), high[:240].reshape(3, 80, 256)], 1)[:, :, :240].astype(f32)
    at = jnp.concatenate([low[240:], high[240:]], 0).reshape(12, 16, 256)[:, :15].astype(f32)
    qkv_grad = at[:7].transpose(1, 0, 2).reshape(15, QKVW)
    out_grad = at[7:11].transpose(1, 0, 2)[:, :, :240].reshape(15, D)
    grad_qkv = jnp.concatenate([qkv_grad[:, 2 * KW : 1600], qkv_grad[:, : 2 * KW]], 1)

    def placed(pair):
        a = jnp.where(first, pair[0], pair[1])
        b = other_core(jnp.where(first, pair[1], pair[0]))
        both = jnp.stack([jnp.where(first, a, b), jnp.where(first, b, a)])
        return from_a(both)[None, :, None]

    return (
        placed(outs),
        placed(grads_in),
        qkv_grad[:, 1600][None],
        grad_qkv[None],
        out_grad[None],
        qkv_grad[:, 1601][None],
        ff[0].T[None],
        ff[1].T[None],
        ff[2][None],
    )


def solution(mesh):
    return jax.shard_map(
        per_device,
        mesh=mesh,
        in_specs=(
            P(None, "gy", "gx", None),
            P(None, "gy", "gx", None),
            P(None, "gy", None),
            P("section", ("gx", "gy")),
            P("section", ("gx", "gy"), None),
            P("section", ("gx", "gy"), None),
            P("section", ("gx", "gy")),
            P("section", "gx", "gy"),
            P("section", "gx", "gy"),
            P("section", "gy", "gx"),
        ),
        out_specs=(
            P("section", None, "gy", "gx", None),
            P("section", None, "gy", "gx", None),
            P("section", ("gx", "gy")),
            P("section", ("gx", "gy"), None),
            P("section", ("gx", "gy"), None),
            P("section", ("gx", "gy")),
            P("section", "gx", "gy"),
            P("section", "gx", "gy"),
            P("section", "gy", "gx"),
        ),
        check_vma=False,
    )
```

time: 1910 us -> 624 us (0.33)
  the two profiles are of different devices: /device:TPU:54 before, /device:TPU:1 now
where the time goes in v1:
time: 624 us; the launch traced here: 614 us
  waiting for transfers between devices  295 us (47%)
  Pallas kernels  116 us (19%)
  starting transfers between devices  105 us (17%)
  local copies, waits for them, and re-layouts  54.6 us (9%)
  other arithmetic  29.1 us (5%)
  between operations  15.2 us (2%)
    ppermute x27, waiting for transfers between devices, reduce_stage(): got.append(lax.ppermute(piece, axis, perm))  130 us
    all_gather x1, waiting for transfers between devices, per_device(): lax.all_gather(jnp.concatenate([halves, attn], 0)[None], ('gx', 'gy'), ax...  121 us
    pallas_call x12, Pallas kernels, call(): pl.pallas_call(kernel, out_shape=outs, in_specs=specs if specs is not Non...  116 us
    ppermute x27, starting transfers between devices, reduce_stage(): got.append(lax.ppermute(piece, axis, perm))  64.7 us
    ppermute x6, waiting for transfers between devices, back(): return lax.ppermute(v, 'gx', [(i + k, i) for i in range(4 - k)])  27.4 us
    ppermute x14, starting transfers between devices, other_core(): return lax.ppermute(v, 'section', [(0, 1), (1, 0)])  16.1 us
    ppermute x6, starting transfers between devices, ahead(): return lax.ppermute(v, 'gx', [(i, i + k) for i in range(4 - k)])  15.9 us
    unnamed x72, local copies, waits for them, and re-layouts  14.7 us
  transfers between devices with their start and end apart: 56, of which 28 were waited for; matrix products, arithmetic and copies ran while one was open for 10% of the time, Pallas kernels for 11%

profile of v1, /device:TPU:1, one launch (start us, length us, event | category | flops | bytes accessed | tf_op | source)
XLA Modules:
  0.0 614.4 jit_solution(12103088662899682744)
XLA Ops:
  15.0 121.4 %all-gather.3.cloned.1.call-done = bf16[41984,256]{1,0:T(8,128)(2,1)} async-done(((bf16[656,256]{1,0:T(8,128)(2,1)}), bf16[41984,256]{1,0:T(8,128)(2,1)}) %all-gather.3.cloned.1.call-update) | async-done | bytes 21495824 | tf_op jit(solution)/shard_map/all_gather | solution.py:472
  136.4 5.5 slice.152.own
  147.3 2.1 fusion.pnb
  149.5 2.4 compare_convert_fusion
  152.0 7.4 %project.2 = (bf16[128,1024]{1,0:T(8,128)(2,1)}, bf16[128,1792]{1,0:T(8,128)(2,1)}, bf16[128,640]{1,0:T(8,128)(2,1)}, f32[8,1024]{1,0:T(8,128)}) custom-call(s32[1]{0:T(128)} %bitcast.26.sel, bf16[64,176,256]{2,1,0:T(8,128)(2,1)} %slice.152.own, bf16[64,176,256]{2,1,0:T(8,128)(2,1)} %collective-permute-done.1.recv, ...), custom_call_target="tpu_custom_call" | custom-call | tf_op jit(solution)/shard_map/project/pallas_call | solution.py:40
  159.4 4.3 collective-permute-start.4
  165.0 2.5 collective-permute-start.2
  168.4 2.3 collective-permute-done.4.r3
  172.7 7.1 %attend.2 = (bf16[128,1024]{1,0:T(8,128)(2,1)}, f32[128,1024]{1,0:T(8,128)}, bf16[128,1024]{1,0:T(8,128)(2,1)}) custom-call(s32[1]{0:T(128)} %bitcast.26.sel, bf16[64,176,256]{2,1,0:T(8,128)(2,1)} %slice.152.own, bf16[64,176,256]{2,1,0:T(8,128)(2,1)} %collective-permute-done.1.recv, bf16[128,1792]{1,0:T(8,128)(2,1)} %get-tuple-element.54.qkv, ...), custom_call_target="tpu_custom_call" | custom-call | tf_op jit(solution)/shard_map/attend/pallas_call | solution.py:40
  183.2 7.5 %ffn.2 = (f32[128,1024]{1,0:T(8,128)}, f32[128,1024]{1,0:T(8,128)}) custom-call(bf16[128,1024]{1,0:T(8,128)(2,1)} %get-tuple-element.58.xo, bf16[128,1024]{1,0:T(8,128)(2,1)} %copy-done.7, bf16[4,16,656,256]{3,2,1,0:T(8,128)(2,1)} %bitcast.194, bf16[4,16,656,256]{3,2,1,0:T(8,128)(2,1)} %bitcast.195, bf16[4,16,656,256]{3,2,1,0:T(8,128)(2,1)} %bitcast.196), custom_call_target="tpu_custom_call" | custom-call | tf_op jit(solution)/shard_map/ffn/pallas_call | solution.py:40
  191.2 1.8 collective-permute-done.6.rest_2_
  193.8 7.8 %project.3 = (bf16[128,1024]{1,0:T(8,128)(2,1)}, bf16[128,1024]{1,0:T(8,128)(2,1)}, bf16[128,1792]{1,0:T(8,128)(2,1)}, bf16[128,640]{1,0:T(8,128)(2,1)}, f32[8,1024]{1,0:T(8,128)}) custom-call(s32[1]{0:T(128)} %bitcast.sel, bf16[64,176,256]{2,1,0:T(8,128)(2,1)} %slice.152.own, bf16[64,176,256]{2,1,0:T(8,128)(2,1)} %collective-permute-done.1.recv, ...), custom_call_target="tpu_custom_call" | custom-call | tf_op jit(solution)/shard_map/project/pallas_call | solution.py:40
  201.6 4.0 collective-permute-start.9
  205.6 2.2 collective-permute-start.8
  207.8 1.6 collective-permute-start.7
  209.4 3.1 collective-permute-done.9.r3
  212.5 2.4 collective-permute-done.7.r1
  215.5 7.1 %attend.3 = (bf16[128,1024]{1,0:T(8,128)(2,1)}, f32[128,1024]{1,0:T(8,128)}, bf16[128,1024]{1,0:T(8,128)(2,1)}) custom-call(s32[1]{0:T(128)} %bitcast.sel, bf16[64,176,256]{2,1,0:T(8,128)(2,1)} %slice.152.own, bf16[64,176,256]{2,1,0:T(8,128)(2,1)} %collective-permute-done.1.recv, bf16[128,1792]{1,0:T(8,128)(2,1)} %get-tuple-element.62.qkv, ...), custom_call_target="tpu_custom_call" | custom-call | tf_op jit(solution)/shard_map/attend/pallas_call | solution.py:40
  226.8 12.6 %ffn_back.2 = (bf16[4,16,240,256]{3,2,1,0:T(8,128)(2,1)}, f32[128,1024]{1,0:T(8,128)}, f32[128,1024]{1,0:T(8,128)}) custom-call(bf16[128,1024]{1,0:T(8,128)(2,1)} %get-tuple-element.66.xo, bf16[128,1024]{1,0:T(8,128)(2,1)} %copy-done.6, bf16[128,1024]{1,0:T(8,128)(2,1)} %bitcast.218, bf16[128,1024]{1,0:T(8,128)(2,1)} %bitcast.223, ...), custom_call_target="tpu_custom_call" | custom-call | tf_op jit(solution)/shard_map/ffn_back/pallas_call | solution.py:40
  240.9 1.9 collective-permute-done.13.nr
  243.6 11.3 %attend_back.2 = (f32[128,1024]{1,0:T(8,128)}, bf16[128,1024]{1,0:T(8,128)(2,1)}, f32[8,1024]{1,0:T(8,128)}, f32[128,1152]{1,0:T(8,128)}, f32[128,640]{1,0:T(8,1...) custom-call(s32[1]{0:T(128)} %bitcast.sel, bf16[64,176,256]{2,1,0:T(8,128)(2,1)} %slice.152.own, ...), custom_call_target="tpu_custom_call" | custom-call | tf_op jit(solution)/shard_map/attend_back/pallas_call | solution.py:40
  258.7 8.6 %collective-permute-done.14.e1 = bf16[128,640]{1,0:T(8,128)(2,1)S(1)} collective-permute-done((bf16[128,640]{1,0:T(8,128)(2,1)}, bf16[128,640]{1,0:T(8,128)(2,1)S(1)}, u32[]{:S(2)}, u32[]{:S(2)}) %collective-permute-start.14) | collective-permute-done | bytes 163872 | tf_op jit(solution)/shard_map/ppermute | solution.py:494
  267.3 2.9 collective-permute-done.15.e2
  270.2 5.1 collective-permute-done.16.e3
  275.9 12.0 %project_back.2 = (bf16[128,1024]{1,0:T(8,128)(2,1)}, bf16[64,192,256]{2,1,0:T(8,128)(2,1)}) custom-call(s32[1]{0:T(128)} %bitcast.sel, bf16[64,176,256]{2,1,0:T(8,128)(2,1)} %slice.152.own, bf16[64,176,256]{2,1,0:T(8,128)(2,1)} %collective-permute-done.1.recv, f32[128,1152]{1,0:T(8,128)} %get-tuple-element.71.dq, f32[128,640]{1,0:T(8,128)} %get-tuple-element.72.dkv, ...), custom_call_target="tpu_custom_call" | custom-call | tf_op jit(solution)/shard_map/project_back/pallas_call | solution.py:40
  290.8 12.8 %ffn_back.3 = (bf16[4,16,240,256]{3,2,1,0:T(8,128)(2,1)}, f32[128,1024]{1,0:T(8,128)}, f32[128,1024]{1,0:T(8,128)}) custom-call(bf16[128,1024]{1,0:T(8,128)(2,1)} %get-tuple-element.58.xo, bf16[128,1024]{1,0:T(8,128)(2,1)} %copy-done.7, bf16[128,1024]{1,0:T(8,128)(2,1)} %get-tuple-element.81.do.dy_ref, bf16[128,1024]{1,0:T(8,128)(2,1)} %copy-done.21, ...), custom_call_target="tpu_custom_call" | custom-call | tf_op jit(solution)/shard_map/ffn_back/pallas_call | solution.py:40
  304.0 3.8 constant_dynamic-slice_fusion
  308.7 11.3 %attend_back.3 = (f32[128,1024]{1,0:T(8,128)}, bf16[128,1024]{1,0:T(8,128)(2,1)}, f32[8,1024]{1,0:T(8,128)}, f32[128,1152]{1,0:T(8,128)}, f32[128,640]{1,0:T(8,1...) custom-call(s32[1]{0:T(128)} %bitcast.26.sel, ...), custom_call_target="tpu_custom_call" | custom-call | tf_op jit(solution)/shard_map/attend_back/pallas_call | solution.py:40
  322.6 1.5 collective-permute-start.21
  324.1 3.9 collective-permute-done.19.e1
  328.0 2.8 collective-permute-done.20.e2
  330.8 4.2 collective-permute-done.21.e3
  335.7 12.0 %project_back.3 = (bf16[128,1024]{1,0:T(8,128)(2,1)}, bf16[64,192,256]{2,1,0:T(8,128)(2,1)}) custom-call(s32[1]{0:T(128)} %bitcast.26.sel, bf16[64,176,256]{2,1,0:T(8,128)(2,1)} %slice.152.own, bf16[64,176,256]{2,1,0:T(8,128)(2,1)} %collective-permute-done.1.recv, f32[128,1152]{1,0:T(8,128)} %get-tuple-element.84.dq, f32[128,640]{1,0:T(8,128)} %get-tuple-element.85.dkv, ...), custom_call_target="tpu_custom_call" | custom-call | tf_op jit(solution)/shard_map/project_back/pallas_call | solution.py:40
  347.7 3.7 constant_dynamic-slice_fusion.5
  352.0 2.6 slice.153
  354.6 1.9 dynamic-slice_bitcast_fusion.5
  358.0 2.1 collective-permute-start.24
  360.1 7.5 %ffn.3 = (f32[128,1024]{1,0:T(8,128)}, f32[128,1024]{1,0:T(8,128)}) custom-call(bf16[128,1024]{1,0:T(8,128)(2,1)} %get-tuple-element.66.xo, bf16[128,1024]{1,0:T(8,128)(2,1)} %copy-done.6, bf16[4,16,656,256]{3,2,1,0:T(8,128)(2,1)} %bitcast.203, bf16[4,16,656,256]{3,2,1,0:T(8,128)(2,1)} %bitcast.204, bf16[4,16,656,256]{3,2,1,0:T(8,128)(2,1)} %bitcast.205), custom_call_target="tpu_custom_call" | custom-call | tf_op jit(solution)/shard_map/ffn/pallas_call | solution.py:40
  367.6 44.1 %collective-permute-done.23 = bf16[4,4,144,256]{3,2,1,0:T(8,128)(2,1)S(1)} collective-permute-done((bf16[4,4,144,256]{3,2,1,0:T(8,128)(2,1)}, bf16[4,4,144,256]{3,2,1,0:T(8,128)(2,1)S(1)}, u32[]{:S(2)}, u32[]{:S(2)}) %collective-permute-start.23) | collective-permute-done | bytes 1179680 | tf_op jit(solution)/shard_map/ppermute | solution.py:394
  413.6 2.7 fusion.9
  416.3 4.2 add_convert_fusion
  420.6 3.1 add_convert_fusion.1
  424.2 2.0 dynamic-slice_bitcast_fusion.2
  430.0 2.4 collective-permute-start.28
  436.2 2.1 slice.154
  439.2 7.5 %collective-permute-done.28 = bf16[4,144,256]{2,1,0:T(8,128)(2,1)} collective-permute-done((bf16[4,144,256]{2,1,0:T(8,128)(2,1)}, bf16[4,144,256]{2,1,0:T(8,128)(2,1)}, u32[]{:S(2)}, u32[]{:S(2)}) %collective-permute-start.28) | collective-permute-done | bytes 294944 | tf_op jit(solution)/shard_map/ppermute | solution.py:394
  449.1 2.8 collective-permute-start.45
  453.6 7.5 %collective-permute-done.29 = bf16[144,256]{1,0:T(8,128)(2,1)S(1)} collective-permute-done((bf16[144,256]{1,0:T(8,128)(2,1)S(1)}, bf16[144,256]{1,0:T(8,128)(2,1)S(1)}, u32[]{:S(2)}, u32[]{:S(2)}) %collective-permute-start.29) | collective-permute-done | bytes 73760 | tf_op jit(solution)/shard_map/ppermute | solution.py:394
  465.9 24.0 %collective-permute-done.31 = bf16[144,256]{1,0:T(8,128)(2,1)S(1)} collective-permute-done((bf16[144,256]{1,0:T(8,128)(2,1)S(1)}, bf16[144,256]{1,0:T(8,128)(2,1)S(1)}, u32[]{:S(2)}, u32[]{:S(2)}) %collective-permute-start.31) | collective-permute-done | bytes 73760 | tf_op jit(solution)/shard_map/ppermute | solution.py:394
  489.9 21.7 %collective-permute-done.30 = bf16[144,256]{1,0:T(8,128)(2,1)S(1)} collective-permute-done((bf16[144,256]{1,0:T(8,128)(2,1)S(1)}, bf16[144,256]{1,0:T(8,128)(2,1)S(1)}, u32[]{:S(2)}, u32[]{:S(2)}) %collective-permute-start.30) | collective-permute-done | bytes 73760 | tf_op jit(solution)/shard_map/ppermute | solution.py:394
  511.6 2.9 collective-permute-start.34
  517.1 2.1 collective-permute-start.22
  519.3 2.9 fusion.3
  522.4 1.7 collective-permute-start.48
  524.1 16.8 %collective-permute-done.34 = bf16[4,4,144,256]{3,2,0,1:T(8,128)(2,1)} collective-permute-done((bf16[4,4,144,256]{3,2,0,1:T(8,128)(2,1)}, bf16[4,4,144,256]{3,2,0,1:T(8,128)(2,1)}, u32[]{:S(2)}, u32[]{:S(2)}) %collective-permute-start.34) | collective-permute-done | bytes 1179680 | tf_op jit(solution)/shard_map/ppermute | solution.py:394
  542.3 4.0 collective-permute-done.35
  546.4 2.6 fusion.6
  549.0 20.4 %collective-permute-start.36 = (bf16[4,144,256]{2,1,0:T(8,128)(2,1)S(1)}, bf16[4,144,256]{2,1,0:T(8,128)(2,1)S(1)}, u32[]{:S(2)}, u32[]{:S(2)}) collective-permute-start(bf16[4,144,256]{2,1,0:T(8,128)(2,1)S(1)} %get-tuple-element.145), channel_id=1, source_target_pairs={{0,4},{1,5},{2,6},{3,7},{4,8},{5,9},{6,10},{7,11},{8,12},{9,13},{1... | collective-permute-start | bytes 884744 | tf_op jit(solution)/shard_map/ppermute | solution.py:394
  569.5 3.0 collective-permute-start.38
  572.4 2.0 collective-permute-start.37
  575.2 4.8 collective-permute-start.51
  580.9 9.4 %collective-permute-start.50 = (bf16[144,256]{1,0:T(8,128)(2,1)S(1)}, bf16[144,256]{1,0:T(8,128)(2,1)S(1)}, u32[]{:S(2)}, u32[]{:S(2)}) collective-permute-start(bf16[144,256]{1,0:T(8,128)(2,1)S(1)} %get-tuple-element.174), channel_id=1, source_target_pairs={{0,3},{1,0},{2,1},{3,2},{4,7},{5,4},{6,5},{7,6},{8,11},{9,8},{10,9... | collective-permute-start | bytes 221192 | tf_op jit(solution)/shard_map/ppermute | solution.py:394
  592.3 1.7 collective-permute-start.40
  597.7 4.4 collective-permute-start.52
  (248 shorter events, 79.5 us)
Async XLA Ops:
  7.2 129.2 %all-gather.3.cloned.1.call-start = ((), (), s32[]{:S(2)}) async-start(), calls=%async_computation.3 | async-start | bytes 21831680 | tf_op jit(solution)/shard_map/all_gather | solution.py:472
  8.3 5.8 collective-permute-start
  14.9 418.7 %reduce-scatter.5.cloned.1.call-start = ((), (), s32[]{:S(2)}) async-start(), calls=%async_computation.2 | async-start | bytes 9830400 | tf_op jit(solution)/shard_map/reduce_scatter | solution.py:527
  136.4 7.0 %copy-start.19 = (bf16[2,1,128,960]{2,3,1,0:T(8,128)(2,1)S(1)}, bf16[2,1,128,960]{2,3,1,0:T(8,128)(2,1)}, u32[]{:S(2)}) copy-start(bf16[2,1,128,960]{2,3,1,0:T(8,128)(2,1)} %param.10) | copy-start | bytes 1474564
  141.9 10.1 %collective-permute-start.1 = (bf16[64,176,256]{2,1,0:T(8,128)(2,1)}, bf16[64,176,256]{2,1,0:T(8,128)(2,1)}, u32[]{:S(2)}, u32[]{:S(2)}) collective-permute-start(bf16[64,176,256]{2,1,0:T(8,128)(2,1)} %slice.152.own), channel_id=1, source_target_pairs={{0,64},{64,0},{1,65},{65,1},{2,66},{66,2},{3,67},{67,3},{4,68},{68... | collective-permute-start | bytes 17301512 | tf_op jit(solution)/shard_map/ppermute | solution.py:378
  159.4 11.2 %collective-permute-start.4 = (bf16[128,640]{1,0:T(8,128)(2,1)}, bf16[128,640]{1,0:T(8,128)(2,1)S(1)}, u32[]{:S(2)}, u32[]{:S(2)}) collective-permute-start(bf16[128,640]{1,0:T(8,128)(2,1)} %get-tuple-element.55), channel_id=1, source_target_pairs={{0,48},{1,49},{2,50},{3,51},{4,52},{5,53},{6,54},{7,55},{8,56},{9,... | collective-permute-start | bytes 491528 | tf_op jit(solution)/shard_map/ppermute | solution.py:491
  163.7 6.9 %collective-permute-start.3 = (bf16[128,640]{1,0:T(8,128)(2,1)}, bf16[128,640]{1,0:T(8,128)(2,1)S(1)}, u32[]{:S(2)}, u32[]{:S(2)}) collective-permute-start(bf16[128,640]{1,0:T(8,128)(2,1)} %get-tuple-element.55), channel_id=1, source_target_pairs={{0,32},{16,48},{1,33},{17,49},{2,34},{18,50},{3,35},{19,51},{4,36}... | collective-permute-start | bytes 491528 | tf_op jit(solution)/shard_map/ppermute | solution.py:491
  165.0 7.0 %collective-permute-start.2 = (bf16[128,640]{1,0:T(8,128)(2,1)}, bf16[128,640]{1,0:T(8,128)(2,1)S(1)}, u32[]{:S(2)}, u32[]{:S(2)}) collective-permute-start(bf16[128,640]{1,0:T(8,128)(2,1)} %get-tuple-element.55), channel_id=1, source_target_pairs={{0,16},{16,32},{32,48},{1,17},{17,33},{33,49},{2,18},{18,34},{34,5... | collective-permute-start | bytes 491528 | tf_op jit(solution)/shard_map/ppermute | solution.py:491
  179.8 2.7 collective-permute-start.5
  190.7 2.3 collective-permute-start.6
  201.6 10.9 %collective-permute-start.9 = (bf16[128,640]{1,0:T(8,128)(2,1)}, bf16[128,640]{1,0:T(8,128)(2,1)S(1)}, u32[]{:S(2)}, u32[]{:S(2)}) collective-permute-start(bf16[128,640]{1,0:T(8,128)(2,1)} %get-tuple-element.63), channel_id=1, source_target_pairs={{0,48},{1,49},{2,50},{3,51},{4,52},{5,53},{6,54},{7,55},{8,56},{9,... | collective-permute-start | bytes 491528 | tf_op jit(solution)/shard_map/ppermute | solution.py:491
  205.6 6.9 %collective-permute-start.8 = (bf16[128,640]{1,0:T(8,128)(2,1)}, bf16[128,640]{1,0:T(8,128)(2,1)S(1)}, u32[]{:S(2)}, u32[]{:S(2)}) collective-permute-start(bf16[128,640]{1,0:T(8,128)(2,1)} %get-tuple-element.63), channel_id=1, source_target_pairs={{0,32},{16,48},{1,33},{17,49},{2,34},{18,50},{3,35},{19,51},{4,36}... | collective-permute-start | bytes 491528 | tf_op jit(solution)/shard_map/ppermute | solution.py:491
  207.8 7.1 %collective-permute-start.7 = (bf16[128,640]{1,0:T(8,128)(2,1)}, bf16[128,640]{1,0:T(8,128)(2,1)S(1)}, u32[]{:S(2)}, u32[]{:S(2)}) collective-permute-start(bf16[128,640]{1,0:T(8,128)(2,1)} %get-tuple-element.63), channel_id=1, source_target_pairs={{0,16},{16,32},{32,48},{1,17},{17,33},{33,49},{2,18},{18,34},{34,5... | collective-permute-start | bytes 491528 | tf_op jit(solution)/shard_map/ppermute | solution.py:491
  215.5 8.4 %copy-start.20 = (bf16[2,1,128,960]{2,3,1,0:T(8,128)(2,1)S(1)}, bf16[2,1,128,960]{2,3,1,0:T(8,128)(2,1)}, u32[]{:S(2)}) copy-start(bf16[2,1,128,960]{2,3,1,0:T(8,128)(2,1)} %param.11) | copy-start | bytes 1474564
  222.6 3.5 collective-permute-start.10
  239.5 357.2 %reduce-scatter.7.cloned.1.call-start = ((), (), s32[]{:S(2)}) async-start(), calls=%async_computation.4 | async-start | bytes 2088960
  240.5 2.3 collective-permute-start.13
  254.8 12.5 %collective-permute-start.14 = (bf16[128,640]{1,0:T(8,128)(2,1)}, bf16[128,640]{1,0:T(8,128)(2,1)S(1)}, u32[]{:S(2)}, u32[]{:S(2)}) collective-permute-start(bf16[128,640]{1,0:T(8,128)(2,1)} %get-tuple-element.73), channel_id=1, source_target_pairs={{16,0},{32,16},{48,32},{17,1},{33,17},{49,33},{18,2},{34,18},{50,3... | collective-permute-start | bytes 491528 | tf_op jit(solution)/shard_map/ppermute | solution.py:494
  256.1 14.0 %collective-permute-start.15 = (bf16[128,640]{1,0:T(8,128)(2,1)}, bf16[128,640]{1,0:T(8,128)(2,1)S(1)}, u32[]{:S(2)}, u32[]{:S(2)}) collective-permute-start(bf16[128,640]{1,0:T(8,128)(2,1)} %get-tuple-element.74), channel_id=1, source_target_pairs={{32,0},{48,16},{33,1},{49,17},{34,2},{50,18},{35,3},{51,19},{36,4}... | collective-permute-start | bytes 491528 | tf_op jit(solution)/shard_map/ppermute | solution.py:494
  257.4 17.8 %collective-permute-start.16 = (bf16[128,640]{1,0:T(8,128)(2,1)}, bf16[128,640]{1,0:T(8,128)(2,1)S(1)}, u32[]{:S(2)}, u32[]{:S(2)}) collective-permute-start(bf16[128,640]{1,0:T(8,128)(2,1)} %get-tuple-element.75), channel_id=1, source_target_pairs={{48,0},{49,1},{50,2},{51,3},{52,4},{53,5},{54,6},{55,7},{56,8},{57... | collective-permute-start | bytes 491528 | tf_op jit(solution)/shard_map/ppermute | solution.py:494
  267.3 7.9 %copy-start.24 = (bf16[128,640]{1,0:T(8,128)(2,1)}, bf16[128,640]{1,0:T(8,128)(2,1)S(1)}, u32[]{:S(2)}) copy-start(bf16[128,640]{1,0:T(8,128)(2,1)S(1)} %collective-permute-done.14.e1) | copy-start | bytes 491524
  287.9 2.2 collective-permute-start.17
  303.6 4.3 collective-permute-start.18
  307.7 108.6 %collective-permute-start.42 = (bf16[64,96,256]{2,1,0:T(8,128)(2,1)}, bf16[64,96,256]{2,1,0:T(8,128)(2,1)}, u32[]{:S(2)}, u32[]{:S(2)}) collective-permute-start(bf16[64,96,256]{2,1,0:T(8,128)(2,1)} %constant_dynamic-slice_fusion), channel_id=1, source_target_pairs={{0,64},{64,0},{1,65},{65,1},{2,66},{66,2},{3,67},{67,3},{4,68},{68... | collective-permute-start | bytes 9437192 | tf_op jit(solution)/shard_map/ppermute | solution.py:378
  320.0 8.0 %collective-permute-start.19 = (bf16[128,640]{1,0:T(8,128)(2,1)}, bf16[128,640]{1,0:T(8,128)(2,1)S(1)}, u32[]{:S(2)}, u32[]{:S(2)}) collective-permute-start(bf16[128,640]{1,0:T(8,128)(2,1)} %get-tuple-element.86), channel_id=1, source_target_pairs={{16,0},{32,16},{48,32},{17,1},{33,17},{49,33},{18,2},{34,18},{50,3... | collective-permute-start | bytes 491528 | tf_op jit(solution)/shard_map/ppermute | solution.py:494
  321.3 9.5 %collective-permute-start.20 = (bf16[128,640]{1,0:T(8,128)(2,1)}, bf16[128,640]{1,0:T(8,128)(2,1)S(1)}, u32[]{:S(2)}, u32[]{:S(2)}) collective-permute-start(bf16[128,640]{1,0:T(8,128)(2,1)} %get-tuple-element.87), channel_id=1, source_target_pairs={{32,0},{48,16},{33,1},{49,17},{34,2},{50,18},{35,3},{51,19},{36,4}... | collective-permute-start | bytes 491528 | tf_op jit(solution)/shard_map/ppermute | solution.py:494
  322.6 12.4 %collective-permute-start.21 = (bf16[128,640]{1,0:T(8,128)(2,1)}, bf16[128,640]{1,0:T(8,128)(2,1)S(1)}, u32[]{:S(2)}, u32[]{:S(2)}) collective-permute-start(bf16[128,640]{1,0:T(8,128)(2,1)} %get-tuple-element.88), channel_id=1, source_target_pairs={{48,0},{49,1},{50,2},{51,3},{52,4},{53,5},{54,6},{55,7},{56,8},{57... | collective-permute-start | bytes 491528 | tf_op jit(solution)/shard_map/ppermute | solution.py:494
  328.0 7.0 %copy-start.22 = (bf16[128,640]{1,0:T(8,128)(2,1)}, bf16[128,640]{1,0:T(8,128)(2,1)S(1)}, u32[]{:S(2)}) copy-start(bf16[128,640]{1,0:T(8,128)(2,1)S(1)} %collective-permute-done.19.e1) | copy-start | bytes 491524
  351.5 69.0 %collective-permute-start.32 = (bf16[64,96,256]{2,1,0:T(8,128)(2,1)}, bf16[64,96,256]{2,1,0:T(8,128)(2,1)}, u32[]{:S(2)}, u32[]{:S(2)}) collective-permute-start(bf16[64,96,256]{2,1,0:T(8,128)(2,1)} %constant_dynamic-slice_fusion.5), channel_id=1, source_target_pairs={{0,64},{64,0},{1,65},{65,1},{2,66},{66,2},{3,67},{67,3},{4,68},{68... | collective-permute-start | bytes 9437192 | tf_op jit(solution)/shard_map/ppermute | solution.py:378
  357.5 54.3 %collective-permute-start.23 = (bf16[4,4,144,256]{3,2,1,0:T(8,128)(2,1)}, bf16[4,4,144,256]{3,2,1,0:T(8,128)(2,1)S(1)}, u32[]{:S(2)}, u32[]{:S(2)}) collective-permute-start(bf16[4,4,144,256]{3,2,1,0:T(8,128)(2,1)} %get-tuple-element.130), channel_id=1, source_target_pairs={{0,16},{16,32},{32,48},{48,0},{1,17},{17,33},{33,49},{49,1},{2,18}... | collective-permute-start | bytes 3538952 | tf_op jit(solution)/shard_map/ppermute | solution.py:394
  357.5 55.1 %collective-permute-start.25 = (bf16[4,4,144,256]{3,2,1,0:T(8,128)(2,1)}, bf16[4,4,144,256]{3,2,1,0:T(8,128)(2,1)S(1)}, u32[]{:S(2)}, u32[]{:S(2)}) collective-permute-start(bf16[4,4,144,256]{3,2,1,0:T(8,128)(2,1)} %get-tuple-element.131), channel_id=1, source_target_pairs={{0,32},{16,48},{32,0},{48,16},{1,33},{17,49},{33,1},{49,17},{2,34}... | collective-permute-start | bytes 3538952 | tf_op jit(solution)/shard_map/ppermute | solution.py:394
  358.0 55.6 %collective-permute-start.24 = (bf16[4,4,144,256]{3,2,1,0:T(8,128)(2,1)S(1)}, bf16[4,4,144,256]{3,2,1,0:T(8,128)(2,1)}, u32[]{:S(2)}, u32[]{:S(2)}) collective-permute-start(bf16[4,4,144,256]{3,2,1,0:T(8,128)(2,1)S(1)} %get-tuple-element.132), channel_id=1, source_target_pairs={{0,48},{16,0},{32,16},{48,32},{1,49},{17,1},{33,17},{49,33},{2,50}... | collective-permute-start | bytes 3538952 | tf_op jit(solution)/shard_map/ppermute | solution.py:394
  411.7 21.9 %collective-permute-start.11 = (f32[128,1024]{1,0:T(8,128)}, f32[128,1024]{1,0:T(8,128)}, u32[]{:S(2)}, u32[]{:S(2)}) collective-permute-start(f32[128,1024]{1,0:T(8,128)} %get-tuple-element.68), channel_id=1, source_target_pairs={{0,64},{64,0},{1,65},{65,1},{2,66},{66,2},{3,67},{67,3},{4,68},{68... | collective-permute-start | bytes 1572872 | tf_op jit(solution)/shard_map/ppermute | solution.py:378
  413.6 7.0 %slice-start = ((s8[6291456]{0:T(1024)(128)(4,1)}), s8[4194304]{0:T(1024)(128)(4,1)S(1)}, s32[]{:S(2)}) async-start(s8[6291456]{0:T(1024)(128)(4,1)} %bitcast.213), calls=%async_computation.5 | async-start | bytes 8388608
  427.7 86.7 %collective-permute-start.43 = (bf16[4,4,144,256]{3,2,1,0:T(8,128)(2,1)}, bf16[4,4,144,256]{3,2,1,0:T(8,128)(2,1)}, u32[]{:S(2)}, u32[]{:S(2)}) collective-permute-start(bf16[4,4,144,256]{3,2,1,0:T(8,128)(2,1)} %get-tuple-element.137), channel_id=1, source_target_pairs={{0,4},{1,5},{2,6},{3,7},{4,8},{5,9},{6,10},{7,11},{8,12},{9,13},{1... | collective-permute-start | bytes 3538952 | tf_op jit(solution)/shard_map/ppermute | solution.py:394
  429.1 10.1 %collective-permute-start.26 = (bf16[4,144,256]{2,1,0:T(8,128)(2,1)}, bf16[4,144,256]{2,1,0:T(8,128)(2,1)}, u32[]{:S(2)}, u32[]{:S(2)}) collective-permute-start(bf16[4,144,256]{2,1,0:T(8,128)(2,1)} %get-tuple-element.142), channel_id=1, source_target_pairs={{0,1},{1,2},{2,3},{3,0},{4,5},{5,6},{6,7},{7,4},{8,9},{9,10},{10,1... | collective-permute-start | bytes 884744 | tf_op jit(solution)/shard_map/ppermute | solution.py:394
  430.0 16.7 %collective-permute-start.28 = (bf16[4,144,256]{2,1,0:T(8,128)(2,1)}, bf16[4,144,256]{2,1,0:T(8,128)(2,1)}, u32[]{:S(2)}, u32[]{:S(2)}) collective-permute-start(bf16[4,144,256]{2,1,0:T(8,128)(2,1)} %get-tuple-element.143), channel_id=1, source_target_pairs={{0,2},{1,3},{2,0},{3,1},{4,6},{5,7},{6,4},{7,5},{8,10},{9,11},{10,... | collective-permute-start | bytes 884744 | tf_op jit(solution)/shard_map/ppermute | solution.py:394
  432.5 14.3 %collective-permute-start.27 = (bf16[4,144,256]{2,1,0:T(8,128)(2,1)}, bf16[4,144,256]{2,1,0:T(8,128)(2,1)}, u32[]{:S(2)}, u32[]{:S(2)}) collective-permute-start(bf16[4,144,256]{2,1,0:T(8,128)(2,1)} %get-tuple-element.144), channel_id=1, source_target_pairs={{0,3},{1,0},{2,1},{3,2},{4,7},{5,4},{6,5},{7,6},{8,11},{9,8},{10,9... | collective-permute-start | bytes 884744 | tf_op jit(solution)/shard_map/ppermute | solution.py:394
  435.1 17.8 %collective-permute-start.12 = (bf16[128,1024]{1,0:T(8,128)(2,1)S(1)}, bf16[128,1024]{1,0:T(8,128)(2,1)S(1)}, u32[]{:S(2)}, u32[]{:S(2)}) collective-permute-start(bf16[128,1024]{1,0:T(8,128)(2,1)S(1)} %get-tuple-element.128), channel_id=1, source_target_pairs={{0,64},{64,0},{1,65},{65,1},{2,66},{66,2},{3,67},{67,3},{4,68},{68... | collective-permute-start | bytes 786440 | tf_op jit(solution)/shard_map/ppermute | solution.py:378
  448.1 13.0 %collective-permute-start.29 = (bf16[144,256]{1,0:T(8,128)(2,1)S(1)}, bf16[144,256]{1,0:T(8,128)(2,1)S(1)}, u32[]{:S(2)}, u32[]{:S(2)}) collective-permute-start(bf16[144,256]{1,0:T(8,128)(2,1)S(1)} %get-tuple-element.166), channel_id=1, source_target_pairs={{0,4},{1,5},{2,6},{3,7},{4,8},{5,9},{6,10},{7,11},{8,12},{9,13},{1... | collective-permute-start | bytes 221192 | tf_op jit(solution)/shard_map/ppermute | solution.py:394
  449.1 68.0 %collective-permute-start.45 = (bf16[4,4,144,256]{3,2,1,0:T(8,128)(2,1)}, bf16[4,4,144,256]{3,2,1,0:T(8,128)(2,1)}, u32[]{:S(2)}, u32[]{:S(2)}) collective-permute-start(bf16[4,4,144,256]{3,2,1,0:T(8,128)(2,1)} %get-tuple-element.138), channel_id=1, source_target_pairs={{0,8},{1,9},{2,10},{3,11},{4,12},{5,13},{6,14},{7,15},{8,0},{9,1},... | collective-permute-start | bytes 3538952 | tf_op jit(solution)/shard_map/ppermute | solution.py:394
  451.9 67.4 %collective-permute-start.44 = (bf16[4,4,144,256]{3,2,1,0:T(8,128)(2,1)}, bf16[4,4,144,256]{3,2,1,0:T(8,128)(2,1)}, u32[]{:S(2)}, u32[]{:S(2)}) collective-permute-start(bf16[4,4,144,256]{3,2,1,0:T(8,128)(2,1)} %get-tuple-element.139), channel_id=1, source_target_pairs={{0,12},{1,13},{2,14},{3,15},{4,0},{5,1},{6,2},{7,3},{8,4},{9,5},{1... | collective-permute-start | bytes 3538952 | tf_op jit(solution)/shard_map/ppermute | solution.py:394
  452.9 37.0 %collective-permute-start.31 = (bf16[144,256]{1,0:T(8,128)(2,1)S(1)}, bf16[144,256]{1,0:T(8,128)(2,1)S(1)}, u32[]{:S(2)}, u32[]{:S(2)}) collective-permute-start(bf16[144,256]{1,0:T(8,128)(2,1)S(1)} %get-tuple-element.167), channel_id=1, source_target_pairs={{0,8},{1,9},{2,10},{3,11},{4,12},{5,13},{6,14},{7,15},{8,0},{9,1},... | collective-permute-start | bytes 221192 | tf_op jit(solution)/shard_map/ppermute | solution.py:394
  461.1 50.5 %collective-permute-start.30 = (bf16[144,256]{1,0:T(8,128)(2,1)S(1)}, bf16[144,256]{1,0:T(8,128)(2,1)S(1)}, u32[]{:S(2)}, u32[]{:S(2)}) collective-permute-start(bf16[144,256]{1,0:T(8,128)(2,1)S(1)} %get-tuple-element.168), channel_id=1, source_target_pairs={{0,12},{1,13},{2,14},{3,15},{4,0},{5,1},{6,2},{7,3},{8,4},{9,5},{1... | collective-permute-start | bytes 221192 | tf_op jit(solution)/shard_map/ppermute | solution.py:394
  465.9 51.1 %copy-start.3 = (bf16[128,1024]{1,0:T(8,128)(2,1)S(1)}, bf16[128,1024]{1,0:T(8,128)(2,1)}, u32[]{:S(2)}) copy-start(bf16[128,1024]{1,0:T(8,128)(2,1)} %get-tuple-element.81.do.dy_ref) | copy-start | bytes 786436
  465.9 51.1 %copy-start.8 = (bf16[128,1024]{1,0:T(8,128)(2,1)S(1)}, bf16[128,1024]{1,0:T(8,128)(2,1)}, u32[]{:S(2)}) copy-start(bf16[128,1024]{1,0:T(8,128)(2,1)} %get-tuple-element.94) | copy-start | bytes 786436
  489.9 32.5 %collective-permute-start.33 = (bf16[4,4,144,256]{3,2,0,1:T(8,128)(2,1)}, bf16[4,4,144,256]{3,2,0,1:T(8,128)(2,1)}, u32[]{:S(2)}, u32[]{:S(2)}) collective-permute-start(bf16[4,4,144,256]{3,2,0,1:T(8,128)(2,1)} %bitcast.190), channel_id=1, source_target_pairs={{0,1},{1,2},{2,3},{3,0},{4,5},{5,6},{6,7},{7,4},{8,9},{9,10},{10,1... | collective-permute-start | bytes 3538952 | tf_op jit(solution)/shard_map/ppermute | solution.py:394
  511.6 29.4 %collective-permute-start.34 = (bf16[4,4,144,256]{3,2,0,1:T(8,128)(2,1)}, bf16[4,4,144,256]{3,2,0,1:T(8,128)(2,1)}, u32[]{:S(2)}, u32[]{:S(2)}) collective-permute-start(bf16[4,4,144,256]{3,2,0,1:T(8,128)(2,1)} %bitcast.189), channel_id=1, source_target_pairs={{0,3},{1,0},{2,1},{3,2},{4,7},{5,4},{6,5},{7,6},{8,11},{9,8},{10,9... | collective-permute-start | bytes 3538952 | tf_op jit(solution)/shard_map/ppermute | solution.py:394
  514.4 31.9 %collective-permute-start.35 = (bf16[4,4,144,256]{3,2,0,1:T(8,128)(2,1)}, bf16[4,4,144,256]{3,2,0,1:T(8,128)(2,1)}, u32[]{:S(2)}, u32[]{:S(2)}) collective-permute-start(bf16[4,4,144,256]{3,2,0,1:T(8,128)(2,1)} %bitcast.188), channel_id=1, source_target_pairs={{0,2},{1,3},{2,0},{3,1},{4,6},{5,7},{6,4},{7,5},{8,10},{9,11},{10,... | collective-permute-start | bytes 3538952 | tf_op jit(solution)/shard_map/ppermute | solution.py:394
  517.1 85.0 %collective-permute-start.22 = (bf16[128,1024]{1,0:T(8,128)(2,1)S(1)}, bf16[128,1024]{1,0:T(8,128)(2,1)S(1)}, u32[]{:S(2)}, u32[]{:S(2)}) collective-permute-start(bf16[128,1024]{1,0:T(8,128)(2,1)S(1)} %broadcast_select_fusion.4), channel_id=1, source_target_pairs={{0,64},{64,0},{1,65},{65,1},{2,66},{66,2},{3,67},{67,3},{4,68},{68... | collective-permute-start | bytes 786440 | tf_op jit(solution)/shard_map/ppermute | solution.py:378
  522.3 47.2 %collective-permute-start.46 = (bf16[4,144,256]{2,1,0:T(8,128)(2,1)S(1)}, bf16[4,144,256]{2,1,0:T(8,128)(2,1)S(1)}, u32[]{:S(2)}, u32[]{:S(2)}) collective-permute-start(bf16[4,144,256]{2,1,0:T(8,128)(2,1)S(1)} %get-tuple-element.148), channel_id=1, source_target_pairs={{0,16},{16,32},{32,48},{48,0},{1,17},{17,33},{33,49},{49,1},{2,18}... | collective-permute-start | bytes 884744 | tf_op jit(solution)/shard_map/ppermute | solution.py:394
  522.4 50.1 %collective-permute-start.48 = (bf16[4,144,256]{2,1,0:T(8,128)(2,1)S(1)}, bf16[4,144,256]{2,1,0:T(8,128)(2,1)S(1)}, u32[]{:S(2)}, u32[]{:S(2)}) collective-permute-start(bf16[4,144,256]{2,1,0:T(8,128)(2,1)S(1)} %get-tuple-element.149), channel_id=1, source_target_pairs={{0,32},{16,48},{32,0},{48,16},{1,33},{17,49},{33,1},{49,17},{2,34}... | collective-permute-start | bytes 884744 | tf_op jit(solution)/shard_map/ppermute | solution.py:394
  540.9 33.5 %collective-permute-start.47 = (bf16[4,144,256]{2,1,0:T(8,128)(2,1)S(1)}, bf16[4,144,256]{2,1,0:T(8,128)(2,1)S(1)}, u32[]{:S(2)}, u32[]{:S(2)}) collective-permute-start(bf16[4,144,256]{2,1,0:T(8,128)(2,1)S(1)} %get-tuple-element.150), channel_id=1, source_target_pairs={{0,48},{16,0},{32,16},{48,32},{1,49},{17,1},{33,17},{49,33},{2,50}... | collective-permute-start | bytes 884744 | tf_op jit(solution)/shard_map/ppermute | solution.py:394
  549.0 26.2 %collective-permute-start.36 = (bf16[4,144,256]{2,1,0:T(8,128)(2,1)S(1)}, bf16[4,144,256]{2,1,0:T(8,128)(2,1)S(1)}, u32[]{:S(2)}, u32[]{:S(2)}) collective-permute-start(bf16[4,144,256]{2,1,0:T(8,128)(2,1)S(1)} %get-tuple-element.145), channel_id=1, source_target_pairs={{0,4},{1,5},{2,6},{3,7},{4,8},{5,9},{6,10},{7,11},{8,12},{9,13},{1... | collective-permute-start | bytes 884744 | tf_op jit(solution)/shard_map/ppermute | solution.py:394
  569.5 11.4 %collective-permute-start.38 = (bf16[4,144,256]{2,1,0:T(8,128)(2,1)S(1)}, bf16[4,144,256]{2,1,0:T(8,128)(2,1)S(1)}, u32[]{:S(2)}, u32[]{:S(2)}) collective-permute-start(bf16[4,144,256]{2,1,0:T(8,128)(2,1)S(1)} %get-tuple-element.146), channel_id=1, source_target_pairs={{0,8},{1,9},{2,10},{3,11},{4,12},{5,13},{6,14},{7,15},{8,0},{9,1},... | collective-permute-start | bytes 884744 | tf_op jit(solution)/shard_map/ppermute | solution.py:394
  572.4 17.8 %collective-permute-start.37 = (bf16[4,144,256]{2,1,0:T(8,128)(2,1)S(1)}, bf16[4,144,256]{2,1,0:T(8,128)(2,1)S(1)}, u32[]{:S(2)}, u32[]{:S(2)}) collective-permute-start(bf16[4,144,256]{2,1,0:T(8,128)(2,1)S(1)} %get-tuple-element.147), channel_id=1, source_target_pairs={{0,12},{1,13},{2,14},{3,15},{4,0},{5,1},{6,2},{7,3},{8,4},{9,5},{1... | collective-permute-start | bytes 884744 | tf_op jit(solution)/shard_map/ppermute | solution.py:394
  574.6 16.9 %collective-permute-start.49 = (bf16[144,256]{1,0:T(8,128)(2,1)S(1)}, bf16[144,256]{1,0:T(8,128)(2,1)S(1)}, u32[]{:S(2)}, u32[]{:S(2)}) collective-permute-start(bf16[144,256]{1,0:T(8,128)(2,1)S(1)} %get-tuple-element.172), channel_id=1, source_target_pairs={{0,1},{1,2},{2,3},{3,0},{4,5},{5,6},{6,7},{7,4},{8,9},{9,10},{10,1... | collective-permute-start | bytes 221192 | tf_op jit(solution)/shard_map/ppermute | solution.py:394
  575.2 17.0 %collective-permute-start.51 = (bf16[144,256]{1,0:T(8,128)(2,1)S(1)}, bf16[144,256]{1,0:T(8,128)(2,1)S(1)}, u32[]{:S(2)}, u32[]{:S(2)}) collective-permute-start(bf16[144,256]{1,0:T(8,128)(2,1)S(1)} %get-tuple-element.173), channel_id=1, source_target_pairs={{0,2},{1,3},{2,0},{3,1},{4,6},{5,7},{6,4},{7,5},{8,10},{9,11},{10,... | collective-permute-start | bytes 221192 | tf_op jit(solution)/shard_map/ppermute | solution.py:394
  580.9 13.1 %collective-permute-start.50 = (bf16[144,256]{1,0:T(8,128)(2,1)S(1)}, bf16[144,256]{1,0:T(8,128)(2,1)S(1)}, u32[]{:S(2)}, u32[]{:S(2)}) collective-permute-start(bf16[144,256]{1,0:T(8,128)(2,1)S(1)} %get-tuple-element.174), channel_id=1, source_target_pairs={{0,3},{1,0},{2,1},{3,2},{4,7},{5,4},{6,5},{7,6},{8,11},{9,8},{10,9... | collective-permute-start | bytes 221192 | tf_op jit(solution)/shard_map/ppermute | solution.py:394
  590.4 4.8 collective-permute-start.39
  591.5 4.7 collective-permute-start.41
  592.3 4.3 collective-permute-start.40
  596.7 7.2 %copy-start.18 = (bf16[1,240,256]{2,1,0:T(8,128)(2,1)S(1)}, bf16[1,240,256]{2,1,0:T(8,128)(2,1)}, u32[]{:S(2)}) copy-start(bf16[1,240,256]{2,1,0:T(8,128)(2,1)} %reduce-scatter.7.cloned.1.call-done) | copy-start | bytes 368644
  597.7 6.2 %collective-permute-start.52 = (bf16[336,256]{1,0:T(8,128)(2,1)S(1)}, bf16[336,256]{1,0:T(8,128)(2,1)S(1)}, u32[]{:S(2)}, u32[]{:S(2)}) collective-permute-start(bf16[336,256]{1,0:T(8,128)(2,1)S(1)} %broadcast_select_fusion.12), channel_id=1, source_target_pairs={{0,64},{64,0},{1,65},{65,1},{2,66},{66,2},{3,67},{67,3},{4,68},{68... | collective-permute-start | bytes 516104 | tf_op jit(solution)/shard_map/ppermute | solution.py:378
  (24 other events, 55.0 us)
Sparse Core Ops, SparseCore 0:
  15.0 121.2 all-gather.2
  239.6 83.7 reduce-scatter.4
  433.8 117.4 reduce-scatter.6

commit v2 on v1

--- a/solution.py
+++ b/solution.py
@@ -53,18 +53,29 @@
     return jax.ShapeDtypeStruct(shape, dt)
 
 
-def pick(sel_ref, own, recv, first, rows, buf, sem):
+def pick(sel_ref, own, recv, buf, sems):
+    def start(sources):
+        row = 0
+        for i, source in enumerate(sources):
+            rows = source.shape[1]
+            pltpu.make_async_copy(source, buf.at[:, pl.ds(row, rows), :], sems.at[i]).start()
+            row += rows
+
     @pl.when(sel_ref[0] == 0)
     def _():
-        pltpu.make_async_copy(own.at[:, pl.ds(first, rows), :], buf, sem).start()
+        start(own)
 
     @pl.when(sel_ref[0] != 0)
     def _():
-        pltpu.make_async_copy(recv.at[:, pl.ds(first, rows), :], buf, sem).start()
-
-
-def arrived(own, first, rows, buf, sem):
-    pltpu.make_async_copy(own.at[:, pl.ds(first, rows), :], buf, sem).wait()
+        start(recv)
+
+
+def arrived(own, buf, sems):
+    row = 0
+    for i, source in enumerate(own):
+        rows = source.shape[1]
+        pltpu.make_async_copy(source, buf.at[:, pl.ds(row, rows), :], sems.at[i]).wait()
+        row += rows
 
 
 def chunk_of(buf, j):
@@ -79,12 +90,12 @@
     return lax.broadcasted_iota(jnp.int32, shape, 1) % HD
 
 
-def project_kernel(has_x, sel, own, recv, pab, pba, cosw, sinw, *rest):
+def project_kernel(has_x, sel, own_a, own_b, recv_a, recv_b, pab, pba, cosw, sinw, *rest):
     if has_x:
-        x_ref, norm_ref, qkv_ref, kv_ref, gain_ref, buf, sem = rest
+        x_ref, norm_ref, qkv_ref, kv_ref, gain_ref, buf, sems = rest
     else:
-        mid_ref, yo_ref, yr_ref, x_out, norm_ref, qkv_ref, kv_ref, gain_ref, buf, sem = rest
-    pick(sel, own, recv, 0, 112, buf, sem)
+        mid_ref, yo_ref, yr_ref, x_out, norm_ref, qkv_ref, kv_ref, gain_ref, buf, sems = rest
+    pick(sel, (own_a, own_b), (recv_a, recv_b), buf, sems)
     if has_x:
         x = x_ref[...].astype(f32)
     else:
@@ -92,7 +103,7 @@
         x_out[...] = xb
         x = xb.astype(f32)
     rstd = rstd_of(x)
-    arrived(own, 0, 112, buf, sem)
+    arrived((own_a, own_b), buf, sems)
     gains = nn(chunk_of(buf, 6).astype(f32).T.astype(bf16), pba[...])[64:72, :]
     gain_ref[...] = gains
     normed = (x * rstd * gains[0:1, :]).astype(bf16)
@@ -118,8 +129,8 @@
     return terms / jnp.sum(terms, axis=1, keepdims=True)
 
 
-def attend_kernel(sel, own, recv, qkv, r1, r2, r3, mask, x_ref, gain_ref, pnb, attb_ref, mid_ref, n2_ref, buf, kvs, att, sem):
-    pick(sel, own, recv, 112, 64, buf, sem)
+def attend_kernel(sel, own, recv, qkv, r1, r2, r3, mask, x_ref, gain_ref, pnb, attb_ref, mid_ref, n2_ref, buf, kvs, att, sems):
+    pick(sel, (own,), (recv,), buf, sems)
     for k, part in enumerate((r3, r2, r1)):
         kvs[TOK * k : TOK * k + TOK, :] = part[...]
     kvs[3 * TOK :, :] = qkv[:, : 2 * KW]
@@ -135,7 +146,7 @@
             att[:, lane : lane + HD] = o3[TOK * h : TOK * h + TOK, :]
     attb = nn(att[...], pnb[...]).astype(bf16)
     attb_ref[...] = attb
-    arrived(own, 112, 64, buf, sem)
+    arrived((own,), buf, sems)
     out = jnp.concatenate([nn(attb, chunk_of(buf, j)) for j in range(4)], axis=1)
     mid = x_ref[...].astype(f32) + out
     mid_ref[...] = mid
@@ -191,9 +202,9 @@
     du_t = d_up.T
     for g in range(4):
         xg = xs[:, 256 * g : 256 * g + 256]
-        grads[g, :, 0:80, :] = nn(dg_t, xg).astype(bf16).reshape(4, 80, 256)
-        grads[g, :, 80:160, :] = nn(du_t, xg).astype(bf16).reshape(4, 80, 256)
-        grads[g, :, 160:240, :] = nn(hid_t, ds[:, 256 * g : 256 * g + 256]).astype(bf16).reshape(4, 80, 256)
+        grads[:, g, 0:80, :] = nn(dg_t, xg).astype(bf16).reshape(4, 80, 256)
+        grads[:, g, 80:160, :] = nn(du_t, xg).astype(bf16).reshape(4, 80, 256)
+        grads[:, g, 160:240, :] = nn(hid_t, ds[:, 256 * g : 256 * g + 256]).astype(bf16).reshape(4, 80, 256)
         dn = nn(d_gate, wg[g].reshape(320, 256)) + nn(d_up, wu[g].reshape(320, 256))
         no[:, 256 * g : 256 * g + 256] += dn[:TOK]
         nr[:, 256 * g : 256 * g + 256] += dn[TOK:]
@@ -205,9 +216,9 @@
 
 def attend_back_kernel(
     sel, own, recv, no, nr, mid_ref, gain_ref, dy_ref, qkv, r1, r2, r3, mask, pnb,
-    dmid_ref, dproj_ref, gg_ref, dq_ref, dkv_ref, d1, d2, d3, buf, kvs, dkv, sem,
+    dmid_ref, dproj_ref, gg_ref, dq_ref, dkv_ref, d1, d2, d3, buf, kvs, dkv, sems,
 ):
-    pick(sel, own, recv, 112, 64, buf, sem)
+    pick(sel, (own,), (recv,), buf, sems)
     for k, part in enumerate((r3, r2, r1)):
         kvs[TOK * k : TOK * k + TOK, :] = part[...]
     kvs[3 * TOK :, :] = qkv[:, : 2 * KW]
@@ -220,7 +231,7 @@
     dmid_ref[...] = dmid
     dproj = dmid.astype(bf16)
     dproj_ref[...] = dproj
-    arrived(own, 112, 64, buf, sem)
+    arrived((own,), buf, sems)
     datt = None
     for j in range(4):
         a = nt(dproj[:, 256 * j : 256 * j + 256], chunk_of(buf, j))
@@ -257,17 +268,17 @@
 
 
 def project_back_kernel(
-    sel, own, recv, dq, dkv, e1, e2, e3, cosw, sinw, norm_ref, x_ref, gain_ref, dmid_ref, pba, attb, dproj, gg,
-    dx_ref, grads, buf, sem,
+    sel, own_a, own_b, recv_a, recv_b, dq, dkv, e1, e2, e3, cosw, sinw, norm_ref, x_ref, gain_ref, dmid_ref, pba, attb,
+    dproj, gg, core, dx_ref, keep, send, buf, sems,
 ):
-    pick(sel, own, recv, 0, 112, buf, sem)
+    pick(sel, (own_a, own_b), (recv_a, recv_b), buf, sems)
     kv = dkv[...] + e1[...].astype(f32) + e2[...].astype(f32) + e3[...].astype(f32)
     d = jnp.concatenate([kv, dq[...]], axis=1)
     low = lane_in_head(d.shape) < HD // 2
     scaled = d * sinw[...]
     turned = jnp.where(low, pltpu.roll(scaled, QKVW - 32, 1), -pltpu.roll(scaled, 32, 1))
     dp = (d * cosw[...] + turned).astype(bf16)
-    arrived(own, 0, 112, buf, sem)
+    arrived((own_a, own_b), buf, sems)
     dn_b = None
     for j in range(7):
         a = nt(dp[:, 256 * j : 256 * j + 256], chunk_of(buf, j))
@@ -282,16 +293,22 @@
     row = lax.broadcasted_iota(jnp.int32, (256, WA), 0)
     gains = jnp.where(row == 64, g1, jnp.where(row == 65, gg[0:1, :], 0.0)).astype(bf16)
     norm_t = norm_ref[...].T
-    for j in range(7):
-        g = nn(norm_t, dp[:, 256 * j : 256 * j + 256])
+    att_t = attb[...].T
+
+    def put(target, j, g):
+        target[:, 16 * (j % 6) : 16 * (j % 6) + 16, :] = g.astype(bf16).reshape(64, 16, 256)
+
+    for j in range(12):
+        if j < 7:
+            g = nn(norm_t, dp[:, 256 * j : 256 * j + 256])
+        elif j < 11:
+            g = nn(att_t, dproj[:, 256 * (j - 7) : 256 * (j - 6)])
+        else:
+            g = jnp.zeros((WA, 256), f32)
         if j == 6:
             g = g + nt(pba[...], gains)
-        grads[:, 16 * j : 16 * j + 16, :] = g.astype(bf16).reshape(64, 16, 256)
-    att_t = attb[...].T
-    for j in range(4):
-        g = nn(att_t, dproj[:, 256 * j : 256 * j + 256])
-        grads[:, 112 + 16 * j : 128 + 16 * j, :] = g.astype(bf16).reshape(64, 16, 256)
-    grads[:, 176:192, :] = jnp.zeros((64, 16, 256), bf16)
+        pl.when(core[0] == j // 6)(functools.partial(put, keep, j, g))
+        pl.when(core[0] != j // 6)(functools.partial(put, send, j, g))
 
 
 VM = pl.BlockSpec(memory_space=pltpu.VMEM)
@@ -305,24 +322,24 @@
 
 def project(sel, own, recv, pab, pba, cosw, sinw, x=None, parts=None):
     outs = [sds((TOK, WA), bf16), sds((TOK, QKVW), bf16), sds((TOK, 2 * KW), bf16), sds((8, WA), f32)]
-    ins = [sel, own, recv, pab, pba, cosw, sinw] + ([x] if parts is None else list(parts))
+    ins = [sel, *own[:2], *recv[:2], pab, pba, cosw, sinw] + ([x] if parts is None else list(parts))
     if parts is not None:
         outs = [sds((TOK, WA), bf16)] + outs
     res = call(
         functools.partial(project_kernel, parts is None),
-        outs, ins, [SM, ANY, ANY] + [VM] * (len(ins) - 3),
-        [weight_scratch(112), pltpu.SemaphoreType.DMA], name="project",
+        outs, ins, [SM] + [ANY] * 4 + [VM] * (len(ins) - 5),
+        [weight_scratch(112), pltpu.SemaphoreType.DMA((2,))], name="project",
     )
     return ([x] + list(res)) if parts is None else res
 
 
 def attend(sel, own, recv, qkv, chunks, mask, x, gains, pnb):
-    ins = [sel, own, recv, qkv, *chunks, mask, x, gains, pnb]
+    ins = [sel, own[2], recv[2], qkv, *chunks, mask, x, gains, pnb]
     return call(
         attend_kernel,
         [sds((TOK, WA), bf16), sds((TOK, WA), f32), sds((TOK, WA), bf16)],
         ins, [SM, ANY, ANY] + [VM] * (len(ins) - 3),
-        [weight_scratch(64), pltpu.VMEM((LEN, 2 * KW), bf16), pltpu.VMEM((TOK, QW), bf16), pltpu.SemaphoreType.DMA],
+        [weight_scratch(64), pltpu.VMEM((LEN, 2 * KW), bf16), pltpu.VMEM((TOK, QW), bf16), pltpu.SemaphoreType.DMA((1,))],
         name="attend",
     )
 
@@ -346,31 +363,31 @@
 def ffn_back(section, xo, xr, do, dr, packed):
     row = whole((TOK, WA))
     return call(
-        ffn_back_kernel, [sds((4, 16, 240, 256), bf16)] + [sds((TOK, WA), f32)] * 2,
+        ffn_back_kernel, [sds((16, 4, 240, 256), bf16)] + [sds((TOK, WA), f32)] * 2,
         [xo, xr, do, dr, packed, packed, packed],
         [row] * 4 + weight_specs(section), grid=(4,),
-        out_specs=[pl.BlockSpec((4, 4, 240, 256), lambda j: (0, j, 0, 0)), row, row], name="ffn_back",
+        out_specs=[pl.BlockSpec((4, 4, 240, 256), lambda j: (j, 0, 0, 0)), row, row], name="ffn_back",
     )
 
 
 def attend_back(sel, own, recv, no, nr, mid, gains, dy, qkv, chunks, mask, pnb):
-    ins = [sel, own, recv, no, nr, mid, gains, dy, qkv, *chunks, mask, pnb]
+    ins = [sel, own[2], recv[2], no, nr, mid, gains, dy, qkv, *chunks, mask, pnb]
     small = sds((TOK, 2 * KW), bf16)
     return call(
         attend_back_kernel,
         [sds((TOK, WA), f32), sds((TOK, WA), bf16), sds((8, WA), f32), sds((TOK, 1152), f32), sds((TOK, 2 * KW), f32), small, small, small],
         ins, [SM, ANY, ANY] + [VM] * (len(ins) - 3),
-        [weight_scratch(64), pltpu.VMEM((LEN, 2 * KW), bf16), pltpu.VMEM((LEN, 2 * KW), f32), pltpu.SemaphoreType.DMA],
+        [weight_scratch(64), pltpu.VMEM((LEN, 2 * KW), bf16), pltpu.VMEM((LEN, 2 * KW), f32), pltpu.SemaphoreType.DMA((1,))],
         name="attend_back",
     )
 
 
-def project_back(sel, own, recv, *rest):
-    ins = [sel, own, recv, *rest]
+def project_back(sel, own, recv, core, *rest):
+    ins = [sel, *own[:2], *recv[:2], *rest, core]
     return call(
-        project_back_kernel, [sds((TOK, WA), bf16), sds((64, 192, 256), bf16)],
-        ins, [SM, ANY, ANY] + [VM] * (len(ins) - 3),
-        [weight_scratch(112), pltpu.SemaphoreType.DMA], name="project_back",
+        project_back_kernel, [sds((TOK, WA), bf16)] + [sds((64, 96, 256), bf16)] * 2,
+        ins, [SM] + [ANY] * 4 + [VM] * (len(ins) - 6) + [SM],
+        [weight_scratch(112), pltpu.SemaphoreType.DMA((2,))], name="project_back",
     )
 
 
@@ -386,31 +403,78 @@
     return "gy", [(i, (i // 4) * 4 + (i % 4 + k) % 4) for i in range(16)]
 
 
-def reduce_stage(v, dim, name, me):
-    got = []
-    for k in (1, 3, 2):
-        piece = lax.dynamic_index_in_dim(v, (me + k) % 4, dim, keepdims=False)
-        axis, perm = shift_perm(name, k)
-        got.append(lax.ppermute(piece, axis, perm))
-    total = lax.dynamic_index_in_dim(v, me, dim, keepdims=False).astype(f32)
-    for piece in got:
-        total = total + piece.astype(f32)
-    return total.astype(bf16)
-
-
-def reduce_parts(parts, place):
-    names = ["x", "z", "y"]
-    orders = [["x", "y", "z"], ["y", "z", "x"], ["z", "x", "y"]]
-    state = [(p, list(names)) for p in parts]
+def permuted(v, name, k):
+    axis, perm = shift_perm(name, k)
+    return lax.ppermute(v, axis, perm)
+
+
+ORDERS = (("x", "y", "z"), ("y", "z", "x"), ("z", "x", "y"))
+GROUPS = (((0, 1), (0, 3), (1, 1), (1, 3), (2, 2)), ((0, 2), (1, 2), (2, 1), (2, 3)))
+
+
+def exchange(pieces, names, grouped, beside=()):
+    keys = list(pieces)
+    pieces = dict(zip(keys, lax.optimization_barrier([pieces[key] for key in keys])))
+    if not grouped:
+        return {key: permuted(pieces[key], names[key[0]], key[1]) for key in keys}, beside
+    got = {key: permuted(pieces[key], names[key[0]], key[1]) for key in GROUPS[0]}
+    tied = lax.optimization_barrier([[got[key] for key in GROUPS[0]], [pieces[key] for key in GROUPS[1]], list(beside)])
+    got = dict(zip(GROUPS[0], tied[0]))
+    for key, piece in zip(GROUPS[1], tied[1]):
+        got[key] = permuted(piece, names[key[0]], key[1])
+    return got, tied[2]
+
+
+def gather_chunks(chunks, beside):
+    state = [(c, ()) for c in chunks]
     for step in range(3):
+        names = [order[step] for order in ORDERS]
+        pieces = {(c, k): state[c][0] for c in range(3) for k in (1, 2, 3)}
+        got, tied = exchange(pieces, names, step == 2, beside)
+        if step == 2:
+            beside = tied
         after = []
-        for index, (v, left) in enumerate(state):
-            name = orders[index % 3][step]
-            dim = left.index(name)
-            v = reduce_stage(v, dim, name, place[name])
-            after.append((v, [n for n in left if n != name]))
+        for c in range(3):
+            v, have = state[c]
+            have = tuple(n for n in ("z", "y", "x") if n in have or n == names[c])
+            v = jnp.stack([v, got[(c, 3)], got[(c, 2)], got[(c, 1)]], axis=have.index(names[c]))
+            after.append((v, have))
         state = after
-    return [v for v, _ in state]
+    return [v.reshape((64,) + v.shape[3:]) for v, _ in state], beside
+
+
+def reduce_bundles(bundles, place, last):
+    left = [("z", "y", "x")] * 3
+    for step in range(3):
+        names = [order[step] for order in ORDERS]
+        if step == 2:
+            bundles[1] = bundles[1] + [last]
+        pieces, mine = {}, []
+        for c in range(3):
+            dim = left[c].index(names[c])
+            me = place[names[c]]
+
+            def part(v, own_first, k):
+                if own_first:
+                    return lax.index_in_dim(v, k, dim, keepdims=False)
+                return lax.dynamic_index_in_dim(v, (me + k) % 4, dim, keepdims=False)
+
+            mine.append([part(v, own_first, 0) for v, own_first in bundles[c]])
+            for k in (1, 2, 3):
+                pieces[(c, k)] = jnp.concatenate([part(v, own_first, k) for v, own_first in bundles[c]], axis=-2)
+        got, _ = exchange(pieces, names, step == 0)
+        for c in range(3):
+            row, summed = 0, []
+            for v, (_, own_first) in zip(mine[c], bundles[c]):
+                rows = v.shape[-2]
+                total = v.astype(f32)
+                for k in (1, 2, 3):
+                    total = total + got[(c, k)][..., row : row + rows, :].astype(f32)
+                row += rows
+                summed.append((total.astype(bf16), own_first))
+            bundles[c] = summed
+            left[c] = tuple(n for n in left[c] if n != names[c])
+    return [[v for v, _ in bundle] for bundle in bundles]
 
 
 def rope_tables(positions):
@@ -435,10 +499,12 @@
     return v.reshape(v.shape[:-1] + (4, 256))[..., :240].reshape(v.shape[:-1] + (D,))
 
 
-def place_matrices():
+def place_matrices(place):
     a = jnp.arange(WA, dtype=jnp.int32)
     in_a = jnp.where(a % 256 < 240, (a // 256) * 240 + a % 256, -1)
-    in_b = jnp.where(a % 16 < 15, (a // 16) * 15 + a % 16, -2)
+    shard = a // 16
+    x, z, y = (place["x"] + shard) % 4, (place["z"] + shard // 16) % 4, (place["y"] + shard // 4) % 4
+    in_b = jnp.where(a % 16 < 15, (x * 16 + z * 4 + y) * 15 + a % 16, -2)
     pab = (in_a[:, None] == in_b[None, :]).astype(bf16)
     pba = (in_b[:, None] == in_a[None, :]).astype(bf16)
     pnb = (jnp.arange(QW, dtype=jnp.int32)[:, None] == in_b[None, :]).astype(bf16)
@@ -469,10 +535,7 @@
         1,
     )
     attn = jnp.pad(attn, ((0, 1), (0, 0))).reshape(16, 11, 256).transpose(1, 0, 2).reshape(AROWS, 256)
-    packed = lax.all_gather(jnp.concatenate([halves, attn], 0)[None], ("gx", "gy"), axis=0, tiled=True)
-    own = packed[:, FROWS:, :]
-    recv = other_core(own)
-    packed = packed.reshape(4, 16, FROWS + AROWS, 256)
+    packed = lax.all_gather(halves[None], ("gx", "gy"), axis=0, tiled=True).reshape(4, 16, FROWS, 256)
 
     own_in = to_a(jnp.where(first, inputs[0, 0], inputs[1, 0]))
     cot0, cot1 = to_a(cotangent[0, 0]), to_a(cotangent[1, 0])
@@ -485,7 +548,10 @@
     key_ids = lax.dynamic_slice_in_dim(jnp.pad(segments, (3 * TOK, 0), constant_values=-1), gx * TOK, LEN, 0)
     mask = ((local_ids[:, None] == key_ids[None, :]) & (key_index[None, :] <= own_index[:, None])).astype(f32)
     cosw, sinw = rope_tables(own_index - doc_start)
-    pab, pba, pnb = place_matrices()
+    beside = [cosw, sinw, mask, own_in, cot_own, cot_other, *place_matrices(place)]
+    own, beside = gather_chunks([attn[:64], attn[64:112], attn[112:]], beside)
+    cosw, sinw, mask, own_in, cot_own, cot_other, pab, pba, pnb = beside
+    recv = [other_core(w) for w in own]
 
     def ahead(v, k):
         return lax.ppermute(v, "gx", [(i, i + k) for i in range(4 - k)])
@@ -516,32 +582,27 @@
         dmid, dproj, gg, dq, dkv, d1, d2, d3 = attend_back(
             sel, own, recv, no, other_core(nr), mid, gains, dy, qkv, chunks, mask, pnb
         )
-        dy, attn_grads[section] = project_back(
-            sel, own, recv, dq, dkv, back(d1, 1), back(d2, 2), back(d3, 3),
+        dy, keep, send = project_back(
+            sel, own, recv, sels[0], dq, dkv, back(d1, 1), back(d2, 2), back(d3, 3),
             cosw, sinw, norm_b, x, gains, dmid, pba, attb, dproj, gg,
         )
         grads_in[section] = dy
+        attn_grads[section] = (keep, other_core(send))
         if section == 1:
             dy_other = other_core(dy)
 
-    late = lax.psum_scatter(ffn_grads[1], "gx", scatter_dimension=0, tiled=True)
-    late = lax.psum_scatter(late[0], "gy", scatter_dimension=0, tiled=True)[0]
-
-    def half_sum(v):
-        send = lax.dynamic_slice_in_dim(v, (1 - core) * 96, 96, 1)
-        mine = lax.dynamic_slice_in_dim(v, core * 96, 96, 1)
-        return (mine.astype(f32) + other_core(send).astype(f32)).astype(bf16)
-
-    halved = [half_sum(attn_grads[0]), half_sum(attn_grads[1])]
-    early = ffn_grads[0].reshape(64, 240, 256)
-    chunks = [
-        jnp.concatenate([early[:, :144]], 1),
-        jnp.concatenate([early[:, 144:], halved[0][:, :48]], 1),
-        jnp.concatenate([halved[0][:, 48:], halved[1]], 1),
+    late = lax.psum_scatter(ffn_grads[1].reshape(16, 960, 256), "gy", scatter_dimension=0, tiled=True).reshape(4, 240, 256)
+    halved = []
+    for keep, got in attn_grads:
+        halved.append((keep.astype(f32) + got.astype(f32)).astype(bf16).reshape(4, 4, 4, 96, 256))
+    early = ffn_grads[0].reshape(4, 4, 4, 240, 256)
+    bundles = [
+        [(early[..., :144, :], False)],
+        [(early[..., 144:, :], False), (halved[0][..., :48, :], True)],
+        [(halved[0][..., 48:, :], True), (halved[1], True)],
     ]
-    done = reduce_parts([c.reshape(4, 4, 4, 144, 256) for c in chunks], place)
-    flat = jnp.concatenate(done, 0)
-    half = [jnp.concatenate([flat[:240], flat[240:336]], 0), jnp.concatenate([late, flat[336:432]], 0)]
+    (e0,), (e1, a0, late), (a1, b) = reduce_bundles(bundles, place, (late, False))
+    half = [jnp.concatenate([e0, e1, a0, a1], 0), jnp.concatenate([late, b], 0)]
     mine = jnp.where(first, half[0], half[1])
     theirs = other_core(jnp.where(first, half[1], half[0]))
     low, high = jnp.where(first, mine, theirs), jnp.where(first, theirs, mine)

time: 624 us -> 505 us (0.81)
  waiting for transfers between devices: 295 us -> 136 us
  starting transfers between devices: 105 us -> 131 us
  other arithmetic: 29.1 us -> 44.1 us
  local copies, waits for them, and re-layouts: 54.6 us -> 44.6 us
  Pallas kernels: 116 us -> 124 us
    all_gather x1, waiting for transfers between devices: 121 us -> 0.01 us  [per_device(): lax.all_gather(halves[None], ('gx', 'gy'), axis=0, tiled=True)]
    ppermute x27 -> x54, waiting for transfers between devices: 130 us -> 86.1 us  [permuted(): return lax.ppermute(v, axis, perm)]
    ppermute x14 -> x16, starting transfers between devices: 16.1 us -> 31.5 us  [other_core(): return lax.ppermute(v, 'section', [(0, 1), (1, 0)])]
    ppermute x14 -> x16, waiting for transfers between devices: 6.52 us -> 17.4 us  [other_core(): return lax.ppermute(v, 'section', [(0, 1), (1, 0)])]
    dynamic_slice x6 -> x1, local copies, waits for them, and re-layouts: 11.1 us -> 1.42 us  [part(): return lax.dynamic_index_in_dim(v, (me + k) % 4, dim, keepdims=False)]
    another operation x0 -> x9, other arithmetic: none -> 9.35 us  [gather_chunks(): jnp.stack([v, got[c, 3], got[c, 2], got[c, 1]], axis=have.index(names[c]))]
    ppermute x27 -> x54, starting transfers between devices: 64.7 us -> 73.8 us  [permuted(): return lax.ppermute(v, axis, perm)]
    pallas_call x12, Pallas kernels: 116 us -> 124 us  [call(): pl.pallas_call(kernel, out_shape=outs, in_specs=specs if specs is not Non...]
  transfers between devices with their start and end apart: 56 -> 84, of which waited for: 28 -> 40; matrix products, arithmetic and copies ran while one was open for 10% -> 13% of each run, Pallas kernels for 11% -> 18%
where the time goes in v2:
time: 505 us; the launch traced here: 495 us
  waiting for transfers between devices  136 us (27%)
  starting transfers between devices  131 us (26%)
  Pallas kernels  124 us (25%)
  local copies, waits for them, and re-layouts  44.6 us (9%)
  other arithmetic  44.1 us (9%)
  between operations  15.6 us (3%)
    pallas_call x12, Pallas kernels, call(): pl.pallas_call(kernel, out_shape=outs, in_specs=specs if specs is not Non...  124 us
    ppermute x54, waiting for transfers between devices, permuted(): return lax.ppermute(v, axis, perm)  86.1 us
    ppermute x54, starting transfers between devices, permuted(): return lax.ppermute(v, axis, perm)  73.8 us
    ppermute x16, starting transfers between devices, other_core(): return lax.ppermute(v, 'section', [(0, 1), (1, 0)])  31.5 us
    ppermute x6, waiting for transfers between devices, back(): return lax.ppermute(v, 'gx', [(i + k, i) for i in range(4 - k)])  22 us
    unnamed x126, local copies, waits for them, and re-layouts  21.7 us
    ppermute x6, starting transfers between devices, ahead(): return lax.ppermute(v, 'gx', [(i, i + k) for i in range(4 - k)])  17.8 us
    ppermute x16, waiting for transfers between devices, other_core(): return lax.ppermute(v, 'section', [(0, 1), (1, 0)])  17.4 us
  transfers between devices with their start and end apart: 84, of which 40 were waited for; matrix products, arithmetic and copies ran while one was open for 13% of the time, Pallas kernels for 18%

profile of v2, /device:TPU:1, one launch (start us, length us, event | category | flops | bytes accessed | tf_op | source)
XLA Modules:
  0.0 495.2 jit_solution(16061539428547856480)
XLA Ops:
  12.5 2.9 collective-permute-start.3
  16.4 2.5 collective-permute-start
  20.7 2.1 fusion.pnb
  22.8 3.8 collective-permute-start.6
  28.8 2.1 collective-permute-done.7
  32.6 2.9 collective-permute-start.12
  42.1 2.8 collective-permute-start.9
  51.0 4.6 collective-permute-done.11
  65.4 2.7 collective-permute-start.21
  68.1 2.4 compare_convert_fusion
  70.5 3.1 collective-permute-done.20
  80.0 4.4 collective-permute-done.23
  86.2 13.1 %collective-permute-start.25 = (bf16[64,64,256]{2,1,0:T(8,128)(2,1)S(1)}, bf16[64,64,256]{2,1,0:T(8,128)(2,1)S(1)}, u32[]{:S(2)}, u32[]{:S(2)}) collective-permute-start(bf16[64,64,256]{2,1,0:T(8,128)(2,1)S(1)} %bitcast.340), channel_id=1, source_target_pairs={{0,64},{64,0},{1,65},{65,1},{2,66},{66,2},{3,67},{67,3},{4,68},{68... | collective-permute-start | bytes 6291464 | tf_op jit(solution)/shard_map/ppermute | solution.py:395
  102.1 5.4 %collective-permute-start.29 = (bf16[64,64,256]{2,1,0:T(8,128)(2,1)}, bf16[64,64,256]{2,1,0:T(8,128)(2,1)}, u32[]{:S(2)}, u32[]{:S(2)}) collective-permute-start(bf16[64,64,256]{2,1,0:T(8,128)(2,1)} %bitcast.56.own), channel_id=1, source_target_pairs={{0,64},{64,0},{1,65},{65,1},{2,66},{66,2},{3,67},{67,3},{4,68},{68... | collective-permute-start | bytes 6291464 | tf_op jit(solution)/shard_map/ppermute | solution.py:395
  108.0 5.5 %collective-permute-done.26.recv_b = bf16[64,48,256]{2,1,0:T(8,128)(2,1)S(1)} collective-permute-done((bf16[64,48,256]{2,1,0:T(8,128)(2,1)S(1)}, bf16[64,48,256]{2,1,0:T(8,128)(2,1)S(1)}, u32[]{:S(2)}, u32[]{:S(2)}) %collective-permute-start.26) | collective-permute-done | bytes 1572896 | tf_op jit(solution)/shard_map/ppermute | solution.py:395
  116.0 7.7 %project.2 = (bf16[128,1024]{1,0:T(8,128)(2,1)}, bf16[128,1792]{1,0:T(8,128)(2,1)}, bf16[128,640]{1,0:T(8,128)(2,1)}, f32[8,1024]{1,0:T(8,128)}) custom-call(s32[1]{0:T(128)} %bitcast.51.sel.core, bf16[64,64,256]{2,1,0:T(8,128)(2,1)} %bitcast.341, bf16[64,48,256]{2,1,0:T(8,128)(2,1)} %bitcast.346, bf16[64,64,256]{2,1,0:T(8,128)(2,1)} %copy-done.2, ...), custom_call_target="tpu_custom_call" | custom-call | tf_op jit(solution)/shard_map/project/pallas_call | solution.py:40
  123.7 5.1 %collective-permute-start.32 = (bf16[128,640]{1,0:T(8,128)(2,1)}, bf16[128,640]{1,0:T(8,128)(2,1)S(1)}, u32[]{:S(2)}, u32[]{:S(2)}) collective-permute-start(bf16[128,640]{1,0:T(8,128)(2,1)} %get-tuple-element.179), channel_id=1, source_target_pairs={{0,48},{1,49},{2,50},{3,51},{4,52},{5,53},{6,54},{7,55},{8,56},{9,... | collective-permute-start | bytes 491528 | tf_op jit(solution)/shard_map/ppermute | solution.py:557
  130.1 2.5 collective-permute-start.30
  132.6 5.5 %collective-permute-done.32.r3 = bf16[128,640]{1,0:T(8,128)(2,1)S(1)} collective-permute-done((bf16[128,640]{1,0:T(8,128)(2,1)}, bf16[128,640]{1,0:T(8,128)(2,1)S(1)}, u32[]{:S(2)}, u32[]{:S(2)}) %collective-permute-start.32) | collective-permute-done | bytes 163872 | tf_op jit(solution)/shard_map/ppermute | solution.py:557
  138.9 7.1 %attend.2 = (bf16[128,1024]{1,0:T(8,128)(2,1)}, f32[128,1024]{1,0:T(8,128)}, bf16[128,1024]{1,0:T(8,128)(2,1)}) custom-call(s32[1]{0:T(128)} %bitcast.51.sel.core, bf16[64,64,256]{2,1,0:T(8,128)(2,1)} %bitcast.56.own, bf16[64,64,256]{2,1,0:T(8,128)(2,1)} %collective-permute-done.29.recv, bf16[128,1792]{1,0:T(8,128)(2,1)} %get-tuple-element.178.qkv, ...), custom_call_target="tpu_custom_call" | custom-call | tf_op jit(solution)/shard_map/attend/pallas_call | solution.py:40
  148.7 7.5 %ffn.2 = (f32[128,1024]{1,0:T(8,128)}, f32[128,1024]{1,0:T(8,128)}) custom-call(bf16[128,1024]{1,0:T(8,128)(2,1)} %get-tuple-element.184.xo, bf16[128,1024]{1,0:T(8,128)(2,1)} %copy-done.26, bf16[4,16,480,256]{3,2,1,0:T(8,128)(2,1)} %bitcast.328, bf16[4,16,480,256]{3,2,1,0:T(8,128)(2,1)} %bitcast.329, bf16[4,16,480,256]{3,2,1,0:T(8,128)(2,1)} %bitcast.330), custom_call_target="tpu_custom_call" | custom-call | tf_op jit(solution)/shard_map/ffn/pallas_call | solution.py:40
  159.6 7.8 %project.3 = (bf16[128,1024]{1,0:T(8,128)(2,1)}, bf16[128,1024]{1,0:T(8,128)(2,1)}, bf16[128,1792]{1,0:T(8,128)(2,1)}, bf16[128,640]{1,0:T(8,128)(2,1)}, f32[8,1024]{1,0:T(8,128)}) custom-call(s32[1]{0:T(128)} %bitcast.sel, bf16[64,64,256]{2,1,0:T(8,128)(2,1)} %bitcast.342, bf16[64,48,256]{2,1,0:T(8,128)(2,1)} %bitcast.347, bf16[64,64,256]{2,1,0:T(8,128)(2,1)} %copy-done.2, ...), custom_call_target="tpu_custom_call" | custom-call | tf_op jit(solution)/shard_map/project/pallas_call | solution.py:40
  167.4 5.2 %collective-permute-start.38 = (bf16[128,640]{1,0:T(8,128)(2,1)}, bf16[128,640]{1,0:T(8,128)(2,1)S(1)}, u32[]{:S(2)}, u32[]{:S(2)}) collective-permute-start(bf16[128,640]{1,0:T(8,128)(2,1)} %get-tuple-element.189), channel_id=1, source_target_pairs={{0,48},{1,49},{2,50},{3,51},{4,52},{5,53},{6,54},{7,55},{8,56},{9,... | collective-permute-start | bytes 491528 | tf_op jit(solution)/shard_map/ppermute | solution.py:557
  174.0 2.5 collective-permute-start.36
  176.5 3.1 collective-permute-done.38.r3
  181.6 7.1 %attend.3 = (bf16[128,1024]{1,0:T(8,128)(2,1)}, f32[128,1024]{1,0:T(8,128)}, bf16[128,1024]{1,0:T(8,128)(2,1)}) custom-call(s32[1]{0:T(128)} %bitcast.sel, bf16[64,64,256]{2,1,0:T(8,128)(2,1)} %bitcast.56.own, bf16[64,64,256]{2,1,0:T(8,128)(2,1)} %collective-permute-done.29.recv, bf16[128,1792]{1,0:T(8,128)(2,1)} %get-tuple-element.188.qkv, ...), custom_call_target="tpu_custom_call" | custom-call | tf_op jit(solution)/shard_map/attend/pallas_call | solution.py:40
  192.1 12.3 %ffn_back.2 = (bf16[16,4,240,256]{3,2,1,0:T(8,128)(2,1)}, f32[128,1024]{1,0:T(8,128)}, f32[128,1024]{1,0:T(8,128)}) custom-call(bf16[128,1024]{1,0:T(8,128)(2,1)} %get-tuple-element.192.xo, bf16[128,1024]{1,0:T(8,128)(2,1)} %copy-done.25, bf16[128,1024]{1,0:T(8,128)(2,1)} %bitcast.363, bf16[128,1024]{1,0:T(8,128)(2,1)} %bitcast.373, ...), custom_call_target="tpu_custom_call" | custom-call | tf_op jit(solution)/shard_map/ffn_back/pallas_call | solution.py:40
  208.3 11.3 %attend_back.2 = (f32[128,1024]{1,0:T(8,128)}, bf16[128,1024]{1,0:T(8,128)(2,1)}, f32[8,1024]{1,0:T(8,128)}, f32[128,1152]{1,0:T(8,128)}, f32[128,640]{1,0:T(8,1...) custom-call(s32[1]{0:T(128)} %bitcast.sel, bf16[64,64,256]{2,1,0:T(8,128)(2,1)} %bitcast.56.own, ...), custom_call_target="tpu_custom_call" | custom-call | tf_op jit(solution)/shard_map/attend_back/pallas_call | solution.py:40
  223.5 4.7 collective-permute-done.43.e1
  228.2 2.7 collective-permute-done.44.e2
  230.9 4.3 collective-permute-done.45.e3
  235.9 16.4 %project_back.2 = (bf16[128,1024]{1,0:T(8,128)(2,1)}, bf16[64,96,256]{2,1,0:T(8,128)(2,1)}, bf16[64,96,256]{2,1,0:T(8,128)(2,1)}) custom-call(s32[1]{0:T(128)} %bitcast.sel, bf16[64,64,256]{2,1,0:T(8,128)(2,1)} %bitcast.343, bf16[64,48,256]{2,1,0:T(8,128)(2,1)} %bitcast.348, bf16[64,64,256]{2,1,0:T(8,128)(2,1)} %copy-done.2, bf16[64,48,256]{2,1,0:T(8,128)(2,1)} %copy-done.3, ...), custom_call_target="tpu_custom_call" | custom-call | tf_op jit(solution)/shard_map/project_back/pallas_call | solution.py:40
  254.8 12.3 %ffn_back.3 = (bf16[16,4,240,256]{3,2,1,0:T(8,128)(2,1)}, f32[128,1024]{1,0:T(8,128)}, f32[128,1024]{1,0:T(8,128)}) custom-call(bf16[128,1024]{1,0:T(8,128)(2,1)} %get-tuple-element.184.xo, bf16[128,1024]{1,0:T(8,128)(2,1)} %copy-done.26, bf16[128,1024]{1,0:T(8,128)(2,1)} %get-tuple-element.209.do.dy_ref, bf16[128,1024]{1,0:T(8,128)(2,1)} %copy-done.42, ...), custom_call_target="tpu_custom_call" | custom-call | tf_op jit(solution)/shard_map/ffn_back/pallas_call | solution.py:40
  270.1 11.2 %attend_back.3 = (f32[128,1024]{1,0:T(8,128)}, bf16[128,1024]{1,0:T(8,128)(2,1)}, f32[8,1024]{1,0:T(8,128)}, f32[128,1152]{1,0:T(8,128)}, f32[128,640]{1,0:T(8,1...) custom-call(s32[1]{0:T(128)} %bitcast.51.sel.core, ...), custom_call_target="tpu_custom_call" | custom-call | tf_op jit(solution)/shard_map/attend_back/pallas_call | solution.py:40
  285.3 3.7 collective-permute-done.48.e1
  289.0 2.7 collective-permute-done.49.e2
  291.7 3.9 collective-permute-done.50.e3
  296.3 16.2 %project_back.3 = (bf16[128,1024]{1,0:T(8,128)(2,1)}, bf16[64,96,256]{2,1,0:T(8,128)(2,1)}, bf16[64,96,256]{2,1,0:T(8,128)(2,1)}) custom-call(s32[1]{0:T(128)} %bitcast.51.sel.core, bf16[64,64,256]{2,1,0:T(8,128)(2,1)} %bitcast.344, bf16[64,48,256]{2,1,0:T(8,128)(2,1)} %bitcast.349, bf16[64,64,256]{2,1,0:T(8,128)(2,1)} %copy-done.2, ...), custom_call_target="tpu_custom_call" | custom-call | tf_op jit(solution)/shard_map/project_back/pallas_call | solution.py:40
  313.4 2.2 slice.468
  315.6 2.7 slice.467
  322.8 3.1 add_convert_fusion
  328.1 3.1 add_convert_fusion.1
  336.7 2.7 collective-permute-start.55
  342.1 2.7 collective-permute-start.58
  344.8 20.6 %collective-permute-done.54 = bf16[4,4,144,256]{3,2,0,1:T(8,128)(2,1)S(1)} collective-permute-done((bf16[4,4,144,256]{3,2,0,1:T(8,128)(2,1)S(1)}, bf16[4,4,144,256]{3,2,0,1:T(8,128)(2,1)S(1)}, u32[]{:S(2)}, u32[]{:S(2)}) %collective-permute-start.54) | collective-permute-done | bytes 1179680 | tf_op jit(solution)/shard_map/ppermute | solution.py:408
  367.4 2.4 collective-permute-done.58
  372.4 7.4 %ffn.3 = (f32[128,1024]{1,0:T(8,128)}, f32[128,1024]{1,0:T(8,128)}) custom-call(bf16[128,1024]{1,0:T(8,128)(2,1)} %get-tuple-element.192.xo, bf16[128,1024]{1,0:T(8,128)(2,1)} %copy-done.25, bf16[4,16,480,256]{3,2,1,0:T(8,128)(2,1)} %bitcast.337, bf16[4,16,480,256]{3,2,1,0:T(8,128)(2,1)} %bitcast.338, bf16[4,16,480,256]{3,2,1,0:T(8,128)(2,1)} %bitcast.339), custom_call_target="tpu_custom_call" | custom-call | tf_op jit(solution)/shard_map/ffn/pallas_call | solution.py:40
  379.8 2.6 collective-permute-start.40
  386.3 3.1 collective-permute-start.61
  390.8 7.2 %collective-permute-done.60 = bf16[4,4,144,256]{3,2,1,0:T(8,128)(2,1)} collective-permute-done((bf16[4,4,144,256]{3,2,1,0:T(8,128)(2,1)}, bf16[4,4,144,256]{3,2,1,0:T(8,128)(2,1)}, u32[]{:S(2)}, u32[]{:S(2)}) %collective-permute-start.60) | collective-permute-done | bytes 1179680 | tf_op jit(solution)/shard_map/ppermute | solution.py:408
  397.9 2.1 fusion.6
  404.2 12.9 %collective-permute-done.61 = bf16[4,4,144,256]{3,2,0,1:T(8,128)(2,1)S(1)} collective-permute-done((bf16[4,4,144,256]{3,2,0,1:T(8,128)(2,1)}, bf16[4,4,144,256]{3,2,0,1:T(8,128)(2,1)S(1)}, u32[]{:S(2)}, u32[]{:S(2)}) %collective-permute-start.61) | collective-permute-done | bytes 1179680 | tf_op jit(solution)/shard_map/ppermute | solution.py:408
  423.7 2.4 collective-permute-start.70
  426.1 2.1 collective-permute-start.71
  430.0 3.2 collective-permute-start.64
  433.6 5.6 %collective-permute-done.70 = bf16[4,144,256]{2,1,0:T(8,128)(2,1)} collective-permute-done((bf16[4,144,256]{2,1,0:T(8,128)(2,1)}, bf16[4,144,256]{2,1,0:T(8,128)(2,1)}, u32[]{:S(2)}, u32[]{:S(2)}) %collective-permute-start.70) | collective-permute-done | bytes 294944 | tf_op jit(solution)/shard_map/ppermute | solution.py:408
  444.4 2.1 collective-permute-start.65
  446.6 2.9 collective-permute-done.67
  449.4 5.2 %collective-permute-done.68 = bf16[4,144,256]{2,1,0:T(8,128)(2,1)S(1)} collective-permute-done((bf16[4,144,256]{2,1,0:T(8,128)(2,1)}, bf16[4,144,256]{2,1,0:T(8,128)(2,1)S(1)}, u32[]{:S(2)}, u32[]{:S(2)}) %collective-permute-start.68) | collective-permute-done | bytes 294944 | tf_op jit(solution)/shard_map/ppermute | solution.py:408
  459.7 3.0 collective-permute-start.73
  463.9 3.3 collective-permute-start.79
  471.8 3.0 collective-permute-done.75
  474.9 2.6 collective-permute-done.76
  477.5 2.3 collective-permute-done.77
  (395 shorter events, 144.1 us)
Async XLA Ops:
  7.2 140.8 %all-gather.3.cloned.1.call-start = ((), (), s32[]{:S(2)}) async-start(), calls=%async_computation.1 | async-start | bytes 15974400 | tf_op jit(solution)/shard_map/all_gather | solution.py:538
  11.7 445.3 %reduce-scatter.4.cloned.1.call-start = ((), (), s32[]{:S(2)}) async-start(), calls=%async_computation.2 | async-start | bytes 8355840
  12.5 10.2 %collective-permute-start.3 = (bf16[48,256]{1,0:T(8,128)(2,1)S(1)}, bf16[48,256]{1,0:T(8,128)(2,1)S(1)}, u32[]{:S(2)}, u32[]{:S(2)}) collective-permute-start(bf16[48,256]{1,0:T(8,128)(2,1)S(1)} %bitcast.417), channel_id=1, source_target_pairs={{0,3},{1,0},{2,1},{3,2},{4,7},{5,4},{6,5},{7,6},{8,11},{9,8},{10,9... | collective-permute-start | bytes 73736 | tf_op jit(solution)/shard_map/ppermute | solution.py:408
  15.4 11.2 %collective-permute-start.4 = (bf16[48,256]{1,0:T(8,128)(2,1)S(1)}, bf16[48,256]{1,0:T(8,128)(2,1)S(1)}, u32[]{:S(2)}, u32[]{:S(2)}) collective-permute-start(bf16[48,256]{1,0:T(8,128)(2,1)S(1)} %bitcast.418), channel_id=1, source_target_pairs={{0,2},{1,3},{2,0},{3,1},{4,6},{5,7},{6,4},{7,5},{8,10},{9,11},{10,... | collective-permute-start | bytes 73736 | tf_op jit(solution)/shard_map/ppermute | solution.py:408
  15.8 10.8 %collective-permute-start.5 = (bf16[48,256]{1,0:T(8,128)(2,1)S(1)}, bf16[48,256]{1,0:T(8,128)(2,1)S(1)}, u32[]{:S(2)}, u32[]{:S(2)}) collective-permute-start(bf16[48,256]{1,0:T(8,128)(2,1)S(1)} %bitcast.419), channel_id=1, source_target_pairs={{0,1},{1,2},{2,3},{3,0},{4,5},{5,6},{6,7},{7,4},{8,9},{9,10},{10,1... | collective-permute-start | bytes 73736 | tf_op jit(solution)/shard_map/ppermute | solution.py:408
  16.4 14.6 %collective-permute-start = (bf16[64,256]{1,0:T(8,128)(2,1)S(1)}, bf16[64,256]{1,0:T(8,128)(2,1)S(1)}, u32[]{:S(2)}, u32[]{:S(2)}) collective-permute-start(bf16[64,256]{1,0:T(8,128)(2,1)S(1)} %bitcast.406), channel_id=1, source_target_pairs={{0,48},{16,0},{32,16},{48,32},{1,49},{17,1},{33,17},{49,33},{2,50}... | collective-permute-start | bytes 98312 | tf_op jit(solution)/shard_map/ppermute | solution.py:408
  18.9 12.1 %collective-permute-start.1 = (bf16[64,256]{1,0:T(8,128)(2,1)S(1)}, bf16[64,256]{1,0:T(8,128)(2,1)S(1)}, u32[]{:S(2)}, u32[]{:S(2)}) collective-permute-start(bf16[64,256]{1,0:T(8,128)(2,1)S(1)} %bitcast.407), channel_id=1, source_target_pairs={{0,32},{16,48},{32,0},{48,16},{1,33},{17,49},{33,1},{49,17},{2,34}... | collective-permute-start | bytes 98312 | tf_op jit(solution)/shard_map/ppermute | solution.py:408
  32.6 6.5 %collective-permute-start.12 = (bf16[4,48,256]{2,1,0:T(8,128)(2,1)}, bf16[4,48,256]{2,1,0:T(8,128)(2,1)S(1)}, u32[]{:S(2)}, u32[]{:S(2)}) collective-permute-start(bf16[4,48,256]{2,1,0:T(8,128)(2,1)} %get-tuple-element.149), channel_id=1, source_target_pairs={{0,12},{1,13},{2,14},{3,15},{4,0},{5,1},{6,2},{7,3},{8,4},{9,5},{1... | collective-permute-start | bytes 294920 | tf_op jit(solution)/shard_map/ppermute | solution.py:408
  35.5 10.0 %collective-permute-start.15 = (bf16[4,64,256]{2,1,0:T(8,128)(2,1)S(1)}, bf16[4,64,256]{2,1,0:T(8,128)(2,1)}, u32[]{:S(2)}, u32[]{:S(2)}) collective-permute-start(bf16[4,64,256]{2,1,0:T(8,128)(2,1)S(1)} %get-tuple-element.152), channel_id=1, source_target_pairs={{0,48},{16,0},{32,16},{48,32},{1,49},{17,1},{33,17},{49,33},{2,50}... | collective-permute-start | bytes 393224 | tf_op jit(solution)/shard_map/ppermute | solution.py:408
  37.1 7.8 %collective-permute-start.14 = (bf16[4,48,256]{2,1,0:T(8,128)(2,1)}, bf16[4,48,256]{2,1,0:T(8,128)(2,1)}, u32[]{:S(2)}, u32[]{:S(2)}) collective-permute-start(bf16[4,48,256]{2,1,0:T(8,128)(2,1)} %get-tuple-element.149), channel_id=1, source_target_pairs={{0,4},{1,5},{2,6},{3,7},{4,8},{5,9},{6,10},{7,11},{8,12},{9,13},{1... | collective-permute-start | bytes 294920 | tf_op jit(solution)/shard_map/ppermute | solution.py:408
  37.3 10.7 %collective-permute-start.16 = (bf16[4,64,256]{2,1,0:T(8,128)(2,1)S(1)}, bf16[4,64,256]{2,1,0:T(8,128)(2,1)}, u32[]{:S(2)}, u32[]{:S(2)}) collective-permute-start(bf16[4,64,256]{2,1,0:T(8,128)(2,1)S(1)} %get-tuple-element.152), channel_id=1, source_target_pairs={{0,32},{16,48},{32,0},{48,16},{1,33},{17,49},{33,1},{49,17},{2,34}... | collective-permute-start | bytes 393224 | tf_op jit(solution)/shard_map/ppermute | solution.py:408
  39.1 8.9 %collective-permute-start.17 = (bf16[4,64,256]{2,1,0:T(8,128)(2,1)S(1)}, bf16[4,64,256]{2,1,0:T(8,128)(2,1)}, u32[]{:S(2)}, u32[]{:S(2)}) collective-permute-start(bf16[4,64,256]{2,1,0:T(8,128)(2,1)S(1)} %get-tuple-element.152), channel_id=1, source_target_pairs={{0,16},{16,32},{32,48},{48,0},{1,17},{17,33},{33,49},{49,1},{2,18}... | collective-permute-start | bytes 393224 | tf_op jit(solution)/shard_map/ppermute | solution.py:408
  42.1 7.8 %collective-permute-start.9 = (bf16[4,64,256]{2,1,0:T(8,128)(2,1)}, bf16[4,64,256]{2,1,0:T(8,128)(2,1)S(1)}, u32[]{:S(2)}, u32[]{:S(2)}) collective-permute-start(bf16[4,64,256]{2,1,0:T(8,128)(2,1)} %get-tuple-element.146), channel_id=1, source_target_pairs={{0,3},{1,0},{2,1},{3,2},{4,7},{5,4},{6,5},{7,6},{8,11},{9,8},{10,9... | collective-permute-start | bytes 393224 | tf_op jit(solution)/shard_map/ppermute | solution.py:408
  45.5 10.1 %collective-permute-start.11 = (bf16[4,64,256]{2,1,0:T(8,128)(2,1)}, bf16[4,64,256]{2,1,0:T(8,128)(2,1)S(1)}, u32[]{:S(2)}, u32[]{:S(2)}) collective-permute-start(bf16[4,64,256]{2,1,0:T(8,128)(2,1)} %get-tuple-element.146), channel_id=1, source_target_pairs={{0,1},{1,2},{2,3},{3,0},{4,5},{5,6},{6,7},{7,4},{8,9},{9,10},{10,1... | collective-permute-start | bytes 393224 | tf_op jit(solution)/shard_map/ppermute | solution.py:408
  56.5 18.1 %collective-permute-start.18 = (bf16[4,4,64,256]{3,2,1,0:T(8,128)(2,1)}, bf16[4,4,64,256]{3,2,1,0:T(8,128)(2,1)}, u32[]{:S(2)}, u32[]{:S(2)}) collective-permute-start(bf16[4,4,64,256]{3,2,1,0:T(8,128)(2,1)} %get-tuple-element.165), channel_id=1, source_target_pairs={{0,4},{1,5},{2,6},{3,7},{4,8},{5,9},{6,10},{7,11},{8,12},{9,13},{1... | collective-permute-start | bytes 1572872 | tf_op jit(solution)/shard_map/ppermute | solution.py:408
  58.0 16.7 %collective-permute-start.19 = (bf16[4,4,64,256]{3,2,1,0:T(8,128)(2,1)}, bf16[4,4,64,256]{3,2,1,0:T(8,128)(2,1)}, u32[]{:S(2)}, u32[]{:S(2)}) collective-permute-start(bf16[4,4,64,256]{3,2,1,0:T(8,128)(2,1)} %get-tuple-element.165), channel_id=1, source_target_pairs={{0,12},{1,13},{2,14},{3,15},{4,0},{5,1},{6,2},{7,3},{8,4},{9,5},{1... | collective-permute-start | bytes 1572872 | tf_op jit(solution)/shard_map/ppermute | solution.py:408
  59.8 14.9 %collective-permute-start.22 = (bf16[4,4,64,256]{3,2,0,1:T(8,128)(2,1)}, bf16[4,4,64,256]{3,2,0,1:T(8,128)(2,1)}, u32[]{:S(2)}, u32[]{:S(2)}) collective-permute-start(bf16[4,4,64,256]{3,2,0,1:T(8,128)(2,1)} %get-tuple-element.174), channel_id=1, source_target_pairs={{0,2},{1,3},{2,0},{3,1},{4,6},{5,7},{6,4},{7,5},{8,10},{9,11},{10,... | collective-permute-start | bytes 1572872 | tf_op jit(solution)/shard_map/ppermute | solution.py:408
  65.1 8.6 %collective-permute-start.20 = (bf16[4,4,48,256]{3,2,1,0:T(8,128)(2,1)S(1)}, bf16[4,4,48,256]{3,2,1,0:T(8,128)(2,1)S(1)}, u32[]{:S(2)}, u32[]{:S(2)}) collective-permute-start(bf16[4,4,48,256]{3,2,1,0:T(8,128)(2,1)S(1)} %copy-done.39), channel_id=1, source_target_pairs={{0,16},{16,32},{32,48},{48,0},{1,17},{17,33},{33,49},{49,1},{2,18}... | collective-permute-start | bytes 1179656 | tf_op jit(solution)/shard_map/ppermute | solution.py:408
  65.4 8.2 %collective-permute-start.21 = (bf16[4,4,48,256]{3,2,1,0:T(8,128)(2,1)S(1)}, bf16[4,4,48,256]{3,2,1,0:T(8,128)(2,1)S(1)}, u32[]{:S(2)}, u32[]{:S(2)}) collective-permute-start(bf16[4,4,48,256]{3,2,1,0:T(8,128)(2,1)S(1)} %copy-done.39), channel_id=1, source_target_pairs={{0,48},{16,0},{32,16},{48,32},{1,49},{17,1},{33,17},{49,33},{2,50}... | collective-permute-start | bytes 1179656 | tf_op jit(solution)/shard_map/ppermute | solution.py:408
  74.7 9.7 %collective-permute-start.23 = (bf16[4,4,64,256]{3,2,1,0:T(8,128)(2,1)}, bf16[4,4,64,256]{3,2,1,0:T(8,128)(2,1)S(1)}, u32[]{:S(2)}, u32[]{:S(2)}) collective-permute-start(bf16[4,4,64,256]{3,2,1,0:T(8,128)(2,1)} %get-tuple-element.165), channel_id=1, source_target_pairs={{0,8},{1,9},{2,10},{3,11},{4,12},{5,13},{6,14},{7,15},{8,0},{9,1},... | collective-permute-start | bytes 1572872 | tf_op jit(solution)/shard_map/ppermute | solution.py:408
  76.6 22.7 %collective-permute-start.27 = (bf16[4,4,64,256]{3,2,0,1:T(8,128)(2,1)}, bf16[4,4,64,256]{3,2,0,1:T(8,128)(2,1)S(1)}, u32[]{:S(2)}, u32[]{:S(2)}) collective-permute-start(bf16[4,4,64,256]{3,2,0,1:T(8,128)(2,1)} %get-tuple-element.174), channel_id=1, source_target_pairs={{0,3},{1,0},{2,1},{3,2},{4,7},{5,4},{6,5},{7,6},{8,11},{9,8},{10,9... | collective-permute-start | bytes 1572872 | tf_op jit(solution)/shard_map/ppermute | solution.py:408
  76.6 22.7 %collective-permute-start.28 = (bf16[4,4,64,256]{3,2,0,1:T(8,128)(2,1)}, bf16[4,4,64,256]{3,2,0,1:T(8,128)(2,1)S(1)}, u32[]{:S(2)}, u32[]{:S(2)}) collective-permute-start(bf16[4,4,64,256]{3,2,0,1:T(8,128)(2,1)} %get-tuple-element.174), channel_id=1, source_target_pairs={{0,1},{1,2},{2,3},{3,0},{4,5},{5,6},{6,7},{7,4},{8,9},{9,10},{10,1... | collective-permute-start | bytes 1572872 | tf_op jit(solution)/shard_map/ppermute | solution.py:408
  78.1 29.4 %collective-permute-start.24 = (bf16[4,4,48,256]{3,2,1,0:T(8,128)(2,1)S(1)}, bf16[4,4,48,256]{3,2,1,0:T(8,128)(2,1)S(1)}, u32[]{:S(2)}, u32[]{:S(2)}) collective-permute-start(bf16[4,4,48,256]{3,2,1,0:T(8,128)(2,1)S(1)} %copy-done.39), channel_id=1, source_target_pairs={{0,32},{16,48},{32,0},{48,16},{1,33},{17,49},{33,1},{49,17},{2,34}... | collective-permute-start | bytes 1179656 | tf_op jit(solution)/shard_map/ppermute | solution.py:408
  86.2 27.3 %collective-permute-start.25 = (bf16[64,64,256]{2,1,0:T(8,128)(2,1)S(1)}, bf16[64,64,256]{2,1,0:T(8,128)(2,1)S(1)}, u32[]{:S(2)}, u32[]{:S(2)}) collective-permute-start(bf16[64,64,256]{2,1,0:T(8,128)(2,1)S(1)} %bitcast.340), channel_id=1, source_target_pairs={{0,64},{64,0},{1,65},{65,1},{2,66},{66,2},{3,67},{67,3},{4,68},{68... | collective-permute-start | bytes 6291464 | tf_op jit(solution)/shard_map/ppermute | solution.py:395
  102.1 30.5 %collective-permute-start.29 = (bf16[64,64,256]{2,1,0:T(8,128)(2,1)}, bf16[64,64,256]{2,1,0:T(8,128)(2,1)}, u32[]{:S(2)}, u32[]{:S(2)}) collective-permute-start(bf16[64,64,256]{2,1,0:T(8,128)(2,1)} %bitcast.56.own), channel_id=1, source_target_pairs={{0,64},{64,0},{1,65},{65,1},{2,66},{66,2},{3,67},{67,3},{4,68},{68... | collective-permute-start | bytes 6291464 | tf_op jit(solution)/shard_map/ppermute | solution.py:395
  123.7 14.4 %collective-permute-start.32 = (bf16[128,640]{1,0:T(8,128)(2,1)}, bf16[128,640]{1,0:T(8,128)(2,1)S(1)}, u32[]{:S(2)}, u32[]{:S(2)}) collective-permute-start(bf16[128,640]{1,0:T(8,128)(2,1)} %get-tuple-element.179), channel_id=1, source_target_pairs={{0,48},{1,49},{2,50},{3,51},{4,52},{5,53},{6,54},{7,55},{8,56},{9,... | collective-permute-start | bytes 491528 | tf_op jit(solution)/shard_map/ppermute | solution.py:557
  128.8 9.3 %collective-permute-start.31 = (bf16[128,640]{1,0:T(8,128)(2,1)}, bf16[128,640]{1,0:T(8,128)(2,1)S(1)}, u32[]{:S(2)}, u32[]{:S(2)}) collective-permute-start(bf16[128,640]{1,0:T(8,128)(2,1)} %get-tuple-element.179), channel_id=1, source_target_pairs={{0,32},{16,48},{1,33},{17,49},{2,34},{18,50},{3,35},{19,51},{4,36}... | collective-permute-start | bytes 491528 | tf_op jit(solution)/shard_map/ppermute | solution.py:557
  130.1 8.0 %collective-permute-start.30 = (bf16[128,640]{1,0:T(8,128)(2,1)}, bf16[128,640]{1,0:T(8,128)(2,1)S(1)}, u32[]{:S(2)}, u32[]{:S(2)}) collective-permute-start(bf16[128,640]{1,0:T(8,128)(2,1)} %get-tuple-element.179), channel_id=1, source_target_pairs={{0,16},{16,32},{32,48},{1,17},{17,33},{33,49},{2,18},{18,34},{34,5... | collective-permute-start | bytes 491528 | tf_op jit(solution)/shard_map/ppermute | solution.py:557
  167.4 12.1 %collective-permute-start.38 = (bf16[128,640]{1,0:T(8,128)(2,1)}, bf16[128,640]{1,0:T(8,128)(2,1)S(1)}, u32[]{:S(2)}, u32[]{:S(2)}) collective-permute-start(bf16[128,640]{1,0:T(8,128)(2,1)} %get-tuple-element.189), channel_id=1, source_target_pairs={{0,48},{1,49},{2,50},{3,51},{4,52},{5,53},{6,54},{7,55},{8,56},{9,... | collective-permute-start | bytes 491528 | tf_op jit(solution)/shard_map/ppermute | solution.py:557
  172.7 6.9 %collective-permute-start.37 = (bf16[128,640]{1,0:T(8,128)(2,1)}, bf16[128,640]{1,0:T(8,128)(2,1)S(1)}, u32[]{:S(2)}, u32[]{:S(2)}) collective-permute-start(bf16[128,640]{1,0:T(8,128)(2,1)} %get-tuple-element.189), channel_id=1, source_target_pairs={{0,32},{16,48},{1,33},{17,49},{2,34},{18,50},{3,35},{19,51},{4,36}... | collective-permute-start | bytes 491528 | tf_op jit(solution)/shard_map/ppermute | solution.py:557
  174.0 7.0 %collective-permute-start.36 = (bf16[128,640]{1,0:T(8,128)(2,1)}, bf16[128,640]{1,0:T(8,128)(2,1)S(1)}, u32[]{:S(2)}, u32[]{:S(2)}) collective-permute-start(bf16[128,640]{1,0:T(8,128)(2,1)} %get-tuple-element.189), channel_id=1, source_target_pairs={{0,16},{16,32},{32,48},{1,17},{17,33},{33,49},{2,18},{18,34},{34,5... | collective-permute-start | bytes 491528 | tf_op jit(solution)/shard_map/ppermute | solution.py:557
  219.6 8.6 %collective-permute-start.43 = (bf16[128,640]{1,0:T(8,128)(2,1)}, bf16[128,640]{1,0:T(8,128)(2,1)S(1)}, u32[]{:S(2)}, u32[]{:S(2)}) collective-permute-start(bf16[128,640]{1,0:T(8,128)(2,1)} %get-tuple-element.201), channel_id=1, source_target_pairs={{16,0},{32,16},{48,32},{17,1},{33,17},{49,33},{18,2},{34,18},{50,3... | collective-permute-start | bytes 491528 | tf_op jit(solution)/shard_map/ppermute | solution.py:560
  220.9 10.0 %collective-permute-start.44 = (bf16[128,640]{1,0:T(8,128)(2,1)}, bf16[128,640]{1,0:T(8,128)(2,1)S(1)}, u32[]{:S(2)}, u32[]{:S(2)}) collective-permute-start(bf16[128,640]{1,0:T(8,128)(2,1)} %get-tuple-element.202), channel_id=1, source_target_pairs={{32,0},{48,16},{33,1},{49,17},{34,2},{50,18},{35,3},{51,19},{36,4}... | collective-permute-start | bytes 491528 | tf_op jit(solution)/shard_map/ppermute | solution.py:560
  222.2 13.0 %collective-permute-start.45 = (bf16[128,640]{1,0:T(8,128)(2,1)}, bf16[128,640]{1,0:T(8,128)(2,1)S(1)}, u32[]{:S(2)}, u32[]{:S(2)}) collective-permute-start(bf16[128,640]{1,0:T(8,128)(2,1)} %get-tuple-element.203), channel_id=1, source_target_pairs={{48,0},{49,1},{50,2},{51,3},{52,4},{53,5},{54,6},{55,7},{56,8},{57... | collective-permute-start | bytes 491528 | tf_op jit(solution)/shard_map/ppermute | solution.py:560
  252.6 68.5 %collective-permute-start.53 = (bf16[64,96,256]{2,1,0:T(8,128)(2,1)}, bf16[64,96,256]{2,1,0:T(8,128)(2,1)}, u32[]{:S(2)}, u32[]{:S(2)}) collective-permute-start(bf16[64,96,256]{2,1,0:T(8,128)(2,1)} %get-tuple-element.227), channel_id=1, source_target_pairs={{0,64},{64,0},{1,65},{65,1},{2,66},{66,2},{3,67},{67,3},{4,68},{68... | collective-permute-start | bytes 9437192 | tf_op jit(solution)/shard_map/ppermute | solution.py:395
  281.4 7.6 %collective-permute-start.48 = (bf16[128,640]{1,0:T(8,128)(2,1)}, bf16[128,640]{1,0:T(8,128)(2,1)S(1)}, u32[]{:S(2)}, u32[]{:S(2)}) collective-permute-start(bf16[128,640]{1,0:T(8,128)(2,1)} %get-tuple-element.214), channel_id=1, source_target_pairs={{16,0},{32,16},{48,32},{17,1},{33,17},{49,33},{18,2},{34,18},{50,3... | collective-permute-start | bytes 491528 | tf_op jit(solution)/shard_map/ppermute | solution.py:560
  282.7 9.0 %collective-permute-start.49 = (bf16[128,640]{1,0:T(8,128)(2,1)}, bf16[128,640]{1,0:T(8,128)(2,1)S(1)}, u32[]{:S(2)}, u32[]{:S(2)}) collective-permute-start(bf16[128,640]{1,0:T(8,128)(2,1)} %get-tuple-element.215), channel_id=1, source_target_pairs={{32,0},{48,16},{33,1},{49,17},{34,2},{50,18},{35,3},{51,19},{36,4}... | collective-permute-start | bytes 491528 | tf_op jit(solution)/shard_map/ppermute | solution.py:560
  284.0 11.6 %collective-permute-start.50 = (bf16[128,640]{1,0:T(8,128)(2,1)}, bf16[128,640]{1,0:T(8,128)(2,1)S(1)}, u32[]{:S(2)}, u32[]{:S(2)}) collective-permute-start(bf16[128,640]{1,0:T(8,128)(2,1)} %get-tuple-element.216), channel_id=1, source_target_pairs={{48,0},{49,1},{50,2},{51,3},{52,4},{53,5},{54,6},{55,7},{56,8},{57... | collective-permute-start | bytes 491528 | tf_op jit(solution)/shard_map/ppermute | solution.py:560
  312.5 14.6 %collective-permute-start.52 = (bf16[64,96,256]{2,1,0:T(8,128)(2,1)}, bf16[64,96,256]{2,1,0:T(8,128)(2,1)}, u32[]{:S(2)}, u32[]{:S(2)}) collective-permute-start(bf16[64,96,256]{2,1,0:T(8,128)(2,1)} %get-tuple-element.225), channel_id=1, source_target_pairs={{0,64},{64,0},{1,65},{65,1},{2,66},{66,2},{3,67},{67,3},{4,68},{68... | collective-permute-start | bytes 9437192 | tf_op jit(solution)/shard_map/ppermute | solution.py:395
  336.7 28.6 %collective-permute-start.54 = (bf16[4,4,144,256]{3,2,0,1:T(8,128)(2,1)S(1)}, bf16[4,4,144,256]{3,2,0,1:T(8,128)(2,1)S(1)}, u32[]{:S(2)}, u32[]{:S(2)}) collective-permute-start(bf16[4,4,144,256]{3,2,0,1:T(8,128)(2,1)S(1)} %bitcast.372), channel_id=1, source_target_pairs={{0,16},{16,32},{32,48},{48,0},{1,17},{17,33},{33,49},{49,1},{2,18}... | collective-permute-start | bytes 3538952 | tf_op jit(solution)/shard_map/ppermute | solution.py:408
  336.7 28.6 %collective-permute-start.55 = (bf16[4,4,144,256]{3,2,0,1:T(8,128)(2,1)S(1)}, bf16[4,4,144,256]{3,2,0,1:T(8,128)(2,1)S(1)}, u32[]{:S(2)}, u32[]{:S(2)}) collective-permute-start(bf16[4,4,144,256]{3,2,0,1:T(8,128)(2,1)S(1)} %bitcast.371), channel_id=1, source_target_pairs={{0,48},{16,0},{32,16},{48,32},{1,49},{17,1},{33,17},{49,33},{2,50}... | collective-permute-start | bytes 3538952 | tf_op jit(solution)/shard_map/ppermute | solution.py:408
  339.4 28.0 %collective-permute-start.56 = (bf16[4,4,144,256]{3,2,1,0:T(8,128)(2,1)S(1)}, bf16[4,4,144,256]{3,2,1,0:T(8,128)(2,1)S(1)}, u32[]{:S(2)}, u32[]{:S(2)}) collective-permute-start(bf16[4,4,144,256]{3,2,1,0:T(8,128)(2,1)S(1)} %pad_maximum_fusion.3), channel_id=1, source_target_pairs={{0,1},{1,2},{2,3},{3,0},{4,5},{5,6},{6,7},{7,4},{8,9},{9,10},{10,1... | collective-permute-start | bytes 3538952 | tf_op jit(solution)/shard_map/ppermute | solution.py:408
  340.7 26.7 %collective-permute-start.57 = (bf16[4,4,144,256]{3,2,1,0:T(8,128)(2,1)S(1)}, bf16[4,4,144,256]{3,2,1,0:T(8,128)(2,1)S(1)}, u32[]{:S(2)}, u32[]{:S(2)}) collective-permute-start(bf16[4,4,144,256]{3,2,1,0:T(8,128)(2,1)S(1)} %pad_maximum_fusion.5), channel_id=1, source_target_pairs={{0,3},{1,0},{2,1},{3,2},{4,7},{5,4},{6,5},{7,6},{8,11},{9,8},{10,9... | collective-permute-start | bytes 3538952 | tf_op jit(solution)/shard_map/ppermute | solution.py:408
  342.1 27.7 %collective-permute-start.58 = (bf16[4,4,144,256]{3,2,0,1:T(8,128)(2,1)S(1)}, bf16[4,4,144,256]{3,2,0,1:T(8,128)(2,1)S(1)}, u32[]{:S(2)}, u32[]{:S(2)}) collective-permute-start(bf16[4,4,144,256]{3,2,0,1:T(8,128)(2,1)S(1)} %pad_maximum_fusion.7), channel_id=1, source_target_pairs={{0,8},{1,9},{2,10},{3,11},{4,12},{5,13},{6,14},{7,15},{8,0},{9,1},... | collective-permute-start | bytes 3538952 | tf_op jit(solution)/shard_map/ppermute | solution.py:408
  370.8 27.1 %collective-permute-start.60 = (bf16[4,4,144,256]{3,2,1,0:T(8,128)(2,1)}, bf16[4,4,144,256]{3,2,1,0:T(8,128)(2,1)}, u32[]{:S(2)}, u32[]{:S(2)}) collective-permute-start(bf16[4,4,144,256]{3,2,1,0:T(8,128)(2,1)} %pad_maximum_fusion.4), channel_id=1, source_target_pairs={{0,2},{1,3},{2,0},{3,1},{4,6},{5,7},{6,4},{7,5},{8,10},{9,11},{10,... | collective-permute-start | bytes 3538952 | tf_op jit(solution)/shard_map/ppermute | solution.py:408
  385.8 42.4 %collective-permute-start.41 = (bf16[128,1024]{1,0:T(8,128)(2,1)S(1)}, bf16[128,1024]{1,0:T(8,128)(2,1)S(1)}, u32[]{:S(2)}, u32[]{:S(2)}) collective-permute-start(bf16[128,1024]{1,0:T(8,128)(2,1)S(1)} %get-tuple-element.303), channel_id=1, source_target_pairs={{0,64},{64,0},{1,65},{65,1},{2,66},{66,2},{3,67},{67,3},{4,68},{68... | collective-permute-start | bytes 786440 | tf_op jit(solution)/shard_map/ppermute | solution.py:395
  386.3 33.1 %collective-permute-start.59 = (bf16[4,4,144,256]{3,2,0,1:T(8,128)(2,1)S(1)}, bf16[4,4,144,256]{3,2,0,1:T(8,128)(2,1)S(1)}, u32[]{:S(2)}, u32[]{:S(2)}) collective-permute-start(bf16[4,4,144,256]{3,2,0,1:T(8,128)(2,1)S(1)} %bitcast.370), channel_id=1, source_target_pairs={{0,32},{16,48},{32,0},{48,16},{1,33},{17,49},{33,1},{49,17},{2,34}... | collective-permute-start | bytes 3538952 | tf_op jit(solution)/shard_map/ppermute | solution.py:408
  386.3 30.9 %collective-permute-start.61 = (bf16[4,4,144,256]{3,2,0,1:T(8,128)(2,1)}, bf16[4,4,144,256]{3,2,0,1:T(8,128)(2,1)S(1)}, u32[]{:S(2)}, u32[]{:S(2)}) collective-permute-start(bf16[4,4,144,256]{3,2,0,1:T(8,128)(2,1)} %pad_maximum_fusion.6), channel_id=1, source_target_pairs={{0,4},{1,5},{2,6},{3,7},{4,8},{5,9},{6,10},{7,11},{8,12},{9,13},{1... | collective-permute-start | bytes 3538952 | tf_op jit(solution)/shard_map/ppermute | solution.py:408
  389.4 27.7 %collective-permute-start.62 = (bf16[4,4,144,256]{3,2,0,1:T(8,128)(2,1)S(1)}, bf16[4,4,144,256]{3,2,0,1:T(8,128)(2,1)S(1)}, u32[]{:S(2)}, u32[]{:S(2)}) collective-permute-start(bf16[4,4,144,256]{3,2,0,1:T(8,128)(2,1)S(1)} %copy-done.16), channel_id=1, source_target_pairs={{0,12},{1,13},{2,14},{3,15},{4,0},{5,1},{6,2},{7,3},{8,4},{9,5},{1... | collective-permute-start | bytes 3538952 | tf_op jit(solution)/shard_map/ppermute | solution.py:408
  423.5 9.8 %collective-permute-start.69 = (bf16[4,144,256]{2,1,0:T(8,128)(2,1)}, bf16[4,144,256]{2,1,0:T(8,128)(2,1)}, u32[]{:S(2)}, u32[]{:S(2)}) collective-permute-start(bf16[4,144,256]{2,1,0:T(8,128)(2,1)} %pad_maximum_fusion.17), channel_id=1, source_target_pairs={{0,16},{16,32},{32,48},{48,0},{1,17},{17,33},{33,49},{49,1},{2,18}... | collective-permute-start | bytes 884744 | tf_op jit(solution)/shard_map/ppermute | solution.py:408
  423.7 15.4 %collective-permute-start.70 = (bf16[4,144,256]{2,1,0:T(8,128)(2,1)}, bf16[4,144,256]{2,1,0:T(8,128)(2,1)}, u32[]{:S(2)}, u32[]{:S(2)}) collective-permute-start(bf16[4,144,256]{2,1,0:T(8,128)(2,1)} %pad_maximum_fusion.18), channel_id=1, source_target_pairs={{0,32},{16,48},{32,0},{48,16},{1,33},{17,49},{33,1},{49,17},{2,34}... | collective-permute-start | bytes 884744 | tf_op jit(solution)/shard_map/ppermute | solution.py:408
  426.1 14.2 %collective-permute-start.71 = (bf16[4,144,256]{2,1,0:T(8,128)(2,1)}, bf16[4,144,256]{2,1,0:T(8,128)(2,1)}, u32[]{:S(2)}, u32[]{:S(2)}) collective-permute-start(bf16[4,144,256]{2,1,0:T(8,128)(2,1)} %pad_maximum_fusion.19), channel_id=1, source_target_pairs={{0,48},{16,0},{32,16},{48,32},{1,49},{17,1},{33,17},{49,33},{2,50}... | collective-permute-start | bytes 884744 | tf_op jit(solution)/shard_map/ppermute | solution.py:408
  430.0 25.7 %collective-permute-start.63 = (bf16[4,144,256]{2,1,0:T(8,128)(2,1)}, bf16[4,144,256]{2,1,0:T(8,128)(2,1)S(1)}, u32[]{:S(2)}, u32[]{:S(2)}) collective-permute-start(bf16[4,144,256]{2,1,0:T(8,128)(2,1)} %get-tuple-element.246), channel_id=1, source_target_pairs={{0,1},{1,2},{2,3},{3,0},{4,5},{5,6},{6,7},{7,4},{8,9},{9,10},{10,1... | collective-permute-start | bytes 884744 | tf_op jit(solution)/shard_map/ppermute | solution.py:408
  430.0 25.7 %collective-permute-start.64 = (bf16[4,144,256]{2,1,0:T(8,128)(2,1)S(1)}, bf16[4,144,256]{2,1,0:T(8,128)(2,1)S(1)}, u32[]{:S(2)}, u32[]{:S(2)}) collective-permute-start(bf16[4,144,256]{2,1,0:T(8,128)(2,1)S(1)} %copy-done.41), channel_id=1, source_target_pairs={{0,2},{1,3},{2,0},{3,1},{4,6},{5,7},{6,4},{7,5},{8,10},{9,11},{10,... | collective-permute-start | bytes 884744 | tf_op jit(solution)/shard_map/ppermute | solution.py:408
  433.3 11.1 %collective-permute-start.66 = (bf16[4,144,256]{2,1,0:T(8,128)(2,1)}, bf16[4,144,256]{2,1,0:T(8,128)(2,1)S(1)}, u32[]{:S(2)}, u32[]{:S(2)}) collective-permute-start(bf16[4,144,256]{2,1,0:T(8,128)(2,1)} %pad_maximum_fusion.14), channel_id=1, source_target_pairs={{0,4},{1,5},{2,6},{3,7},{4,8},{5,9},{6,10},{7,11},{8,12},{9,13},{1... | collective-permute-start | bytes 884744 | tf_op jit(solution)/shard_map/ppermute | solution.py:408
  439.2 10.2 %collective-permute-start.67 = (bf16[4,144,256]{2,1,0:T(8,128)(2,1)}, bf16[4,144,256]{2,1,0:T(8,128)(2,1)S(1)}, u32[]{:S(2)}, u32[]{:S(2)}) collective-permute-start(bf16[4,144,256]{2,1,0:T(8,128)(2,1)} %pad_maximum_fusion.15), channel_id=1, source_target_pairs={{0,8},{1,9},{2,10},{3,11},{4,12},{5,13},{6,14},{7,15},{8,0},{9,1},... | collective-permute-start | bytes 884744 | tf_op jit(solution)/shard_map/ppermute | solution.py:408
  440.3 14.3 %collective-permute-start.68 = (bf16[4,144,256]{2,1,0:T(8,128)(2,1)}, bf16[4,144,256]{2,1,0:T(8,128)(2,1)S(1)}, u32[]{:S(2)}, u32[]{:S(2)}) collective-permute-start(bf16[4,144,256]{2,1,0:T(8,128)(2,1)} %pad_maximum_fusion.16), channel_id=1, source_target_pairs={{0,12},{1,13},{2,14},{3,15},{4,0},{5,1},{6,2},{7,3},{8,4},{9,5},{1... | collective-permute-start | bytes 884744 | tf_op jit(solution)/shard_map/ppermute | solution.py:408
  444.4 11.3 %collective-permute-start.65 = (bf16[4,144,256]{2,1,0:T(8,128)(2,1)S(1)}, bf16[4,144,256]{2,1,0:T(8,128)(2,1)S(1)}, u32[]{:S(2)}, u32[]{:S(2)}) collective-permute-start(bf16[4,144,256]{2,1,0:T(8,128)(2,1)S(1)} %copy-done.40), channel_id=1, source_target_pairs={{0,3},{1,0},{2,1},{3,2},{4,7},{5,4},{6,5},{7,6},{8,11},{9,8},{10,9... | collective-permute-start | bytes 884744 | tf_op jit(solution)/shard_map/ppermute | solution.py:408
  459.7 7.5 %collective-permute-start.73 = (bf16[144,256]{1,0:T(8,128)(2,1)S(1)}, bf16[144,256]{1,0:T(8,128)(2,1)S(1)}, u32[]{:S(2)}, u32[]{:S(2)}) collective-permute-start(bf16[144,256]{1,0:T(8,128)(2,1)S(1)} %get-tuple-element.257), channel_id=1, source_target_pairs={{0,8},{1,9},{2,10},{3,11},{4,12},{5,13},{6,14},{7,15},{8,0},{9,1},... | collective-permute-start | bytes 221192 | tf_op jit(solution)/shard_map/ppermute | solution.py:408
  462.7 20.1 %collective-permute-start.51 = (bf16[128,1024]{1,0:T(8,128)(2,1)S(1)}, bf16[128,1024]{1,0:T(8,128)(2,1)S(1)}, u32[]{:S(2)}, u32[]{:S(2)}) collective-permute-start(bf16[128,1024]{1,0:T(8,128)(2,1)S(1)} %broadcast_select_fusion.4), channel_id=1, source_target_pairs={{0,64},{64,0},{1,65},{65,1},{2,66},{66,2},{3,67},{67,3},{4,68},{68... | collective-permute-start | bytes 786440 | tf_op jit(solution)/shard_map/ppermute | solution.py:395
  463.9 7.2 %collective-permute-start.79 = (bf16[144,256]{1,0:T(8,128)(2,1)S(1)}, bf16[144,256]{1,0:T(8,128)(2,1)S(1)}, u32[]{:S(2)}, u32[]{:S(2)}) collective-permute-start(bf16[144,256]{1,0:T(8,128)(2,1)S(1)} %pad_maximum_fusion.33), channel_id=1, source_target_pairs={{0,2},{1,3},{2,0},{3,1},{4,6},{5,7},{6,4},{7,5},{8,10},{9,11},{10,... | collective-permute-start | bytes 221192 | tf_op jit(solution)/shard_map/ppermute | solution.py:408
  467.9 7.0 %collective-permute-start.75 = (bf16[384,256]{1,0:T(8,128)(2,1)S(1)}, bf16[384,256]{1,0:T(8,128)(2,1)S(1)}, u32[]{:S(2)}, u32[]{:S(2)}) collective-permute-start(bf16[384,256]{1,0:T(8,128)(2,1)S(1)} %pad_maximum_fusion.23), channel_id=1, source_target_pairs={{0,16},{16,32},{32,48},{48,0},{1,17},{17,33},{33,49},{49,1},{2,18}... | collective-permute-start | bytes 589832 | tf_op jit(solution)/shard_map/ppermute | solution.py:408
  468.9 8.6 %collective-permute-start.76 = (bf16[384,256]{1,0:T(8,128)(2,1)S(1)}, bf16[384,256]{1,0:T(8,128)(2,1)S(1)}, u32[]{:S(2)}, u32[]{:S(2)}) collective-permute-start(bf16[384,256]{1,0:T(8,128)(2,1)S(1)} %pad_maximum_fusion.24), channel_id=1, source_target_pairs={{0,32},{16,48},{32,0},{48,16},{1,33},{17,49},{33,1},{49,17},{2,34}... | collective-permute-start | bytes 589832 | tf_op jit(solution)/shard_map/ppermute | solution.py:408
  471.1 8.8 %collective-permute-start.77 = (bf16[384,256]{1,0:T(8,128)(2,1)S(1)}, bf16[384,256]{1,0:T(8,128)(2,1)S(1)}, u32[]{:S(2)}, u32[]{:S(2)}) collective-permute-start(bf16[384,256]{1,0:T(8,128)(2,1)S(1)} %pad_maximum_fusion.25), channel_id=1, source_target_pairs={{0,48},{16,0},{32,16},{48,32},{1,49},{17,1},{33,17},{49,33},{2,50}... | collective-permute-start | bytes 589832 | tf_op jit(solution)/shard_map/ppermute | solution.py:408
  (76 other events, 365.8 us)
Sparse Core Ops, SparseCore 0:
  11.8 124.2 all-gather.2
  204.6 85.3 reduce-scatter.3
